TPU v7x, 32 devices: a whole 2x2x4 slice. The times are simulated.
32 devices in a mesh: dp: 8 (over y, x, core), tensor: 4 (over z).
Axes of the slice: x: 2, y: 2, z: 4, core: 2. Of those that a mesh axis runs over, the one named last changes fastest.
Arguments:
- inputs: bfloat16 [16, 1024, 1024], P('dp', 'tensor'), may hold values from -6 to 6
- query_weight: bfloat16 [1024, 1024], P(None, 'tensor'), may hold values from -0.1875 to 0.1875
- key_weight: bfloat16 [1024, 512], P(None, 'tensor'), may hold values from -0.1875 to 0.1875
- value_weight: bfloat16 [1024, 512], P(None, 'tensor'), may hold values from -0.1875 to 0.1875
- out_weight: bfloat16 [1024, 1024], P('tensor'), may hold values from -1.5 to 1.5
- gate_weight: bfloat16 [1024, 4608], P(None, 'tensor'), may hold values from -0.1875 to 0.1875
- up_weight: bfloat16 [1024, 4608], P(None, 'tensor'), may hold values from -0.1875 to 0.1875
- down_weight: bfloat16 [4608, 1024], P('tensor'), may hold values from -0.1875 to 0.1875
- attn_gain: float32 [1024], replicated, may hold values from 0.5 to 1.5
- ffn_gain: float32 [1024], replicated, may hold values from 0.5 to 1.5
- query_gain: float32 [64], replicated, may hold values from 0.5 to 1.5
- key_gain: float32 [64], replicated, may hold values from 0.5 to 1.5
- cotangent: bfloat16 [16, 1024, 1024], P('dp', 'tensor'), may hold values from -6 to 6
- segment_ids: int32 [16, 1024], P('dp'), may hold values from 0 to 1023, as said below
- padding: int32 [16, 1024], P('dp'), may hold values from 0 to 1, as said below
- row_count: int32 [8], P('dp'), may hold values from 1 to 2, as said below
Outputs:
- outputs: bfloat16 [16, 1024, 1024], P('dp', 'tensor')
- input_grad: float32 [16, 1024, 1024], P('dp', 'tensor')
- query_grad: float32 [1024, 1024], P('dp', 'tensor')
- key_grad: float32 [1024, 512], P('dp', 'tensor')
- value_grad: float32 [1024, 512], P('dp', 'tensor')
- out_grad: float32 [1024, 1024], P(('tensor', 'dp'))
- gate_grad: float32 [1024, 4608], P('dp', 'tensor')
- up_grad: float32 [1024, 4608], P('dp', 'tensor')
- down_grad: float32 [4608, 1024], P(('tensor', 'dp'))
- attn_gain_grad: float32 [1024], replicated
- ffn_gain_grad: float32 [1024], replicated
- query_gain_grad: float32 [64], replicated
- key_gain_grad: float32 [64], replicated
Inputs may be any that keep to these rules, and one draw needn't show every extreme that they name: `segment_ids`: within each row the ids start at 0 and never fall; a document is a run of equal ids. The last position of each row is a document of its own, numbered 1024 - 1. `padding`: each row is 1 on a prefix and 0 after it. `row_count`: some device holds 2 rows and some other device 1 in every draw.
All inputs are finite; a program needn't handle non-finite values.
Results may differ from a plain program's by a relative error of at most 0.02.
Values may be sent and summed in bfloat16 or wider, within the bound.
A program may use at most 256 MiB of HBM per device.

v0:
```python
import jax
import jax.numpy as jnp
from jax import lax
from jax.sharding import PartitionSpec as P

EPS = 1e-05
THETA = 1000000.0
MASKED = -1e30
row_block = 512


def rms_scale(values):
    return lax.rsqrt(jnp.mean(values * values, axis=-1, keepdims=True) + EPS)


def rope_tables(length, width):
    half_width = width // 2
    frequency = THETA ** (-(2.0 * jnp.arange(half_width, dtype=jnp.float32)) / width)
    angles = jnp.arange(length, dtype=jnp.float32)[:, None] * frequency[None, :]
    return (jnp.cos(angles), jnp.sin(angles))


def rotate(values, cos_table, sin_table):
    half_width = values.shape[-1] // 2
    leading = values[..., :half_width]
    trailing = values[..., half_width:]
    cos_part = cos_table[:, None, :]
    sin_part = sin_table[:, None, :]
    return jnp.concatenate(
        [leading * cos_part - trailing * sin_part, trailing * cos_part + leading * sin_part],
        axis=-1,
    )


def rotate_back(grads, cos_table, sin_table):
    half_width = grads.shape[-1] // 2
    leading = grads[..., :half_width]
    trailing = grads[..., half_width:]
    cos_part = cos_table[:, None, :]
    sin_part = sin_table[:, None, :]
    return jnp.concatenate(
        [leading * cos_part + trailing * sin_part, trailing * cos_part - leading * sin_part],
        axis=-1,
    )


def norm_back(grads, unit, scale, gain):
    scaled = grads * gain
    return scale * (scaled - unit * jnp.mean(scaled * unit, axis=-1, keepdims=True))


def allowed_block(segment, alive_row, start_row, count_rows, count_keys):
    query_pos = start_row + lax.iota(jnp.int32, count_rows)
    key_pos = lax.iota(jnp.int32, count_keys)
    same_doc = segment[start_row : start_row + count_rows][:, None] == segment[:count_keys][None, :]
    earlier = key_pos[None, :] < query_pos[:, None]
    itself = key_pos[None, :] == query_pos[:, None]
    return itself | earlier & same_doc & (alive_row[:count_keys][None, :] > 0)


def block_scores(query_block, key_block, allowed, scale):
    raw_scores = (
        jnp.einsum("igrd,jgd->grij", query_block, key_block, preferred_element_type=jnp.float32)
        * scale
    )
    return jnp.where(allowed[None, None], raw_scores, MASKED)


def outer_sum(left_list, right_list):
    left_all = jnp.concatenate(left_list, axis=0)
    right_all = jnp.concatenate(right_list, axis=0)
    return jnp.einsum("sa,sb->ab", left_all, right_all, preferred_element_type=jnp.float32)


def per_device(
    inputs,
    query_weight,
    key_weight,
    value_weight,
    out_weight,
    gate_weight,
    up_weight,
    down_weight,
    attn_gain,
    ffn_gain,
    query_gain,
    key_gain,
    cotangent,
    segment_ids,
    padding,
    row_count,
):
    slots = inputs.shape[0]
    local_len = inputs.shape[1]
    seq_len = segment_ids.shape[1]
    head_dim = query_gain.shape[0]
    query_heads = query_weight.shape[1] // head_dim
    key_heads = key_weight.shape[1] // head_dim
    per_group = query_heads // key_heads
    scale = head_dim ** (-0.5)
    block = min(row_block, seq_len)
    blocks = seq_len // block
    offset = lax.axis_index("tensor") * local_len
    cos_table, sin_table = rope_tables(seq_len, head_dim)
    grad_attn_gain = jnp.zeros(attn_gain.shape, jnp.float32)
    grad_ffn_gain = jnp.zeros(ffn_gain.shape, jnp.float32)
    grad_query_gain = jnp.zeros(query_gain.shape, jnp.float32)
    grad_key_gain = jnp.zeros(key_gain.shape, jnp.float32)
    normed_list = []
    query_list = []
    key_list = []
    value_list = []
    attended_list = []
    attn_in_list = []
    normed_two_list = []
    gate_list = []
    up_list = []
    active_list = []
    down_in_list = []
    outputs = []
    input_grads = []
    for slot_index in range(slots):
        segment = segment_ids[slot_index]
        alive_row = padding[slot_index] * (slot_index < row_count[0]).astype(jnp.int32)
        alive_local = lax.dynamic_slice_in_dim(alive_row, offset, local_len).astype(jnp.float32)
        rows_in = inputs[slot_index].astype(jnp.float32)
        scale_one = rms_scale(rows_in)
        unit_one = rows_in * scale_one
        normed = lax.all_gather(
            (unit_one * attn_gain).astype(jnp.bfloat16), "tensor", axis=0, tiled=True
        )
        query_proj = jnp.dot(normed, query_weight, preferred_element_type=jnp.float32).reshape(
            seq_len, query_heads, head_dim
        )
        key_proj = jnp.dot(normed, key_weight, preferred_element_type=jnp.float32).reshape(
            seq_len, key_heads, head_dim
        )
        values = (
            jnp.dot(normed, value_weight, preferred_element_type=jnp.float32)
            .astype(jnp.bfloat16)
            .reshape(seq_len, key_heads, head_dim)
        )
        query_scale = rms_scale(query_proj)
        query_unit = query_proj * query_scale
        queries = (
            rotate(query_unit * query_gain, cos_table, sin_table)
            .astype(jnp.bfloat16)
            .reshape(seq_len, key_heads, per_group, head_dim)
        )
        key_scale = rms_scale(key_proj)
        key_unit = key_proj * key_scale
        keys_all = rotate(key_unit * key_gain, cos_table, sin_table).astype(jnp.bfloat16)
        attended_parts = []
        log_totals = []
        for block_index in range(blocks):
            start_row = block_index * block
            count_keys = start_row + block
            allowed = allowed_block(segment, alive_row, start_row, block, count_keys)
            scores = block_scores(
                queries[start_row : start_row + block], keys_all[:count_keys], allowed, scale
            )
            row_peak = jnp.max(scores, axis=-1, keepdims=True)
            exponent = jnp.exp(scores - row_peak)
            row_total = jnp.sum(exponent, axis=-1, keepdims=True)
            weights_soft = (exponent / row_total).astype(jnp.bfloat16)
            attended_parts.append(
                jnp.einsum(
                    "grij,jgd->igrd",
                    weights_soft,
                    values[:count_keys],
                    preferred_element_type=jnp.float32,
                )
            )
            log_totals.append(row_peak + jnp.log(row_total))
        attended = (
            jnp.concatenate(attended_parts, axis=0)
            .reshape(seq_len, query_heads * head_dim)
            .astype(jnp.bfloat16)
        )
        hidden = rows_in + lax.psum_scatter(
            jnp.dot(attended, out_weight, preferred_element_type=jnp.float32).astype(jnp.bfloat16),
            "tensor",
            scatter_dimension=0,
            tiled=True,
        ).astype(jnp.float32)
        scale_two = rms_scale(hidden)
        unit_two = hidden * scale_two
        normed_two = lax.all_gather(
            (unit_two * ffn_gain).astype(jnp.bfloat16), "tensor", axis=0, tiled=True
        )
        gate_value = jnp.dot(normed_two, gate_weight, preferred_element_type=jnp.float32)
        upward = jnp.dot(normed_two, up_weight, preferred_element_type=jnp.float32)
        active = (jax.nn.silu(gate_value) * upward).astype(jnp.bfloat16)
        result = hidden + lax.psum_scatter(
            jnp.dot(active, down_weight, preferred_element_type=jnp.float32).astype(jnp.bfloat16),
            "tensor",
            scatter_dimension=0,
            tiled=True,
        ).astype(jnp.float32)
        outputs.append(result.astype(jnp.bfloat16))
        out_cot = cotangent[slot_index].astype(jnp.float32) * alive_local[:, None]
        down_in = lax.all_gather(out_cot.astype(jnp.bfloat16), "tensor", axis=0, tiled=True)
        active_grad = jnp.einsum(
            "sd,fd->sf", down_in, down_weight, preferred_element_type=jnp.float32
        )
        sigma = jax.nn.sigmoid(gate_value)
        gate_rows = (active_grad * upward * sigma * (1.0 + gate_value * (1.0 - sigma))).astype(
            jnp.bfloat16
        )
        up_rows = (active_grad * gate_value * sigma).astype(jnp.bfloat16)
        normed_two_list.append(normed_two)
        gate_list.append(gate_rows)
        up_list.append(up_rows)
        active_list.append(active)
        down_in_list.append(down_in)
        normed_two_grad = lax.psum_scatter(
            (
                jnp.einsum("sf,df->sd", gate_rows, gate_weight, preferred_element_type=jnp.float32)
                + jnp.einsum("sf,df->sd", up_rows, up_weight, preferred_element_type=jnp.float32)
            ).astype(jnp.bfloat16),
            "tensor",
            scatter_dimension=0,
            tiled=True,
        ).astype(jnp.float32)
        grad_ffn_gain = grad_ffn_gain + jnp.sum(normed_two_grad * unit_two, axis=0)
        hidden_grad = out_cot + norm_back(normed_two_grad, unit_two, scale_two, ffn_gain)
        attn_in = lax.all_gather(hidden_grad.astype(jnp.bfloat16), "tensor", axis=0, tiled=True)
        attended_list.append(attended)
        attn_in_list.append(attn_in)
        attended_grad = (
            jnp.einsum("sd,ed->se", attn_in, out_weight, preferred_element_type=jnp.float32)
            .astype(jnp.bfloat16)
            .reshape(seq_len, key_heads, per_group, head_dim)
        )
        value_acc = jnp.zeros((seq_len, key_heads, head_dim), jnp.float32)
        key_acc = jnp.zeros((seq_len, key_heads, head_dim), jnp.float32)
        query_parts = []
        for block_index in range(blocks):
            start_row = block_index * block
            count_keys = start_row + block
            allowed = allowed_block(segment, alive_row, start_row, block, count_keys)
            query_block = queries[start_row : start_row + block]
            scores = block_scores(query_block, keys_all[:count_keys], allowed, scale)
            soft_rows = jnp.exp(scores - log_totals[block_index])
            soft_low = soft_rows.astype(jnp.bfloat16)
            grad_block = attended_grad[start_row : start_row + block]
            value_acc = value_acc.at[:count_keys].add(
                jnp.einsum(
                    "grij,igrd->jgd", soft_low, grad_block, preferred_element_type=jnp.float32
                )
            )
            prob_grad = jnp.einsum(
                "igrd,jgd->grij",
                grad_block,
                values[:count_keys],
                preferred_element_type=jnp.float32,
            )
            row_inner = jnp.sum(prob_grad * soft_rows, axis=-1, keepdims=True)
            score_grad = (soft_rows * (prob_grad - row_inner)).astype(jnp.bfloat16)
            query_parts.append(
                jnp.einsum(
                    "grij,jgd->igrd",
                    score_grad,
                    keys_all[:count_keys],
                    preferred_element_type=jnp.float32,
                )
                * scale
            )
            key_acc = key_acc.at[:count_keys].add(
                jnp.einsum(
                    "grij,igrd->jgd", score_grad, query_block, preferred_element_type=jnp.float32
                )
                * scale
            )
        value_rows = value_acc.astype(jnp.bfloat16).reshape(seq_len, key_heads * head_dim)
        query_rot = (
            jnp.concatenate(query_parts, axis=0)
            .astype(jnp.bfloat16)
            .astype(jnp.float32)
            .reshape(seq_len, query_heads, head_dim)
        )
        key_rot = key_acc.astype(jnp.bfloat16).astype(jnp.float32)
        query_norm_grad = rotate_back(query_rot, cos_table, sin_table)
        key_norm_grad = rotate_back(key_rot, cos_table, sin_table)
        grad_query_gain = grad_query_gain + jnp.sum(query_norm_grad * query_unit, axis=(0, 1))
        grad_key_gain = grad_key_gain + jnp.sum(key_norm_grad * key_unit, axis=(0, 1))
        query_rows = (
            norm_back(query_norm_grad, query_unit, query_scale, query_gain)
            .astype(jnp.bfloat16)
            .reshape(seq_len, query_heads * head_dim)
        )
        key_rows = (
            norm_back(key_norm_grad, key_unit, key_scale, key_gain)
            .astype(jnp.bfloat16)
            .reshape(seq_len, key_heads * head_dim)
        )
        normed_list.append(normed)
        query_list.append(query_rows)
        key_list.append(key_rows)
        value_list.append(value_rows)
        normed_grad = lax.psum_scatter(
            (
                jnp.einsum(
                    "se,de->sd", query_rows, query_weight, preferred_element_type=jnp.float32
                )
                + jnp.einsum("se,de->sd", key_rows, key_weight, preferred_element_type=jnp.float32)
                + jnp.einsum(
                    "se,de->sd", value_rows, value_weight, preferred_element_type=jnp.float32
                )
            ).astype(jnp.bfloat16),
            "tensor",
            scatter_dimension=0,
            tiled=True,
        ).astype(jnp.float32)
        grad_attn_gain = grad_attn_gain + jnp.sum(normed_grad * unit_one, axis=0)
        input_grads.append(hidden_grad + norm_back(normed_grad, unit_one, scale_one, attn_gain))
    grad_query = outer_sum(normed_list, query_list)
    grad_key = outer_sum(normed_list, key_list)
    grad_value = outer_sum(normed_list, value_list)
    grad_out = outer_sum(attended_list, attn_in_list)
    grad_gate = outer_sum(normed_two_list, gate_list)
    grad_up = outer_sum(normed_two_list, up_list)
    grad_down = outer_sum(active_list, down_in_list)
    query_sum, key_sum, value_sum, out_sum, gate_sum, up_sum, down_sum = (
        lax.psum_scatter(grad_query, "dp", scatter_dimension=0, tiled=True),
        lax.psum_scatter(grad_key, "dp", scatter_dimension=0, tiled=True),
        lax.psum_scatter(grad_value, "dp", scatter_dimension=0, tiled=True),
        lax.psum_scatter(grad_out, "dp", scatter_dimension=0, tiled=True),
        lax.psum_scatter(grad_gate, "dp", scatter_dimension=0, tiled=True),
        lax.psum_scatter(grad_up, "dp", scatter_dimension=0, tiled=True),
        lax.psum_scatter(grad_down, "dp", scatter_dimension=0, tiled=True),
    )
    gain_sums = lax.psum(
        (grad_attn_gain, grad_ffn_gain, grad_query_gain, grad_key_gain), ("dp", "tensor")
    )
    return (
        jnp.stack(outputs),
        jnp.stack(input_grads),
        query_sum,
        key_sum,
        value_sum,
        out_sum,
        gate_sum,
        up_sum,
        down_sum,
        gain_sums[0],
        gain_sums[1],
        gain_sums[2],
        gain_sums[3],
    )


def solution(mesh):
    return jax.shard_map(
        per_device,
        mesh=mesh,
        in_specs=(
            P("dp", "tensor", None),
            P(None, "tensor"),
            P(None, "tensor"),
            P(None, "tensor"),
            P("tensor", None),
            P(None, "tensor"),
            P(None, "tensor"),
            P("tensor", None),
            P(),
            P(),
            P(),
            P(),
            P("dp", "tensor", None),
            P("dp", None),
            P("dp", None),
            P("dp"),
        ),
        out_specs=(
            P("dp", "tensor", None),
            P("dp", "tensor", None),
            P("dp", "tensor"),
            P("dp", "tensor"),
            P("dp", "tensor"),
            P(("tensor", "dp"), None),
            P("dp", "tensor"),
            P("dp", "tensor"),
            P(("tensor", "dp"), None),
            P(),
            P(),
            P(),
            P(),
        ),
        check_vma=False,
    )
```

profile of v0, /device:TPU:9, one launch (start us, length us, event | category | flops | bytes accessed | tf_op | source)
XLA Modules:
  0.0 1153.2 jit_solution(7343258783926955106)
XLA Ops:
  19.4 37.5 %all-gather.13.cloned.1.call-done = bf16[1024,1024]{1,0:T(8,128)(2,1)} async-done(((bf16[256,1024]{1,0:T(8,128)(2,1)}), bf16[1024,1024]{1,0:T(8,128)(2,1)}) %all-gather.13.cloned.1.call-update) | async-done | bytes 2097168 | tf_op jit(solution)/shard_map/all_gather | solution.py:129
  63.3 40.4 %all-gather.9.cloned.1.call-done = bf16[1024,1024]{1,0:T(8,128)(2,1)} async-done(((bf16[256,1024]{1,0:T(8,128)(2,1)}), bf16[1024,1024]{1,0:T(8,128)(2,1)}) %all-gather.9.cloned.1.call-update) | async-done | bytes 2097168 | tf_op jit(solution)/shard_map/all_gather | solution.py:129
  142.4 25.8 %reduce-scatter.20.cloned.1.call-done = bf16[256,1024]{1,0:T(8,128)(2,1)} async-done(((bf16[1024,1024]{1,0:T(8,128)(2,1)}), bf16[256,1024]{1,0:T(8,128)(2,1)}) %reduce-scatter.20.cloned.1.call-update) | async-done | bytes 524304 | tf_op jit(solution)/shard_map/reduce_scatter | solution.py:180
  168.2 46.0 %reduce-scatter.16.cloned.1.call-done = bf16[256,1024]{1,0:T(8,128)(2,1)} async-done(((bf16[1024,1024]{1,0:T(8,128)(2,1)}), bf16[256,1024]{1,0:T(8,128)(2,1)}) %reduce-scatter.16.cloned.1.call-update) | async-done | bytes 524304 | tf_op jit(solution)/shard_map/reduce_scatter | solution.py:180
  224.4 40.6 %all-gather.15.cloned.1.call-done = bf16[1024,1024]{1,0:T(8,128)(2,1)} async-done(((bf16[256,1024]{1,0:T(8,128)(2,1)}), bf16[1024,1024]{1,0:T(8,128)(2,1)}) %all-gather.15.cloned.1.call-update) | async-done | bytes 2097168 | tf_op jit(solution)/shard_map/all_gather | solution.py:188
  277.1 34.7 %all-gather.21.cloned.1.call-done = bf16[1024,1024]{1,0:T(8,128)(2,1)} async-done(((bf16[256,1024]{1,0:T(8,128)(2,1)}), bf16[1024,1024]{1,0:T(8,128)(2,1)}) %all-gather.21.cloned.1.call-update) | async-done | bytes 2097168 | tf_op jit(solution)/shard_map/all_gather | solution.py:202
  329.0 29.5 %all-gather.11.cloned.1.call-done = bf16[1024,1024]{1,0:T(8,128)(2,1)} async-done(((bf16[256,1024]{1,0:T(8,128)(2,1)}), bf16[1024,1024]{1,0:T(8,128)(2,1)}) %all-gather.11.cloned.1.call-update) | async-done | bytes 2097168 | tf_op jit(solution)/shard_map/all_gather | solution.py:188
  370.6 34.2 %all-gather.17.cloned.1.call-done = bf16[1024,1024]{1,0:T(8,128)(2,1)} async-done(((bf16[256,1024]{1,0:T(8,128)(2,1)}), bf16[1024,1024]{1,0:T(8,128)(2,1)}) %all-gather.17.cloned.1.call-update) | async-done | bytes 2097168 | tf_op jit(solution)/shard_map/all_gather | solution.py:202
  433.7 15.5 %reduce-scatter.28.cloned.1.call-done = bf16[256,1024]{1,0:T(8,128)(2,1)} async-done(((bf16[1024,1024]{1,0:T(8,128)(2,1)}), bf16[256,1024]{1,0:T(8,128)(2,1)}) %reduce-scatter.28.cloned.1.call-update) | async-done | bytes 524304 | tf_op jit(solution)/shard_map/reduce_scatter | solution.py:216
  449.2 46.0 %reduce-scatter.24.cloned.1.call-done = bf16[256,1024]{1,0:T(8,128)(2,1)} async-done(((bf16[1024,1024]{1,0:T(8,128)(2,1)}), bf16[256,1024]{1,0:T(8,128)(2,1)}) %reduce-scatter.24.cloned.1.call-update) | async-done | bytes 524304 | tf_op jit(solution)/shard_map/reduce_scatter | solution.py:216
  498.3 42.4 %reduce-scatter.22.cloned.1.call-done = bf16[256,1024]{1,0:T(8,128)(2,1)} async-done(((bf16[1024,1024]{1,0:T(8,128)(2,1)}), bf16[256,1024]{1,0:T(8,128)(2,1)}) %reduce-scatter.22.cloned.1.call-update) | async-done | bytes 524304 | tf_op jit(solution)/shard_map/reduce_scatter | solution.py:194
  540.8 45.5 %reduce-scatter.18.cloned.1.call-done = bf16[256,1024]{1,0:T(8,128)(2,1)} async-done(((bf16[1024,1024]{1,0:T(8,128)(2,1)}), bf16[256,1024]{1,0:T(8,128)(2,1)}) %reduce-scatter.18.cloned.1.call-update) | async-done | bytes 524304 | tf_op jit(solution)/shard_map/reduce_scatter | solution.py:194
  593.6 43.1 %all-gather.23.cloned.1.call-done = bf16[1024,1024]{1,0:T(8,128)(2,1)} async-done(((bf16[256,1024]{1,0:T(8,128)(2,1)}), bf16[1024,1024]{1,0:T(8,128)(2,1)}) %all-gather.23.cloned.1.call-update) | async-done | bytes 2097168 | tf_op jit(solution)/shard_map/all_gather | solution.py:227
  645.7 37.8 %all-gather.19.cloned.1.call-done = bf16[1024,1024]{1,0:T(8,128)(2,1)} async-done(((bf16[256,1024]{1,0:T(8,128)(2,1)}), bf16[1024,1024]{1,0:T(8,128)(2,1)}) %all-gather.19.cloned.1.call-update) | async-done | bytes 2097168 | tf_op jit(solution)/shard_map/all_gather | solution.py:227
  741.4 11.0 fusion.18
  797.4 16.7 %reduce-scatter.30.cloned.1.call-done = bf16[256,1024]{1,0:T(8,128)(2,1)} async-done(((bf16[1024,1024]{1,0:T(8,128)(2,1)}), bf16[256,1024]{1,0:T(8,128)(2,1)}) %reduce-scatter.30.cloned.1.call-update) | async-done | bytes 524304 | tf_op jit(solution)/shard_map/reduce_scatter | solution.py:301
  816.1 42.4 %all-reduce.4 = (f32[1024]{0:T(1024)}, f32[1024]{0:T(1024)}, f32[64]{0:T(128)}, f32[64]{0:T(128)}) all-reduce(f32[1024]{0:T(1024)S(1)} %add.361, f32[1024]{0:T(1024)S(1)} %add.362, f32[64]{0:T(128)S(1)} %add.363, f32[64]{0:T(128)S(1)} %add.364), channel_id=1, replica_groups=mesh['dp'=8,'tensor'=4] {'dp','tensor'}, use_global_device_ids=true, to_apply=%region_45.46 | all-reduce | flops 2176 | bytes 17408 | tf_op jit(solution)/shard_map/psum | solution.py:333
  862.7 11.5 reduce-scatter.44.cloned.1.call-done
  874.2 58.2 %reduce-scatter.40.cloned.1.call-done = f32[128,1152]{1,0:T(8,128)} async-done(((f32[1024,1152]{1,0:T(8,128)}), f32[128,1152]{1,0:T(8,128)}) %reduce-scatter.40.cloned.1.call-update) | async-done | bytes 589840 | tf_op jit(solution)/shard_map/reduce_scatter | solution.py:329
  932.4 57.9 %reduce-scatter.42.cloned.1.call-done = f32[128,1152]{1,0:T(8,128)} async-done(((f32[1024,1152]{1,0:T(8,128)}), f32[128,1152]{1,0:T(8,128)}) %reduce-scatter.42.cloned.1.call-update) | async-done | bytes 589840 | tf_op jit(solution)/shard_map/reduce_scatter | solution.py:330
  990.3 37.5 %reduce-scatter.36.cloned.1.call-done = f32[128,128]{1,0:T(8,128)} async-done(((f32[1024,128]{1,0:T(8,128)}), f32[128,128]{1,0:T(8,128)}) %reduce-scatter.36.cloned.1.call-update) | async-done | bytes 65552 | tf_op jit(solution)/shard_map/reduce_scatter | solution.py:327
  1027.8 37.8 %reduce-scatter.34.cloned.1.call-done = f32[128,128]{1,0:T(8,128)} async-done(((f32[1024,128]{1,0:T(8,128)}), f32[128,128]{1,0:T(8,128)}) %reduce-scatter.34.cloned.1.call-update) | async-done | bytes 65552 | tf_op jit(solution)/shard_map/reduce_scatter | solution.py:326
  1065.6 40.5 %reduce-scatter.38.cloned.1.call-done = f32[32,1024]{1,0:T(8,128)} async-done(((f32[256,1024]{1,0:T(8,128)}), f32[32,1024]{1,0:T(8,128)}) %reduce-scatter.38.cloned.1.call-update) | async-done | bytes 131088 | tf_op jit(solution)/shard_map/reduce_scatter | solution.py:328
  1106.1 40.1 %reduce-scatter.32.cloned.1.call-done = f32[128,256]{1,0:T(8,128)} async-done(((f32[1024,256]{1,0:T(8,128)}), f32[128,256]{1,0:T(8,128)}) %reduce-scatter.32.cloned.1.call-update) | async-done | bytes 131088 | tf_op jit(solution)/shard_map/reduce_scatter | solution.py:325
  (524 shorter events, 263.0 us)
Async XLA Ops:
  7.2 304.6 %copy-start = (bf16[1152,1024]{1,0:T(8,128)(2,1)S(1)}, bf16[1152,1024]{1,0:T(8,128)(2,1)}, u32[]{:S(2)}) copy-start(bf16[1152,1024]{1,0:T(8,128)(2,1)} %param.47) | copy-start | bytes 7077892
  7.2 49.7 %all-gather.13.cloned.1.call-start = ((), (), s32[]{:S(2)}) async-start(), calls=%async_computation.19 | async-start | bytes 2621440 | tf_op jit(solution)/shard_map/all_gather | solution.py:129
  11.5 92.3 %all-gather.9.cloned.1.call-start = ((), (), s32[]{:S(2)}) async-start(), calls=%async_computation.15 | async-start | bytes 2621440 | tf_op jit(solution)/shard_map/all_gather | solution.py:129
  12.2 156.0 %reduce-scatter.20.cloned.1.call-start = ((), (), s32[]{:S(2)}) async-start(), calls=%async_computation.20 | async-start | bytes 2621440 | tf_op jit(solution)/shard_map/reduce_scatter | solution.py:180
  126.0 88.2 %reduce-scatter.16.cloned.1.call-start = ((), (), s32[]{:S(2)}) async-start(), calls=%async_computation.16 | async-start | bytes 2621440 | tf_op jit(solution)/shard_map/reduce_scatter | solution.py:180
  142.4 122.7 %all-gather.15.cloned.1.call-start = ((), (), s32[]{:S(2)}) async-start(), calls=%async_computation.21 | async-start | bytes 2621440 | tf_op jit(solution)/shard_map/all_gather | solution.py:188
  219.1 92.6 %all-gather.21.cloned.1.call-start = ((), (), s32[]{:S(2)}) async-start(), calls=%async_computation.27 | async-start | bytes 2621440 | tf_op jit(solution)/shard_map/all_gather | solution.py:202
  222.9 135.7 %all-gather.11.cloned.1.call-start = ((), (), s32[]{:S(2)}) async-start(), calls=%async_computation.17 | async-start | bytes 2621440 | tf_op jit(solution)/shard_map/all_gather | solution.py:188
  223.6 181.2 %all-gather.17.cloned.1.call-start = ((), (), s32[]{:S(2)}) async-start(), calls=%async_computation.23 | async-start | bytes 2621440 | tf_op jit(solution)/shard_map/all_gather | solution.py:202
  224.4 224.9 %reduce-scatter.28.cloned.1.call-start = ((), (), s32[]{:S(2)}) async-start(), calls=%async_computation.28 | async-start | bytes 2621440 | tf_op jit(solution)/shard_map/reduce_scatter | solution.py:216
  328.8 166.4 %reduce-scatter.24.cloned.1.call-start = ((), (), s32[]{:S(2)}) async-start(), calls=%async_computation.24 | async-start | bytes 2621440 | tf_op jit(solution)/shard_map/reduce_scatter | solution.py:216
  421.7 119.0 %reduce-scatter.22.cloned.1.call-start = ((), (), s32[]{:S(2)}) async-start(), calls=%async_computation.22 | async-start | bytes 2621440 | tf_op jit(solution)/shard_map/reduce_scatter | solution.py:194
  427.7 158.6 %reduce-scatter.18.cloned.1.call-start = ((), (), s32[]{:S(2)}) async-start(), calls=%async_computation.18 | async-start | bytes 2621440 | tf_op jit(solution)/shard_map/reduce_scatter | solution.py:194
  433.6 203.1 %all-gather.23.cloned.1.call-start = ((), (), s32[]{:S(2)}) async-start(), calls=%async_computation.29 | async-start | bytes 2621440 | tf_op jit(solution)/shard_map/all_gather | solution.py:227
  590.8 92.6 %all-gather.19.cloned.1.call-start = ((), (), s32[]{:S(2)}) async-start(), calls=%async_computation.25 | async-start | bytes 2621440 | tf_op jit(solution)/shard_map/all_gather | solution.py:227
  591.4 206.0 %reduce-scatter.26.cloned.1.call-start = ((), (), s32[]{:S(2)}) async-start(), calls=%async_computation.26 | async-start | bytes 2621440 | tf_op jit(solution)/shard_map/reduce_scatter | solution.py:301
  726.5 87.6 %reduce-scatter.30.cloned.1.call-start = ((), (), s32[]{:S(2)}) async-start(), calls=%async_computation.30 | async-start | bytes 2621440 | tf_op jit(solution)/shard_map/reduce_scatter | solution.py:301
  741.3 132.9 %reduce-scatter.44.cloned.1.call-start = ((), (), s32[]{:S(2)}) async-start(), calls=%async_computation.37 | async-start | bytes 5308416 | tf_op jit(solution)/shard_map/reduce_scatter | solution.py:331
  752.3 180.1 %reduce-scatter.40.cloned.1.call-start = ((), (), s32[]{:S(2)}) async-start(), calls=%async_computation.35 | async-start | bytes 5308416 | tf_op jit(solution)/shard_map/reduce_scatter | solution.py:329
  764.3 226.0 %reduce-scatter.42.cloned.1.call-start = ((), (), s32[]{:S(2)}) async-start(), calls=%async_computation.36 | async-start | bytes 5308416 | tf_op jit(solution)/shard_map/reduce_scatter | solution.py:330
  775.5 252.3 %reduce-scatter.36.cloned.1.call-start = ((), (), s32[]{:S(2)}) async-start(), calls=%async_computation.33 | async-start | bytes 589824 | tf_op jit(solution)/shard_map/reduce_scatter | solution.py:327
  782.0 283.6 %reduce-scatter.34.cloned.1.call-start = ((), (), s32[]{:S(2)}) async-start(), calls=%async_computation.32 | async-start | bytes 589824 | tf_op jit(solution)/shard_map/reduce_scatter | solution.py:326
  786.4 319.7 %reduce-scatter.38.cloned.1.call-start = ((), (), s32[]{:S(2)}) async-start(), calls=%async_computation.34 | async-start | bytes 1179648 | tf_op jit(solution)/shard_map/reduce_scatter | solution.py:328
  791.2 355.1 %reduce-scatter.32.cloned.1.call-start = ((), (), s32[]{:S(2)}) async-start(), calls=%async_computation.31 | async-start | bytes 1179648 | tf_op jit(solution)/shard_map/reduce_scatter | solution.py:325
  (162 other events, 3300.3 us)
Sparse Core Ops, SparseCore 0:
  11.6 45.2 all-gather.12
  59.1 44.6 all-gather.8
  126.1 42.0 reduce-scatter.19
  171.1 43.1 reduce-scatter.15
  219.2 45.7 all-gather.14
  267.0 44.6 all-gather.20
  313.9 44.6 all-gather.10
  360.1 44.6 all-gather.16
  407.1 42.0 reduce-scatter.27
  452.0 43.1 reduce-scatter.23
  497.5 43.1 reduce-scatter.21
  543.0 43.1 reduce-scatter.17
  590.9 45.7 all-gather.22
  638.7 44.6 all-gather.18
  726.7 42.2 reduce-scatter.25
  771.2 42.8 reduce-scatter.29
  818.0 56.1 reduce-scatter.43
  878.5 53.8 reduce-scatter.39
  936.4 53.8 reduce-scatter.41
  994.1 33.6 reduce-scatter.35
  1031.5 34.1 reduce-scatter.33
  1069.7 36.3 reduce-scatter.37
  1110.2 36.0 reduce-scatter.31
where the time goes:
time: 1170 us; the launch traced here: 1150 us
  waiting for transfers between devices  822 us (70%)
  matrix products  185 us (16%)
  other arithmetic  59.7 us (5%)
  blocking collectives  42.4 us (4%)
  local copies, waits for them, and re-layouts  23.8 us (2%)
  between operations  17.3 us (1%)
    reduce_scatter x2, waiting for transfers between devices, per_device(): lax.psum_scatter(jnp.dot(active, down_weight, preferred_element_type=jnp....  87.9 us
    all_gather x2, waiting for transfers between devices, per_device(): lax.all_gather(hidden_grad.astype(jnp.bfloat16), 'tensor', axis=0, tiled=...  80.9 us
    all_gather x2, waiting for transfers between devices, per_device(): lax.all_gather((unit_one * attn_gain).astype(jnp.bfloat16), 'tensor', axi...  78 us
    reduce_scatter x2, waiting for transfers between devices, per_device(): lax.psum_scatter(jnp.dot(attended, out_weight, preferred_element_type=jnp...  71.8 us
    all_gather x2, waiting for transfers between devices, per_device(): lax.all_gather((unit_two * ffn_gain).astype(jnp.bfloat16), 'tensor', axis...  70.2 us
    all_gather x2, waiting for transfers between devices, per_device(): lax.all_gather(out_cot.astype(jnp.bfloat16), 'tensor', axis=0, tiled=True)  68.9 us
    reduce_scatter x2, waiting for transfers between devices, per_device(): lax.psum_scatter((jnp.einsum('sf,df->sd', gate_rows, gate_weight, preferr...  61.6 us
    reduce_scatter x1, waiting for transfers between devices, per_device(): lax.psum_scatter(grad_gate, 'dp', scatter_dimension=0, tiled=True)  58.2 us
  transfers between devices with their start and end apart: 23, of which 22 were waited for; matrix products, arithmetic and copies ran while one was open for 16% of the time, Pallas kernels for 0%

commit v1 on v0

v1 whole, which is shorter than its diff:
```python
import functools

import jax
import jax.numpy as jnp
from jax import lax
from jax.experimental import pallas as pl
from jax.experimental.pallas import tpu as pltpu
from jax.sharding import PartitionSpec as P

EPS = 1e-05
THETA = 1000000.0
MASKED = -1e30
row_block = 512
ALIVE = 4096
MESH = pl.DeviceIdType.MESH
BF16 = jnp.bfloat16
F32 = jnp.float32


class Place:
    def __init__(self):
        self.dp = lax.axis_index("dp")
        self.z = lax.axis_index("tensor")
        self.c = lax.rem(self.dp, 2)
        self.j = lax.rem(self.dp // 2, 4)
        self.half = self.z // 2
        self.par = lax.rem(self.z, 2)
        self.near = self.half == self.c

    def plane(self, k):
        j = self.j
        bit = lax.rem(j // k, 2)
        return (self.dp + (1 - 2 * bit) * 2 * k, self.z)

    def column(self, c, z):
        return (self.dp - self.c + c, z)

    def quarter(self, k):
        j = self.j
        low, high = lax.rem(j, 2), j // 2
        if k & 1:
            low = 1 - low
        if k & 2:
            high = 1 - high
        return 2 * high + low


def greet(place):
    barrier = pltpu.get_barrier_semaphore()
    for k in (1, 2):
        pl.semaphore_signal(barrier, inc=1, device_id=place.plane(k), device_id_type=MESH)
    for dc in range(2):
        for dz in range(4):
            if dc or dz:
                c = lax.rem(place.c + dc, 2)
                z = lax.rem(place.z + dz, 4)
                pl.semaphore_signal(barrier, inc=1, device_id=place.column(c, z), device_id_type=MESH)
    pl.semaphore_wait(barrier, 9)


def remote(src, dst, send, recv, device):
    return pltpu.make_async_remote_copy(
        src_ref=src, dst_ref=dst, send_sem=send, recv_sem=recv, device_id=device, device_id_type=MESH
    )


def gather_kernel(nw, x_ref, ct_ref, *refs):
    shards = refs[:nw]
    xo, co = refs[nw : nw + 2]
    full = refs[nw + 2 : 2 * nw + 2]
    tok_s, tok_r, tok_l, own_l, zs, zr, fs, fr = refs[2 * nw + 2 :]
    place = Place()
    z, c, par, near, j = place.z, place.c, place.par, place.near, place.j
    seg = x_ref.shape[1]
    greet(place)

    def token_copies(a, src, dst, go):
        for b in range(2):
            slot = par if b == 0 else 1 - par
            target = place.column(place.half, 2 * c + slot)
            here = dst.at[pl.ds(pl.multiple_of(par * seg, seg), seg)]
            if b == 0:
                @pl.when(near)
                def _():
                    cp = pltpu.make_async_copy(src.at[slot], here, tok_l.at[a])
                    cp.start() if go else cp.wait()

                @pl.when(jnp.logical_not(near))
                def _():
                    cp = remote(src.at[slot], here, tok_s.at[a, b], tok_r.at[a, par], target)
                    cp.start() if go else cp.wait_send()
            else:
                cp = remote(src.at[slot], here, tok_s.at[a, b], tok_r.at[a, par], target)
                cp.start() if go else cp.wait_send()

    def token_arrivals(a, src, dst):
        for h in range(2):
            @pl.when(jnp.logical_not(near & (par == h)))
            def _():
                remote(src.at[0], dst.at[pl.ds(h * seg, seg)], tok_s.at[a, 0], tok_r.at[a, h], place.plane(1)).wait_recv()

    def z_copies(w, go):
        q = shards[w].shape[0] // 4
        rows = pl.ds(pl.multiple_of(j * q, q), q)

        @pl.when(near)
        def _():
            cp = pltpu.make_async_copy(shards[w], full[w].at[par], own_l.at[w])
            cp.start() if go else cp.wait()
            far = 2 - 2 * place.half
            for i, to in enumerate((2 * place.half + 1 - par, far + par, far + 1 - par)):
                cp = remote(shards[w].at[rows], full[w].at[par, rows], zs.at[w, i], zr.at[w, par], place.column(c, to))
                cp.start() if go else cp.wait_send()

    def part(w, p, k, half=None):
        q = shards[w].shape[0] // 4
        start, size = pl.multiple_of(place.quarter(k) * q, q), q
        if half is not None:
            size = q // 2
            start = pl.multiple_of(start + half * size, size)
        return full[w].at[p, pl.ds(start, size)]

    def missing(p, body):
        pl.when(jnp.logical_or(jnp.logical_not(near), par != p))(body)

    def step_copy(w, p, i):
        k, half, to = ((0, None, 1), (0, None, 2), (1, 0, 2), (2, 1, 1))[i]
        return remote(part(w, p, k, half), part(w, p, k, half), fs.at[w, p, i], fr.at[w, p, i], place.plane(to))

    token_copies(0, x_ref, xo, True)
    for w in range(nw):
        z_copies(w, True)
        if w == 1:
            token_copies(1, ct_ref, co, True)

    def first(w):
        for p in range(2):
            @functools.partial(missing, p)
            def _():
                remote(part(w, p, 0), part(w, p, 0), zs.at[w, 0], zr.at[w, p], place.plane(1)).wait_recv()
                step_copy(w, p, 0).start()
                step_copy(w, p, 1).start()

    def second(w):
        for p in range(2):
            @functools.partial(missing, p)
            def _():
                step_copy(w, p, 0).wait_recv()
                step_copy(w, p, 2).start()
                step_copy(w, p, 1).wait_recv()
                step_copy(w, p, 3).start()

    for w in range(nw + 1):
        if w < nw:
            first(w)
        if w:
            second(w - 1)
    for w in range(nw):
        for p in range(2):
            @functools.partial(missing, p)
            def _():
                step_copy(w, p, 2).wait_recv()
                step_copy(w, p, 3).wait_recv()
                for i in range(4):
                    step_copy(w, p, i).wait_send()
    for w in range(nw):
        z_copies(w, False)
    for a, (src, dst) in enumerate(((x_ref, xo), (ct_ref, co))):
        token_copies(a, src, dst, False)
        token_arrivals(a, src, dst)


def gather(x, ct, shards):
    nw = len(shards)
    tokens = x.shape[0] * x.shape[1]
    anywhere = pl.BlockSpec(memory_space=pl.ANY)
    dma = pltpu.SemaphoreType.DMA
    out = pl.pallas_call(
        functools.partial(gather_kernel, nw),
        out_shape=[jax.ShapeDtypeStruct((tokens, x.shape[2]), x.dtype)] * 2
        + [jax.ShapeDtypeStruct((2,) + s.shape, s.dtype) for s in shards],
        in_specs=[anywhere] * (2 + nw),
        out_specs=[anywhere] * (2 + nw),
        scratch_shapes=[
            dma((2, 2)), dma((2, 2)), dma((2,)), dma((nw,)), dma((nw, 3)), dma((nw, 2)), dma((nw, 2, 4)), dma((nw, 2, 4)),
        ],
        compiler_params=pltpu.CompilerParams(collective_id=0, has_side_effects=True),
        name="gather",
    )(x, ct, *shards)
    return out[0], out[1], out[2:]


def scatter_kernel(nw, o_ref, i_ref, gain_ref, *refs):
    grads = refs[:nw]
    oo, io, gain_out = refs[nw : nw + 3]
    sums = refs[nw + 3 : 2 * nw + 3]
    scr = refs[2 * nw + 3 :]
    diag, plane_in, col_in, mate = scr[:nw], scr[nw : 2 * nw], scr[2 * nw : 3 * nw], scr[3 * nw : 4 * nw]
    gain_in, tok_s, tok_r, tok_l, ps, pr, cs, cr, ms, mr, gs, gr = scr[4 * nw :]
    place = Place()
    z, c, par, near, j = place.z, place.c, place.par, place.near, place.j
    seg = o_ref.shape[0] // 2
    greet(place)

    def token_copies(a, src, dst, go):
        for b in range(2):
            h = par if b == 0 else 1 - par
            piece = src.at[pl.ds(pl.multiple_of(h * seg, seg), seg)]
            target = place.column(place.half, 2 * c + h)
            there = dst.at[par]

            def far_copy():
                cp = remote(piece, there, tok_s.at[a, b], tok_r.at[a, par], target)
                cp.start() if go else cp.wait_send()

            if b == 0:
                @pl.when(near)
                def _():
                    cp = pltpu.make_async_copy(piece, there, tok_l.at[a])
                    cp.start() if go else cp.wait()

                pl.when(jnp.logical_not(near))(far_copy)
            else:
                far_copy()

    def token_arrivals(a, src, dst):
        for s in range(2):
            @pl.when(jnp.logical_not(near & (par == s)))
            def _():
                remote(src.at[pl.ds(0, seg)], dst.at[s], tok_s.at[a, 0], tok_r.at[a, s], place.plane(1)).wait_recv()

    def rows_of(w, k, half=None):
        q = grads[w].shape[1] // 4
        start, size = pl.multiple_of(place.quarter(k) * q, q), q
        if half is not None:
            size = q // 2
            start = pl.multiple_of(start + half * size, size)
        return pl.ds(start, size)

    def diag_copy(w, half):
        return remote(grads[w].at[:, rows_of(w, 3, half)], diag[w].at[half], ps.at[w, half], pr.at[w, half], place.plane(1 + half))

    def plane_copy(w, i, half):
        e = grads[w].shape[1] // 8
        src = grads[w].at[:, rows_of(w, 1 + i, half)] if half == i else diag[w].at[half]
        n = 2 + 2 * i + half
        return remote(src, plane_in[w].at[i, :, pl.ds(half * e, e)], ps.at[w, n], pr.at[w, n], place.plane(1 + i))

    token_copies(0, o_ref, oo, True)
    token_copies(1, i_ref, io, True)
    for w in range(nw):
        diag_copy(w, 0).start()
        diag_copy(w, 1).start()
        plane_copy(w, 0, 0).start()
        plane_copy(w, 1, 1).start()

    def gain_copy(i):
        to = (place.column(1 - c, z), place.plane(1), place.plane(2), place.column(c, 2 * place.half + 1 - par),
              place.column(c, 2 - 2 * place.half + par))[i]
        return remote(gain_out, gain_in.at[i], gs.at[i], gr.at[i], to)

    gain_out[...] = gain_ref[...]

    def add_diag(w):
        for half in (0, 1):
            diag_copy(w, half).wait()
            rows = rows_of(w, 2 - half, half)
            for p in range(2):
                diag[w][half, p] = (grads[w][p, rows, :].astype(F32) + diag[w][half, p].astype(F32)).astype(BF16)
            plane_copy(w, 1 - half, half).start()

    outer = jnp.where(c == 0, z == 3, z == 0)
    inner = jnp.where(c == 0, z == 2, z == 1)

    def outer_copy(w):
        return remote(plane_in[w].at[0], col_in[w], cs.at[w, 0], cr.at[w, 0], place.column(c, z - 1 + 2 * c))

    def inner_copy(w, p):
        return remote(plane_in[w].at[0, p], col_in[w].at[1], cs.at[w, p], cr.at[w, 1], place.column(c, 2 * c + p))

    def near_copy(w):
        to = place.column(c, 2 * place.half + 1 - par)
        return remote(plane_in[w].at[0, 1 - par], col_in[w].at[0], cs.at[w, 0], cr.at[w, 0], to)

    def mate_copy(w):
        return remote(mate[w].at[0], mate[w].at[1], ms.at[w], mr.at[w], place.column(1 - c, z))

    def add_plane(w):
        mine = rows_of(w, 0)
        for i in range(2):
            for half in range(2):
                plane_copy(w, i, half).wait()
        for p in range(2):
            total = grads[w][p, mine, :].astype(F32) + plane_in[w][0, p].astype(F32) + plane_in[w][1, p].astype(F32)
            plane_in[w][0, p] = total.astype(BF16)
        pl.when(outer)(lambda: outer_copy(w).start())
        pl.when(near)(lambda: near_copy(w).start())

    def add_outer(w):
        @pl.when(inner)
        def _():
            outer_copy(w).wait_recv()
            for p in range(2):
                plane_in[w][0, p] = (plane_in[w][0, p].astype(F32) + col_in[w][p].astype(F32)).astype(BF16)
                inner_copy(w, p).start()

    def add_column(w):
        @pl.when(near)
        def _():
            e = grads[w].shape[1] // 8
            near_copy(w).wait_recv()
            inner_copy(w, 0).wait_recv()
            for hc in range(2):
                here = pl.ds(hc * e, e)
                total = (
                    plane_in[w][0, par, here, :].astype(F32)
                    + col_in[w][0, here, :].astype(F32)
                    + col_in[w][1, here, :].astype(F32)
                )

                @pl.when(c == hc)
                def _():
                    sums[w][...] = total

                @pl.when(c != hc)
                def _():
                    mate[w][0] = total

            mate_copy(w).start()

    def finish(w):
        @pl.when(near)
        def _():
            mate_copy(w).wait_send()
            near_copy(w).wait_send()

        @pl.when(jnp.logical_not(near))
        def _():
            mate_copy(w).wait_recv()
            sums[w][...] = mate[w][1]

        pl.when(outer)(lambda: outer_copy(w).wait_send())

        @pl.when(inner)
        def _():
            inner_copy(w, 0).wait_send()
            inner_copy(w, 1).wait_send()

    for w in range(nw + 3):
        if w < nw:
            add_diag(w)
        if 0 <= w - 1 < nw:
            add_plane(w - 1)
        if 0 <= w - 2 < nw:
            add_outer(w - 2)
        if 0 <= w - 3 < nw:
            add_column(w - 3)
        if w < 5:
            gain_copy(w).start()
            gain_copy(w).wait()
            gain_out[...] += gain_in[w]
    for w in range(nw):
        finish(w)
    for a, (src, dst) in enumerate(((o_ref, oo), (i_ref, io))):
        token_copies(a, src, dst, False)
        token_arrivals(a, src, dst)


def scatter(o, i, gains, grads):
    nw = len(grads)
    assert nw + 3 >= 5
    seg = o.shape[0] // 2
    anywhere = pl.BlockSpec(memory_space=pl.ANY)
    vmem = pl.BlockSpec(memory_space=pltpu.VMEM)
    dma = pltpu.SemaphoreType.DMA
    shapes = [g.shape for g in grads]
    out = pl.pallas_call(
        functools.partial(scatter_kernel, nw),
        out_shape=[jax.ShapeDtypeStruct((2, seg, o.shape[1]), BF16)] * 2
        + [jax.ShapeDtypeStruct(gains.shape, F32)]
        + [jax.ShapeDtypeStruct((r // 8, n), F32) for _, r, n in shapes],
        in_specs=[anywhere] * 2 + [vmem] * (1 + nw),
        out_specs=[anywhere] * 2 + [vmem] * (1 + nw),
        scratch_shapes=[pltpu.VMEM((2, 2, r // 8, n), BF16) for _, r, n in shapes]
        + [pltpu.VMEM((2, 2, r // 4, n), BF16) for _, r, n in shapes]
        + [pltpu.VMEM((2, r // 4, n), BF16) for _, r, n in shapes]
        + [pltpu.VMEM((2, r // 8, n), F32) for _, r, n in shapes]
        + [pltpu.VMEM((5,) + gains.shape, F32)]
        + [
            dma((2, 2)), dma((2, 2)), dma((2,)), dma((nw, 6)), dma((nw, 6)), dma((nw, 2)), dma((nw, 2)), dma((nw,)),
            dma((nw,)), dma((5,)), dma((5,)),
        ],
        compiler_params=pltpu.CompilerParams(collective_id=1, has_side_effects=True, vmem_limit_bytes=60 * 1024 * 1024),
        name="scatter",
    )(o, i, gains, *grads)
    return out[0], out[1], out[2], out[3:]


def rms_scale(values):
    return lax.rsqrt(jnp.mean(values * values, axis=-1, keepdims=True) + EPS)


def rope_tables(length, width):
    half_width = width // 2
    frequency = THETA ** (-(2.0 * jnp.arange(half_width, dtype=F32)) / width)
    angles = jnp.arange(length, dtype=F32)[:, None] * frequency[None, :]
    return (jnp.cos(angles), jnp.sin(angles))


def rotate(values, cos_table, sin_table):
    half_width = values.shape[-1] // 2
    leading = values[..., :half_width]
    trailing = values[..., half_width:]
    cos_part = cos_table[:, None, :]
    sin_part = sin_table[:, None, :]
    return jnp.concatenate(
        [leading * cos_part - trailing * sin_part, trailing * cos_part + leading * sin_part], axis=-1
    )


def norm_back(grads, unit, scale, gain):
    scaled = grads * gain
    return scale * (scaled - unit * jnp.mean(scaled * unit, axis=-1, keepdims=True))


def allowed_block(segment, alive_row, start_row, count_rows, count_keys):
    query_pos = start_row + lax.iota(jnp.int32, count_rows)
    key_pos = lax.iota(jnp.int32, count_keys)
    same_doc = segment[start_row : start_row + count_rows][:, None] == segment[:count_keys][None, :]
    earlier = key_pos[None, :] < query_pos[:, None]
    itself = key_pos[None, :] == query_pos[:, None]
    return itself | earlier & same_doc & (alive_row[:count_keys][None, :] > 0)


def block_scores(query_block, key_block, allowed, scale):
    raw_scores = jnp.einsum("igrd,jgd->grij", query_block, key_block, preferred_element_type=F32) * scale
    return jnp.where(allowed[None, None], raw_scores, MASKED)


def dot(spec, a, b):
    return jnp.einsum(spec, a, b, preferred_element_type=F32)


def per_device(n_dp, inputs, query_weight, key_weight, value_weight, out_weight, gate_weight, up_weight, down_weight,
               attn_gain, ffn_gain, query_gain, key_gain, cotangent, segment_ids, padding, row_count):
    slots, _, width = inputs.shape
    seq_len = segment_ids.shape[1]
    head_dim = query_gain.shape[0]
    hq, hk = query_weight.shape[1] // head_dim, key_weight.shape[1] // head_dim
    per_group = hq // hk
    nq, nk = hq * head_dim, hk * head_dim
    scale = head_dim ** (-0.5)
    z = lax.axis_index("tensor")
    c = lax.axis_index("dp") % 2
    groups = n_dp // 8
    mate = [(i, i ^ 1) for i in range(n_dp)]

    def swap(v):
        return lax.ppermute(v, "dp", mate)

    def both(own):
        other = swap(own)
        return jnp.where(c == 0, jnp.concatenate([own, other], 0), jnp.concatenate([other, own], 0))

    half = seq_len // 2

    def own_sum(partial):
        partial = partial.astype(BF16)
        keep = lax.dynamic_slice_in_dim(partial, c * half, half)
        give = lax.dynamic_slice_in_dim(partial, (1 - c) * half, half)
        return keep.astype(F32) + swap(give).astype(F32)

    alive_all = padding * (jnp.arange(slots)[:, None] < row_count[0]).astype(jnp.int32)
    code = (segment_ids + ALIVE * alive_all)[z % 2]
    code = jnp.where(c == z // 2, code, swap(code))
    segment, alive_row = code % ALIVE, code // ALIVE

    qkv_shard = jnp.concatenate([query_weight, key_weight, value_weight], axis=1)
    x, ct, (wqkv, wo, wg, wu, wd) = gather(
        inputs, cotangent, [qkv_shard, out_weight, gate_weight, up_weight, down_weight]
    )
    cos_table, sin_table = rope_tables(seq_len, head_dim)
    rows_in = x.astype(F32)
    scale_one = rms_scale(rows_in)
    unit_one = rows_in * scale_one
    normed = both((unit_one * attn_gain).astype(BF16))
    proj = dot("sd,pde->spe", normed, wqkv)
    query_proj = proj[:, :, :nq].reshape(seq_len, 2 * hq, head_dim)
    key_proj = proj[:, :, nq : nq + nk].reshape(seq_len, 2 * hk, head_dim)
    values = proj[:, :, nq + nk :].astype(BF16).reshape(seq_len, 2 * hk, head_dim)
    query_scale = rms_scale(query_proj)
    query_unit = query_proj * query_scale
    queries = (
        rotate(query_unit * query_gain, cos_table, sin_table).astype(BF16).reshape(seq_len, 2 * hk, per_group, head_dim)
    )
    key_scale = rms_scale(key_proj)
    key_unit = key_proj * key_scale
    keys_all = rotate(key_unit * key_gain, cos_table, sin_table).astype(BF16)
    block = min(row_block, seq_len)
    blocks = seq_len // block
    attended_parts, log_totals = [], []
    for b in range(blocks):
        start_row, count_keys = b * block, b * block + block
        allowed = allowed_block(segment, alive_row, start_row, block, count_keys)
        scores = block_scores(queries[start_row : start_row + block], keys_all[:count_keys], allowed, scale)
        row_peak = jnp.max(scores, axis=-1, keepdims=True)
        exponent = jnp.exp(scores - row_peak)
        row_total = jnp.sum(exponent, axis=-1, keepdims=True)
        weights_soft = (exponent / row_total).astype(BF16)
        attended_parts.append(dot("grij,jgd->igrd", weights_soft, values[:count_keys]))
        log_totals.append(row_peak + jnp.log(row_total))
    attended = jnp.concatenate(attended_parts, axis=0).reshape(seq_len, 2, nq).astype(BF16)
    hidden = rows_in + own_sum(dot("spe,ped->sd", attended, wo))
    scale_two = rms_scale(hidden)
    unit_two = hidden * scale_two
    normed_two = both((unit_two * ffn_gain).astype(BF16))
    gate_value = dot("sd,pdf->spf", normed_two, wg)
    upward = dot("sd,pdf->spf", normed_two, wu)
    active = (jax.nn.silu(gate_value) * upward).astype(BF16)
    outputs = (hidden + own_sum(dot("spf,pfd->sd", active, wd))).astype(BF16)
    alive_own = lax.dynamic_slice_in_dim(alive_row, c * half, half).astype(F32)
    out_cot = ct.astype(F32) * alive_own[:, None]
    down_in = both(out_cot.astype(BF16))
    active_grad = dot("sd,pfd->spf", down_in, wd)
    sigma = jax.nn.sigmoid(gate_value)
    gate_rows = (active_grad * upward * sigma * (1.0 + gate_value * (1.0 - sigma))).astype(BF16)
    up_rows = (active_grad * gate_value * sigma).astype(BF16)
    grad_down = dot("spf,sd->pfd", active, down_in).astype(BF16)
    grad_gate = dot("sd,spf->pdf", normed_two, gate_rows).astype(BF16)
    grad_up = dot("sd,spf->pdf", normed_two, up_rows).astype(BF16)
    normed_two_grad = own_sum(dot("spf,pdf->sd", gate_rows, wg) + dot("spf,pdf->sd", up_rows, wu))
    grad_ffn_gain = jnp.sum(normed_two_grad * unit_two, axis=0)
    hidden_grad = out_cot + norm_back(normed_two_grad, unit_two, scale_two, ffn_gain)
    attn_in = both(hidden_grad.astype(BF16))
    grad_out = dot("spe,sd->ped", attended, attn_in).astype(BF16)
    attended_grad = dot("sd,ped->spe", attn_in, wo).astype(BF16).reshape(seq_len, 2 * hk, per_group, head_dim)
    value_acc = jnp.zeros((seq_len, 2 * hk, head_dim), F32)
    key_acc = jnp.zeros((seq_len, 2 * hk, head_dim), F32)
    query_parts = []
    for b in range(blocks):
        start_row, count_keys = b * block, b * block + block
        allowed = allowed_block(segment, alive_row, start_row, block, count_keys)
        query_block = queries[start_row : start_row + block]
        scores = block_scores(query_block, keys_all[:count_keys], allowed, scale)
        soft_rows = jnp.exp(scores - log_totals[b])
        soft_low = soft_rows.astype(BF16)
        grad_block = attended_grad[start_row : start_row + block]
        value_acc = value_acc.at[:count_keys].add(dot("grij,igrd->jgd", soft_low, grad_block))
        prob_grad = dot("igrd,jgd->grij", grad_block, values[:count_keys])
        row_inner = jnp.sum(prob_grad * soft_rows, axis=-1, keepdims=True)
        score_grad = (soft_rows * (prob_grad - row_inner)).astype(BF16)
        query_parts.append(dot("grij,jgd->igrd", score_grad, keys_all[:count_keys]) * scale)
        key_acc = key_acc.at[:count_keys].add(dot("grij,igrd->jgd", score_grad, query_block) * scale)
    value_rows = value_acc.astype(BF16).reshape(seq_len, 2, nk)
    query_rot = jnp.concatenate(query_parts, axis=0).astype(BF16).astype(F32).reshape(seq_len, 2 * hq, head_dim)
    key_rot = key_acc.astype(BF16).astype(F32)
    query_norm_grad = rotate(query_rot, cos_table, -sin_table)
    key_norm_grad = rotate(key_rot, cos_table, -sin_table)
    grad_query_gain = jnp.sum(query_norm_grad * query_unit, axis=(0, 1))
    grad_key_gain = jnp.sum(key_norm_grad * key_unit, axis=(0, 1))
    query_rows = norm_back(query_norm_grad, query_unit, query_scale, query_gain).astype(BF16).reshape(seq_len, 2, nq)
    key_rows = norm_back(key_norm_grad, key_unit, key_scale, key_gain).astype(BF16).reshape(seq_len, 2, nk)
    qkv_rows = jnp.concatenate([query_rows, key_rows, value_rows], axis=-1)
    grad_qkv = dot("sd,spe->pde", normed, qkv_rows).astype(BF16)
    normed_grad = own_sum(dot("spe,pde->sd", qkv_rows, wqkv))
    grad_attn_gain = jnp.sum(normed_grad * unit_one, axis=0)
    input_grad = hidden_grad + norm_back(normed_grad, unit_one, scale_one, attn_gain)

    gains = jnp.concatenate([grad_attn_gain, grad_ffn_gain, grad_query_gain, grad_key_gain])
    n_gain = gains.shape[0]
    gains = jnp.pad(gains, (0, -n_gain % 1024)).reshape(-1, 128)

    def spread(g):
        if groups == 1:
            return g
        p, r, n = g.shape
        rr = r // n_dp
        return g.reshape(p, groups, 4, 2, rr, n).transpose(0, 2, 3, 1, 4, 5).reshape(p, r, n)

    outs, in_grad, gains, sums = scatter(
        outputs, input_grad.astype(BF16), gains, [spread(g) for g in (grad_down, grad_gate, grad_up, grad_out, grad_qkv)]
    )
    if groups > 1:
        same = [[g * 8 + k for g in range(groups)] for k in range(8)]
        sums = [lax.psum_scatter(s, "dp", scatter_dimension=0, axis_index_groups=same, tiled=True) for s in sums]
        gains = lax.psum(gains, "dp", axis_index_groups=same)
    down_sum, gate_sum, up_sum, out_sum, qkv_sum = sums
    gains = gains.reshape(-1)
    return (
        outs,
        in_grad.astype(F32),
        qkv_sum[:, :nq],
        qkv_sum[:, nq : nq + nk],
        qkv_sum[:, nq + nk :],
        out_sum,
        gate_sum,
        up_sum,
        down_sum,
        gains[:width],
        gains[width : 2 * width],
        gains[2 * width : 2 * width + head_dim],
        gains[2 * width + head_dim : 2 * width + 2 * head_dim],
    )


def solution(mesh):
    return jax.shard_map(
        functools.partial(per_device, mesh.shape["dp"]),
        mesh=mesh,
        in_specs=(
            P("dp", "tensor", None),
            P(None, "tensor"),
            P(None, "tensor"),
            P(None, "tensor"),
            P("tensor", None),
            P(None, "tensor"),
            P(None, "tensor"),
            P("tensor", None),
            P(),
            P(),
            P(),
            P(),
            P("dp", "tensor", None),
            P("dp", None),
            P("dp", None),
            P("dp"),
        ),
        out_specs=(
            P("dp", "tensor", None),
            P("dp", "tensor", None),
            P("dp", "tensor"),
            P("dp", "tensor"),
            P("dp", "tensor"),
            P(("tensor", "dp"), None),
            P("dp", "tensor"),
            P("dp", "tensor"),
            P(("tensor", "dp"), None),
            P(),
            P(),
            P(),
            P(),
        ),
        check_vma=False,
    )
```

time: 1170 us -> 749 us (0.64); the launches traced: 1150 us -> 746 us
  waiting for transfers between devices: 822 us -> 4.19 us
  Pallas kernels: 0 us -> 384 us
  starting transfers between devices: 2.05 us -> 124 us
  blocking collectives: 42.4 us -> 0 us
  matrix products: 185 us -> 145 us
  between operations: 17.3 us -> 2.91 us
    reduce_scatter x15 -> x0, waiting for transfers between devices: 522 us -> none  [the longest x2 87.9 us: per_device(): lax.psum_scatter(jnp.dot(active, down_weight, preferred_element_type=jnp....]
    pallas_call x0 -> x2, Pallas kernels: none -> 384 us  [the longest x1 206 us: scatter(): pl.pallas_call(functools.partial(scatter_kernel, nw), out_shape=[jax.Shap...]
    all_gather x8 -> x0, waiting for transfers between devices: 298 us -> none  [the longest x2 80.9 us: per_device(): lax.all_gather(hidden_grad.astype(jnp.bfloat16), 'tensor', axis=0, tiled=...]
    ppermute x0 -> x9, starting transfers between devices: none -> 124 us  [swap(): return lax.ppermute(v, 'dp', mate)]
    dot_general x55 -> x25, matrix products: 179 us -> 136 us  [dot(): return jnp.einsum(spec, a, b, preferred_element_type=F32)]
    psum x1 -> x0, blocking collectives: 42.4 us -> none  [per_device(): lax.psum((grad_attn_gain, grad_ffn_gain, grad_query_gain, grad_key_gain),...]
  transfers between devices with their start and end apart: 23 -> 9, of which waited for: 22 -> 2; matrix products, arithmetic and copies ran while one was open for 16% -> 9% of each run, Pallas kernels for 0% -> 0%
where the time goes in v1:
time: 749 us; the launch traced here: 746 us
  Pallas kernels  384 us (51%)
  matrix products  145 us (19%)
  starting transfers between devices  124 us (17%)
  other arithmetic  55.1 us (7%)
  local copies, waits for them, and re-layouts  30.2 us (4%)
    pallas_call x1, Pallas kernels, scatter(): pl.pallas_call(functools.partial(scatter_kernel, nw), out_shape=[jax.Shap...  206 us
    pallas_call x1, Pallas kernels, gather(): pl.pallas_call(functools.partial(gather_kernel, nw), out_shape=[jax.Shape...  177 us
    dot_general x25, matrix products, dot(): return jnp.einsum(spec, a, b, preferred_element_type=F32)  136 us
    ppermute x9, starting transfers between devices, swap(): return lax.ppermute(v, 'dp', mate)  124 us
  transfers between devices with their start and end apart: 9, of which 2 were waited for; matrix products, arithmetic and copies ran while one was open for 9% of the time, Pallas kernels for 0%

profile of v1, /device:TPU:9, one launch (start us, length us, event | category | flops | bytes accessed | tf_op | source)
XLA Modules:
  0.0 745.6 jit_solution(16309192434337276729)
XLA Ops:
  2.9 177.4 %gather.1 = (bf16[512,1024]{1,0:T(8,128)(2,1)}, bf16[512,1024]{1,0:T(8,128)(2,1)}, bf16[2,1024,512]{2,1,0:T(8,128)(2,1)}, bf16[2,256,1024]{2,1,0:T(8,128)(2,1)},...) custom-call(bf16[2,256,1024]{2,1,0:T(8,128)(2,1)} %x_ref.1, ...), custom_call_target="tpu_custom_call" | custom-call | tf_op jit(solution)/shard_map/gather/pallas_call | solution.py:178
  183.5 121.9 %collective-permute-start = (bf16[512,1024]{1,0:T(8,128)(2,1)S(1)}, bf16[512,1024]{1,0:T(8,128)(2,1)S(1)}, u32[]{:S(2)}, u32[]{:S(2)}) collective-permute-start(bf16[512,1024]{1,0:T(8,128)(2,1)S(1)} %fusion.25), channel_id=1, source_target_pairs={{0,4},{4,0},{8,12},{12,8},{16,20},{20,16},{24,28},{28,24},{1,5},{5... | collective-permute-start | bytes 3145736 | tf_op jit(solution)/shard_map/ppermute | solution.py:459
  310.5 4.5 fusion.121
  325.9 7.5 %fusion.122 = (f32[4,2,512]{2,1,0:T(2,128)S(1)}, f32[4,2,512,1024]{2,3,1,0:T(8,128)}) fusion(bf16[512,4,2,64]{0,3,2,1:T(8,128)(2,1)S(1)} %bitcast.272, bf16[1024,4,32]{0,2,1:T(8,128)(2,1)S(1)} %get-tuple-element.134, bf16[1024,4,32]{0,2,1:T(8,128)(2,1)S(1)} %get-tuple-element.133, pred[512,1024]{0,1:T(8,128)(4,1)S(1)} %fusion.41), kind=kOutput, calls=%fused_computation.217 | convolution fusion | flops 550498304 | bytes 18366464 | tf_op jit(solution)/shard_map/igrd,jgd->grij/dot_general | solution.py:436
  333.4 8.0 %fusion.3 = f32[4,2,512]{2,1,0:T(2,128)S(1)} fusion(f32[4,2,512,1024]{2,3,1,0:T(8,128)} %get-tuple-element.155, f32[4,2,512]{2,1,0:T(2,128)S(1)} %get-tuple-element.154), kind=kLoop, calls=%fused_computation.9 | loop fusion | flops 8384512 | bytes 16809984 | tf_op jit(solution)/shard_map/reduce_sum | solution.py:508
  341.4 7.5 %fusion.77 = bf16[512,4,2,64]{0,3,2,1:T(8,128)(2,1)S(1)} fusion(bf16[1024,4,64,1]{0,2,3,1:T(8,128)(2,1)S(1)} %bitcast.270, f32[4,2,512,1024]{2,3,1,0:T(8,128)} %get-tuple-element.155, f32[4,2,512]{2,1,0:T(2,128)S(1)} %fusion.3, f32[4,2,512]{2,1,0:T(2,128)S(1)} %get-tuple-element.154), kind=kOutput, calls=%fused_computation.121 | convolution fusion | flops 549715968 | bytes 17858560 | tf_op jit(solution)/shard_map/grij,jgd->igrd/dot_general | solution.py:441
  359.8 11.4 %fusion.112 = f32[1024,2,1152]{2,0,1:T(8,128)} fusion(bf16[2,1024,1152]{2,1,0:T(8,128)(2,1)} %get-tuple-element.96, bf16[512,1024]{1,0:T(8,128)(2,1)S(1)} %collective-permute-done.3, bf16[512,1024]{1,0:T(8,128)(2,1)S(1)} %multiply_convert_fusion.3, pred[]{:T(512)S(6)} %eq.57), kind=kOutput, calls=%fused_computation.209 | convolution fusion | flops 4841275392 | bytes 16252929 | tf_op jit(solution)/shard_map/sd,pdf->spf/dot_general | solution.py:441
  371.2 8.9 %fusion.114 = f32[1024,2,1152]{2,0,1:T(8,128)} fusion(bf16[2,1024,1152]{2,1,0:T(8,128)(2,1)S(1)} %bitcast.299, bf16[512,1024]{1,0:T(8,128)(2,1)S(1)} %collective-permute-done.3, bf16[512,1024]{1,0:T(8,128)(2,1)S(1)} %multiply_convert_fusion.3, pred[]{:T(512)S(6)} %eq.57), kind=kOutput, calls=%fused_computation.210 | convolution fusion | flops 4841275392 | bytes 16252929 | tf_op jit(solution)/shard_map/sd,pdf->spf/dot_general | solution.py:441
  381.1 18.5 %multiply_convert_fusion = (bf16[1024,2,1152]{2,0,1:T(8,128)(2,1)}, bf16[1024,2,1152]{2,0,1:T(8,128)(2,1)}, bf16[1024,2,1152]{2,0,1:T(8,128)(2,1)}) fusion(f32[1024,2,1152]{2,0,1:T(8,128)} %fusion.114, f32[1024,2,1152]{2,0,1:T(8,128)} %fusion.112, bf16[2,1152,1024]{2,1,0:T(8,128)(2,1)} %get-tuple-element.97, bf16[512,1024]{1,0:T(8,128)(2,1)} %copy-done.72, ...), kind=kOutput, calls=%fused_computation.11 | convolution fusion | flops 4879024128 | bytes 39845888 | tf_op jit(solution)/shard_map/sd,pfd->spf/dot_general | solution.py:441
  399.6 8.5 %fusion.124 = f32[1024,1024,1]{1,0,2:T(8,128)S(1)} fusion(bf16[1024,2,1152]{2,0,1:T(8,128)(2,1)} %get-tuple-element.118, bf16[2,1024,1152]{2,1,0:T(8,128)(2,1)} %get-tuple-element.95), kind=kOutput, calls=%fused_computation.219 | convolution fusion | flops 4831838208 | bytes 13631488 | tf_op jit(solution)/shard_map/spf,pdf->sd/dot_general | solution.py:441
  408.1 7.8 %fusion.18 = bf16[1024,1024]{1,0:T(8,128)(2,1)S(1)} fusion(f32[1024,1024,1]{1,0,2:T(8,128)S(1)} %fusion.124, bf16[1024,2,1152]{2,0,1:T(8,128)(2,1)S(1)} %copy-done.77, bf16[2,1024,1152]{2,1,0:T(8,128)(2,1)} %get-tuple-element.96), kind=kOutput, calls=%fused_computation.37 | convolution fusion | flops 4833935360 | bytes 15728640 | tf_op jit(solution)/shard_map/spf,pdf->sd/dot_general | solution.py:441
  417.6 5.2 bitcast_convert_fusion.1
  428.1 4.4 fusion.116
  433.0 7.7 %fusion.15.refs_2_ = bf16[2,1024,1152]{2,1,0:T(8,128)(2,1)} fusion(bf16[1024,2,1152]{2,0,1:T(8,128)(2,1)S(1)} %bitcast.307, bf16[512,1024]{1,0:T(8,128)(2,1)S(1)} %copy-done.76, bf16[512,1024]{1,0:T(8,128)(2,1)S(1)} %copy-done.39, pred[]{:T(512)S(6)} %eq.57), kind=kOutput, calls=%fused_computation.33 | convolution fusion | flops 4843634688 | bytes 11534337 | tf_op jit(solution)/shard_map/sd,spf->pdf/dot_general | solution.py:441
  440.7 7.3 fusion.14.refs_1_
  459.5 7.8 %fusion = (f32[4,2,512]{2,1,0:T(2,128)S(1)}, f32[4,1024,512,2]{2,1,3,0:T(8,128)}) fusion(f32[4,2,512,1024]{2,3,1,0:T(8,128)S(1)} %bitcast.249, f32[4,2,512]{2,1,0:T(2,128)S(1)} %bitcast.282, bf16[1024,4,64,1]{0,2,3,1:T(8,128)(2,1)S(1)} %bitcast.271, bf16[512,4,2,64]{0,3,2,1:T(8,128)(2,1)S(1)} %bitcast.263), kind=kOutput, calls=%fused_computation.2 | convolution fusion | flops 549449728 | bytes 34635776 | tf_op jit(solution)/shard_map/igrd,jgd->grij/dot_general | solution.py:441
  467.3 8.3 %fusion.2 = bf16[4,2,512,1024]{2,3,1,0:T(8,128)(2,1)S(1)} fusion(f32[4,1024,512,2]{2,1,3,0:T(8,128)} %get-tuple-element.159, f32[4,2,512,1024]{2,3,1,0:T(8,128)S(1)} %bitcast.249, f32[4,2,512]{2,1,0:T(2,128)S(1)} %get-tuple-element.158, f32[4,2,512]{2,1,0:T(2,128)S(1)} %bitcast.283), kind=kLoop, calls=%fused_computation.4 | loop fusion | flops 16777216 | bytes 41975808 | tf_op jit(solution)/shard_map/convert_element_type | solution.py:551
  480.1 5.0 fusion.67
  488.3 4.5 fusion.63
  498.3 3.8 bitcast_convert_fusion
  504.5 7.2 convolution_convert_fusion.2.refs_0_
  511.9 4.0 convolution_convert_fusion.3.refs_3_
  515.9 3.9 convert_bitcast_fusion.refs_4_
  526.3 206.2 %scatter.1 = (bf16[2,256,1024]{2,1,0:T(8,128)(2,1)}, bf16[2,256,1024]{2,1,0:T(8,128)(2,1)}, f32[24,128]{1,0:T(8,128)}, f32[144,1024]{1,0:T(8,128)}, f32[128,1152...) custom-call(bf16[512,1024]{1,0:T(8,128)(2,1)} %get-tuple-element.130.o_ref, ...), custom_call_target="tpu_custom_call" | custom-call | tf_op jit(solution)/shard_map/scatter/pallas_call | solution.py:377
  (308 shorter events, 85.5 us)
Async XLA Ops:
  2.9 179.0 %copy-start.56 = (f32[1024]{0:T(1024)S(1)}, f32[1024]{0:T(1024)}, u32[]{:S(2)}) copy-start(f32[1024]{0:T(1024)} %param.36) | copy-start | bytes 12292
  2.9 303.7 %copy-start.62 = (s32[2,1024]{1,0:T(2,128)S(1)}, s32[2,1024]{1,0:T(2,128)}, u32[]{:S(2)}) copy-start(s32[2,1024]{1,0:T(2,128)} %param.41) | copy-start | bytes 24580
  2.9 303.7 %copy-start.63 = (s32[2,1024]{1,0:T(2,128)S(1)}, s32[2,1024]{1,0:T(2,128)}, u32[]{:S(2)}) copy-start(s32[2,1024]{1,0:T(2,128)} %param.42) | copy-start | bytes 24580
  181.9 125.5 %copy-start.58 = (f32[512]{0:T(512)}, f32[512]{0:T(512)S(1)}, u32[]{:S(2)}) copy-start(f32[512]{0:T(512)S(1)} %add_rsqrt_fusion.3) | copy-start | bytes 6148
  183.4 131.5 %copy-start.32 = (bf16[512,1024]{1,0:T(8,128)(2,1)}, bf16[512,1024]{1,0:T(8,128)(2,1)S(1)}, u32[]{:S(2)}) copy-start(bf16[512,1024]{1,0:T(8,128)(2,1)S(1)} %fusion.25) | copy-start | bytes 3145732
  183.5 127.0 %collective-permute-start = (bf16[512,1024]{1,0:T(8,128)(2,1)S(1)}, bf16[512,1024]{1,0:T(8,128)(2,1)S(1)}, u32[]{:S(2)}, u32[]{:S(2)}) collective-permute-start(bf16[512,1024]{1,0:T(8,128)(2,1)S(1)} %fusion.25), channel_id=1, source_target_pairs={{0,4},{4,0},{8,12},{12,8},{16,20},{20,16},{24,28},{28,24},{1,5},{5... | collective-permute-start | bytes 3145736 | tf_op jit(solution)/shard_map/ppermute | solution.py:459
  307.3 1.4 collective-permute-start.1
  315.4 26.0 %copy-start.23 = (bf16[1024,2,128]{0,2,1:T(8,128)(2,1)}, bf16[1024,2,128]{0,2,1:T(8,128)(2,1)S(1)}, u32[]{:S(2)}) copy-start(bf16[1024,2,128]{0,2,1:T(8,128)(2,1)S(1)} %slice.239) | copy-start | bytes 1572868
  351.8 2.9 collective-permute-start.2
  356.8 14.4 %slice-start.8 = ((s8[4718592]{0:T(1024)(128)(4,1)}), s8[4194304]{0:T(1024)(128)(4,1)S(1)}, s32[]{:S(2)}) async-start(s8[4718592]{0:T(1024)(128)(4,1)} %bitcast.298), calls=%async_computation.8 | async-start | bytes 8388608
  357.1 14.1 %copy-start.38 = (bf16[512,1024]{1,0:T(8,128)(2,1)}, bf16[512,1024]{1,0:T(8,128)(2,1)S(1)}, u32[]{:S(2)}) copy-start(bf16[512,1024]{1,0:T(8,128)(2,1)S(1)} %multiply_convert_fusion.3) | copy-start | bytes 3145732
  357.1 2.7 collective-permute-start.3
  357.8 23.2 %copy-start.34 = (bf16[512,1024]{1,0:T(8,128)(2,1)}, bf16[512,1024]{1,0:T(8,128)(2,1)S(1)}, u32[]{:S(2)}) copy-start(bf16[512,1024]{1,0:T(8,128)(2,1)S(1)} %fusion.40) | copy-start | bytes 3145732
  357.9 22.2 %collective-permute-start.5 = (bf16[512,1024]{1,0:T(8,128)(2,1)S(1)}, bf16[512,1024]{1,0:T(8,128)(2,1)S(1)}, u32[]{:S(2)}, u32[]{:S(2)}) collective-permute-start(bf16[512,1024]{1,0:T(8,128)(2,1)S(1)} %fusion.40), channel_id=1, source_target_pairs={{0,4},{4,0},{8,12},{12,8},{16,20},{20,16},{24,28},{28,24},{1,5},{5... | collective-permute-start | bytes 3145736 | tf_op jit(solution)/shard_map/ppermute | solution.py:459
  359.8 11.4 %slice-start.9 = ((s8[4718592]{0:T(1024)(128)(4,1)}), s8[524288]{0:T(1024)(128)(4,1)S(1)}, s32[]{:S(2)}) async-start(s8[4718592]{0:T(1024)(128)(4,1)} %bitcast.298), calls=%async_computation.9 | async-start | bytes 1048576
  399.6 17.9 %slice-start.6 = ((s8[4718592]{0:T(1024)(128)(4,1)}), s8[4194304]{0:T(1024)(128)(4,1)S(1)}, s32[]{:S(2)}) async-start(s8[4718592]{0:T(1024)(128)(4,1)} %bitcast.296), calls=%async_computation.6 | async-start | bytes 8388608
  399.6 17.9 %slice-start.10 = ((s8[4718592]{0:T(1024)(128)(4,1)}), s8[4194304]{0:T(1024)(128)(4,1)S(1)}, s32[]{:S(2)}) async-start(s8[4718592]{0:T(1024)(128)(4,1)} %bitcast.300), calls=%async_computation.10 | async-start | bytes 8388608
  417.2 8.7 %collective-permute-start.6 = (bf16[512,1024]{1,0:T(8,128)(2,1)}, bf16[512,1024]{1,0:T(8,128)(2,1)S(1)}, u32[]{:S(2)}, u32[]{:S(2)}) collective-permute-start(bf16[512,1024]{1,0:T(8,128)(2,1)} %constant_dynamic-slice_fusion.1), channel_id=1, source_target_pairs={{0,4},{4,0},{8,12},{12,8},{16,20},{20,16},{24,28},{28,24},{1,5},{5... | collective-permute-start | bytes 3145736 | tf_op jit(solution)/shard_map/ppermute | solution.py:459
  424.5 3.6 collective-permute-start.4
  432.5 15.5 %copy-start.41 = (bf16[512,1024]{1,0:T(8,128)(2,1)}, bf16[512,1024]{1,0:T(8,128)(2,1)S(1)}, u32[]{:S(2)}) copy-start(bf16[512,1024]{1,0:T(8,128)(2,1)S(1)} %get-tuple-element.111) | copy-start | bytes 3145732
  432.5 15.5 %collective-permute-start.7 = (bf16[512,1024]{1,0:T(8,128)(2,1)S(1)}, bf16[512,1024]{1,0:T(8,128)(2,1)S(1)}, u32[]{:S(2)}, u32[]{:S(2)}) collective-permute-start(bf16[512,1024]{1,0:T(8,128)(2,1)S(1)} %get-tuple-element.111), channel_id=1, source_target_pairs={{0,4},{4,0},{8,12},{12,8},{16,20},{20,16},{24,28},{28,24},{1,5},{5... | collective-permute-start | bytes 3145736 | tf_op jit(solution)/shard_map/ppermute | solution.py:459
  433.0 16.5 %slice-start.4 = ((s8[8388608]{0:T(1024)(128)(4,1)}), s8[4194304]{0:T(1024)(128)(4,1)S(1)}, s32[]{:S(2)}) async-start(s8[8388608]{0:T(1024)(128)(4,1)} %bitcast.250), calls=%async_computation.4 | async-start | bytes 8388608
  504.3 15.5 %collective-permute-start.8 = (bf16[512,1024]{1,0:T(8,128)(2,1)}, bf16[512,1024]{1,0:T(8,128)(2,1)}, u32[]{:S(2)}, u32[]{:S(2)}) collective-permute-start(bf16[512,1024]{1,0:T(8,128)(2,1)} %constant_dynamic-slice_fusion), channel_id=1, source_target_pairs={{0,4},{4,0},{8,12},{12,8},{16,20},{20,16},{24,28},{28,24},{1,5},{5... | collective-permute-start | bytes 3145736 | tf_op jit(solution)/shard_map/ppermute | solution.py:459
  732.6 11.9 %copy-start.45 = (f32[144,1024]{1,0:T(8,128)S(1)}, f32[144,1024]{1,0:T(8,128)}, u32[]{:S(2)}) copy-start(f32[144,1024]{1,0:T(8,128)} %get-tuple-element.183) | copy-start | bytes 1769476
  (81 other events, 384.6 us)

commit v2 on v1

v2 whole, which is shorter than its diff:
```python
import functools

import jax
import jax.numpy as jnp
import numpy as np
from jax import lax
from jax.experimental import pallas as pl
from jax.experimental.pallas import tpu as pltpu
from jax.sharding import PartitionSpec as P

EPS = 1e-05
THETA = 1000000.0
ALIVE = 4096
MESH = pl.DeviceIdType.MESH
BF16 = jnp.bfloat16
F32 = jnp.float32


class Place:
    def __init__(self):
        self.dp = lax.axis_index("dp")
        self.z = lax.axis_index("tensor")
        self.c = lax.rem(self.dp, 2)
        self.j = lax.rem(self.dp // 2, 4)
        self.half = self.z // 2
        self.par = lax.rem(self.z, 2)
        self.near = self.half == self.c

    def plane(self, k):
        j = self.j
        bit = lax.rem(j // k, 2)
        return (self.dp + (1 - 2 * bit) * 2 * k, self.z)

    def column(self, c, z):
        return (self.dp - self.c + c, z)

    def quarter(self, k):
        j = self.j
        low, high = lax.rem(j, 2), j // 2
        if k & 1:
            low = 1 - low
        if k & 2:
            high = 1 - high
        return 2 * high + low


def greet(place):
    barrier = pltpu.get_barrier_semaphore()
    for k in (1, 2):
        pl.semaphore_signal(barrier, inc=1, device_id=place.plane(k), device_id_type=MESH)
    for dc in range(2):
        for dz in range(4):
            if dc or dz:
                c = lax.rem(place.c + dc, 2)
                z = lax.rem(place.z + dz, 4)
                pl.semaphore_signal(barrier, inc=1, device_id=place.column(c, z), device_id_type=MESH)
    pl.semaphore_wait(barrier, 9)


def remote(src, dst, send, recv, device):
    return pltpu.make_async_remote_copy(
        src_ref=src, dst_ref=dst, send_sem=send, recv_sem=recv, device_id=device, device_id_type=MESH
    )


def lane_swap(v):
    lane = lax.broadcasted_iota(jnp.int32, v.shape, 1)
    return jnp.where(lane % 64 < 32, pltpu.roll(v, 96, 1), pltpu.roll(v, 32, 1))


def head_mean(v, ones_ref, n):
    high = v.astype(BF16)
    low = (v - high.astype(F32)).astype(BF16)
    ones = ones_ref[:n, :n]
    return jnp.dot(high, ones, preferred_element_type=F32) + jnp.dot(low, ones, preferred_element_type=F32)


def mm(a, b):
    return jnp.dot(a, b, preferred_element_type=F32)


def mm_nt(a, b):
    return lax.dot_general(a, b, (((1,), (1,)), ((), ())), preferred_element_type=F32)


def mm_tn(a, b):
    return lax.dot_general(a, b, (((0,), (0,)), ((), ())), preferred_element_type=F32)


BLK = 256


def rows_at(start, size):
    return pl.ds(pl.multiple_of(start, size), size)


def first_kernel(x_ref, ct_ref, wqkv_ref, wo_ref, wg_ref, wu_ref, wd_ref, qcode_ref, kcode_ref, alive_ref, gain1_ref,
                 gain2_ref, gainqk_ref, cos_ref, sin_ref, ones_ref,
                 gg, gu, gd, o_wqkv, o_wo, o_x, o_din, o_normed, o_n2, o_hidden, o_qk, o_q, o_k, o_v, o_att, o_linv,
                 wqkv, wo, xbuf, cbuf, normed, n2, din, hidden, qk, qs, k2, v2, mask, att, linv, give, take,
                 tok_s, tok_r, tok_l, own_l, zs, zr, fs, fr, ms, mr, outs):
    shards = (wqkv_ref, wo_ref, wg_ref, wu_ref, wd_ref)
    full = (wqkv, wo, gg, gu, gd)
    nw = 5
    place = Place()
    z, c, par, near, j = place.z, place.c, place.par, place.near, place.j
    inner = jnp.where(c == 0, z == 2, z == 1)
    outer = jnp.where(c == 0, z == 3, z == 0)
    seg = x_ref.shape[1]
    half = 2 * seg
    seq = 2 * half
    mate = place.column(1 - c, z)
    greet(place)

    def token_copies(a, src, dst, go):
        for b in range(2):
            slot = par if b == 0 else 1 - par
            target = place.column(place.half, 2 * c + slot)
            here = dst.at[rows_at(par * seg, seg)]

            def far_copy():
                cp = remote(src.at[slot], here, tok_s.at[a, b], tok_r.at[a, par], target)
                cp.start() if go else cp.wait_send()

            if b == 0:
                @pl.when(near)
                def _():
                    cp = pltpu.make_async_copy(src.at[slot], here, tok_l.at[a])
                    cp.start() if go else cp.wait()

                pl.when(jnp.logical_not(near))(far_copy)
            else:
                far_copy()

    def token_arrivals(a, src, dst):
        @pl.when(near)
        def _():
            pltpu.make_async_copy(src.at[par], dst.at[rows_at(par * seg, seg)], tok_l.at[a]).wait()

        for h in range(2):
            @pl.when(jnp.logical_not(near & (par == h)))
            def _():
                remote(src.at[0], dst.at[pl.ds(h * seg, seg)], tok_s.at[a, 0], tok_r.at[a, h], place.plane(1)).wait_recv()

    def token_sent(a, src, dst):
        for b in range(2):
            slot = par if b == 0 else 1 - par

            def wait():
                remote(src.at[slot], dst.at[pl.ds(0, seg)], tok_s.at[a, b], tok_r.at[a, 0], place.plane(1)).wait_send()

            if b == 0:
                pl.when(jnp.logical_not(near))(wait)
            else:
                wait()

    def part(w, p, k, side=None):
        q = shards[w].shape[0] // 4
        start, size = pl.multiple_of(place.quarter(k) * q, q), q
        if side is not None:
            size = q // 2
            start = pl.multiple_of(start + side * size, size)
        return full[w].at[p, pl.ds(start, size)]

    def z_copies(w, go):
        q = shards[w].shape[0] // 4

        @pl.when(near)
        def _():
            for i, to in enumerate((2 * place.half + 1 - par, 2 - c)):
                cp = remote(shards[w].at[rows_at(j * q, q)], part(w, par, 0), zs.at[w, i], zr.at[w, par], place.column(c, to))
                cp.start() if go else cp.wait_send()

    def z_onward(w, p):
        return remote(part(w, p, 0), part(w, p, 0), zs.at[w, p], zr.at[w, p], place.column(c, 3 - 3 * c))

    def missing(p, body):
        pl.when(jnp.logical_or(jnp.logical_not(near), par != p))(body)

    def step_copy(w, p, i):
        k, side, to = ((0, None, 1), (0, None, 2), (1, 0, 2), (2, 1, 1))[i]
        return remote(part(w, p, k, side), part(w, p, k, side), fs.at[w, p, i], fr.at[w, p, i], place.plane(to))

    def first(w):
        for p in range(2):
            @functools.partial(missing, p)
            def _():
                z_onward(w, p).wait_recv()
                pl.when(inner)(lambda: z_onward(w, p).start())
                step_copy(w, p, 0).start()
                step_copy(w, p, 1).start()

    def second(w):
        for p in range(2):
            @functools.partial(missing, p)
            def _():
                step_copy(w, p, 0).wait_recv()
                step_copy(w, p, 2).start()
                step_copy(w, p, 1).wait_recv()
                step_copy(w, p, 3).start()

    def third(w):
        for p in range(2):
            @functools.partial(missing, p)
            def _():
                step_copy(w, p, 2).wait_recv()
                step_copy(w, p, 3).wait_recv()

    def sent(w):
        z_copies(w, False)
        for p in range(2):
            @functools.partial(missing, p)
            def _():
                pl.when(inner)(lambda: z_onward(w, p).wait_send())
                for i in range(4):
                    step_copy(w, p, i).wait_send()

    def own_load(w):
        return pltpu.make_async_copy(shards[w], full[w].at[par], own_l.at[w])

    def save(n, src, dst):
        cp = pltpu.make_async_copy(src, dst, outs.at[n])
        saves.append(cp)
        cp.start()

    saves = []

    token_copies(0, x_ref, xbuf, True)
    for w in range(nw):
        z_copies(w, True)
        if w < 2:
            pl.when(near)(lambda: own_load(w).start())
    token_copies(1, ct_ref, cbuf, True)

    for i in range(seq // BLK):
        for jb in range(i + 1):
            same = qcode_ref[i * BLK : (i + 1) * BLK, :] == kcode_ref[:, jb * BLK : (jb + 1) * BLK]
            if i == jb:
                ri = lax.broadcasted_iota(jnp.int32, (BLK, BLK), 0)
                ci = lax.broadcasted_iota(jnp.int32, (BLK, BLK), 1)
                same = jnp.logical_or(ri == ci, jnp.logical_and(ci < ri, same))
            mask[i * BLK : (i + 1) * BLK, jb * BLK : (jb + 1) * BLK] = jnp.where(same, 1.0, 0.0).astype(F32)
    v2[:, :, 128:] = jnp.ones((v2.shape[0], v2.shape[1], 128), BF16)

    token_arrivals(0, x_ref, xbuf)
    step = 128

    @pl.loop(0, half // step)
    def _(r):
        xs = xbuf[rows_at(r * step, step), :].astype(F32)
        sc = lax.rsqrt(jnp.mean(xs * xs, axis=-1, keepdims=True) + EPS)
        normed[rows_at(c * half + r * step, step), :] = (xs * sc * gain1_ref[...]).astype(BF16)

    def swap_rows(buf, n):
        own = rows_at(c * half, half)
        return remote(buf.at[own], buf.at[own], ms.at[n], mr.at[n], mate)

    def swap_wait(buf, n):
        remote(buf.at[rows_at((1 - c) * half, half)], buf.at[rows_at((1 - c) * half, half)], ms.at[n], mr.at[n], mate).wait_recv()

    swap_rows(normed, 0).start()
    first(0)
    first(1)
    second(0)
    second(1)
    save(0, xbuf, o_x)
    swap_wait(normed, 0)
    save(1, normed, o_normed)
    pl.when(near)(lambda: own_load(0).wait())
    third(0)

    @pl.loop(0, seq // BLK)
    def _(r):
        rows = rows_at(r * BLK, BLK)
        cos, sin = cos_ref[rows, :], sin_ref[rows, :]
        lane = lax.broadcasted_iota(jnp.int32, (BLK, 128), 1)
        left = lane < 64
        for p in range(2):
            proj = mm(normed[rows, :], wqkv[p])
            pq = proj[:, :384]
            qk[p, rows, :] = pq
            sc = lax.rsqrt(head_mean(pq * pq, ones_ref, 384) + EPS)
            n = pq * sc * gainqk_ref[...]
            for s in range(3):
                v = n[:, s * 128 : (s + 1) * 128]
                rot = v * cos + lane_swap(v) * sin
                if s < 2:
                    qr = rot.astype(BF16).astype(F32) * 0.125
                    qs[2 * p + s, 0, rows, :] = jnp.where(left, qr, 0.0).astype(BF16)
                    qs[2 * p + s, 1, rows, :] = jnp.where(left, 0.0, qr).astype(BF16)
                else:
                    kr = pltpu.roll(rot, 64, 1)
                    k2[2 * p, rows, :] = jnp.where(left, rot, kr).astype(BF16)
                    k2[2 * p + 1, rows, :] = jnp.where(left, kr, rot).astype(BF16)
            v = proj[:, 384:]
            vr = pltpu.roll(v, 64, 1)
            v2[2 * p, rows, :128] = jnp.where(left, v, vr).astype(BF16)
            v2[2 * p + 1, rows, :128] = jnp.where(left, vr, v).astype(BF16)

    save(2, wqkv, o_wqkv)
    save(3, qk, o_qk)
    save(4, qs, o_q)
    save(5, k2, o_k)
    save(6, v2.at[:, :, pl.ds(0, 128)], o_v)
    first(2)
    for i in range(seq // BLK):
        n = (i + 1) * BLK
        rows = pl.ds(i * BLK, BLK)

        @pl.loop(0, k2.shape[0])
        def _(g):
            s = mm_nt(qs[g, :, rows, :].reshape(2 * BLK, 128), k2[g, :n, :])
            e = jnp.exp(s).reshape(2, BLK, n) * mask[rows, :n][None]
            acc = mm(e.astype(BF16).reshape(2 * BLK, n), v2[g, :n, :])
            inv = 1.0 / acc[:, 128:]
            o = acc[:, :128] * inv
            left = lax.broadcasted_iota(jnp.int32, (BLK, 128), 1) < 64
            cols = pl.ds(pl.multiple_of(g * 128, 128), 128)
            att[rows, cols] = jnp.where(left, o[:BLK], o[BLK:]).astype(BF16)
            linv[rows, cols] = jnp.where(left, inv[:BLK], inv[BLK:])

        if i == 1:
            second(2)
            first(3)
    save(7, att, o_att)
    save(8, linv, o_linv)
    second(3)
    pl.when(near)(lambda: own_load(1).wait())
    third(1)
    save(9, wo, o_wo)

    def out_rows(start):
        return mm(att[rows_at(start, BLK), :], wo[...].reshape(2 * wo.shape[1], wo.shape[2]))

    @pl.loop(0, half // BLK)
    def _(r):
        give[rows_at(r * BLK, BLK), :] = out_rows((1 - c) * half + r * BLK).astype(BF16)

    swap_give = remote(give, take, ms.at[1], mr.at[1], mate)
    swap_give.start()

    @pl.loop(0, half // BLK)
    def _(r):
        hidden[rows_at(r * BLK, BLK), :] = out_rows(c * half + r * BLK) + xbuf[rows_at(r * BLK, BLK), :].astype(F32)

    first(4)
    swap_give.wait_recv()

    @pl.loop(0, half // step)
    def _(r):
        h = hidden[rows_at(r * step, step), :] + take[rows_at(r * step, step), :].astype(F32)
        hidden[rows_at(r * step, step), :] = h
        sc = lax.rsqrt(jnp.mean(h * h, axis=-1, keepdims=True) + EPS)
        n2[rows_at(c * half + r * step, step), :] = (h * sc * gain2_ref[...]).astype(BF16)

    swap_rows(n2, 2).start()
    save(10, hidden, o_hidden)
    second(4)
    token_arrivals(1, ct_ref, cbuf)

    @pl.loop(0, half // step)
    def _(r):
        v = cbuf[rows_at(r * step, step), :].astype(F32) * alive_ref[rows_at(r * step, step), :]
        din[rows_at(c * half + r * step, step), :] = v.astype(BF16)

    swap_rows(din, 3).start()
    swap_wait(n2, 2)
    save(11, n2, o_n2)
    swap_wait(din, 3)
    save(12, din, o_din)
    for w in range(2, nw):
        third(w)
    for w in range(nw):
        sent(w)
    token_sent(0, x_ref, xbuf)
    token_sent(1, ct_ref, cbuf)
    swap_rows(normed, 0).wait_send()
    swap_give.wait_send()
    swap_rows(n2, 2).wait_send()
    swap_rows(din, 3).wait_send()
    for cp in saves:
        cp.wait()


def first_part(x, ct, shards, qcode, kcode, alive, gain1, gain2, gainqk, cos, sin, ones):
    anywhere = pl.BlockSpec(memory_space=pl.ANY)
    vmem = pl.BlockSpec(memory_space=pltpu.VMEM)
    dma = pltpu.SemaphoreType.DMA
    seg, width = x.shape[1], x.shape[2]
    half, seq = 2 * seg, 4 * seg
    wqkv, wo, wg, wu, wd = shards
    groups = 4
    SDS = jax.ShapeDtypeStruct
    kept = dict(
        wqkv=((2,) + wqkv.shape, BF16), wo=((2,) + wo.shape, BF16), x=((half, width), BF16), din=((seq, width), BF16),
        normed=((seq, width), BF16), n2=((seq, width), BF16), hidden=((half, width), F32), qk=((2, seq, 384), F32),
        q=((groups, 2, seq, 128), BF16), k=((groups, seq, 128), BF16), v=((groups, seq, 128), BF16), att=((seq, 512), BF16),
        linv=((seq, 512), F32),
    )
    order = ("wqkv", "wo", "x", "din", "normed", "n2", "hidden", "qk", "q", "k", "v", "att", "linv")
    out_shape = [SDS((2,) + w.shape, BF16) for w in (wg, wu, wd)] + [SDS(*kept[k]) for k in order]

    def vm(k):
        return pltpu.VMEM(*kept[k])

    nw = 5
    out = pl.pallas_call(
        first_kernel,
        out_shape=out_shape,
        in_specs=[anywhere] * 7 + [vmem] * 9,
        out_specs=[anywhere] * len(out_shape),
        scratch_shapes=[
            vm("wqkv"), vm("wo"), vm("x"), pltpu.VMEM((half, width), BF16), vm("normed"), vm("n2"), vm("din"), vm("hidden"), vm("qk"),
            vm("q"), vm("k"), pltpu.VMEM((groups, seq, 256), BF16), pltpu.VMEM((seq, seq), F32), vm("att"), vm("linv"), pltpu.VMEM((half, width), BF16),
            pltpu.VMEM((half, width), BF16),
            dma((2, 2)), dma((2, 2)), dma((2,)), dma((nw,)), dma((nw, 2)), dma((nw, 2)), dma((nw, 2, 4)), dma((nw, 2, 4)),
            dma((4,)), dma((4,)), dma((13,)),
        ],
        compiler_params=pltpu.CompilerParams(collective_id=0, has_side_effects=True, vmem_limit_bytes=60 * 1024 * 1024),
        name="gather_attention",
    )(x, ct, *shards, qcode, kcode, alive, gain1, gain2, gainqk, cos, sin, ones)
    gathered, rest = out[:3], dict(zip(order, out[3:]))
    return gathered, rest


TILE = 384
PIECES = 3


def second_kernel(gg, gu, gd, wg_ref, wu_ref, wd_ref, wqkv_ref, wo_ref, x_ref, din_ref, normed_ref, n2_ref, hidden_ref, qk_ref,
                  q_ref, k_ref, v_ref, att_ref, linv_ref, qrow_ref, kcol_ref, gain1_ref, gain2_ref, gainqk_ref, cos_ref, sin_ref,
                  ones_ref,
                  oo, io, gain_out, s_gu0, s_gu1, s_gu2, s_d, s_o, s_qkv,
                  p_gu0, p_gu1, p_gu2, p_d, p_o, p_qkv, c_gu0, c_gu1, c_gu2, c_d, c_o, c_qkv,
                  g_a, g_b, g_d, g_o, g_qkv, d_gu0, d_gu1, d_gu2, d_d, d_o, d_qkv, stage, last, give, take, obuf, hgrad,
                  gain_in, attn_in,
                  tok_s, tok_r, tok_l, ps, pr, cs, cr, ls, lr, ll, gs, gr, ms, mr, ld, wl, st_sem):
    grads = (g_a, g_b, g_a, g_d, g_o, g_qkv)
    diag = (d_gu0, d_gu1, d_gu2, d_d, d_o, d_qkv)
    plane_in = (p_gu0, p_gu1, p_gu2, p_d, p_o, p_qkv)
    col_in = (c_gu0, c_gu1, c_gu2, c_d, c_o, c_qkv)
    sums = (s_gu0, s_gu1, s_gu2, s_d, s_o, s_qkv)
    nw = 6
    D_, O_, QKV_ = 3, 4, 5
    place = Place()
    z, c, par, near, j = place.z, place.c, place.par, place.near, place.j
    inner = jnp.where(c == 0, z == 2, z == 1)
    outer = jnp.where(c == 0, z == 3, z == 0)
    half = obuf.shape[0]
    seq = 2 * half
    seg = half // 2
    width = obuf.shape[1]
    mate = place.column(1 - c, z)
    own_at = c * half
    other_at = (1 - c) * half
    step = 128
    greet(place)

    def token_copies(a, src, dst, go):
        for b in range(2):
            h = par if b == 0 else 1 - par
            piece = src.at[rows_at(h * seg, seg)]
            target = place.column(place.half, 2 * c + h)
            there = dst.at[par]

            def far_copy():
                cp = remote(piece, there, tok_s.at[a, b], tok_r.at[a, par], target)
                cp.start() if go else cp.wait_send()

            if b == 0:
                @pl.when(near)
                def _():
                    cp = pltpu.make_async_copy(piece, there, tok_l.at[a])
                    cp.start() if go else cp.wait()

                pl.when(jnp.logical_not(near))(far_copy)
            else:
                far_copy()

    def token_arrivals(a, src, dst):
        for s in range(2):
            @pl.when(jnp.logical_not(near & (par == s)))
            def _():
                remote(src.at[pl.ds(0, seg)], dst.at[s], tok_s.at[a, 0], tok_r.at[a, s], place.plane(1)).wait_recv()

    def rows_of(w, k, side=None):
        q = grads[w].shape[1] // 4
        start, size = pl.multiple_of(place.quarter(k) * q, q), q
        if side is not None:
            size = q // 2
            start = pl.multiple_of(start + side * size, size)
        return pl.ds(start, size)

    def diag_copy(w, side):
        return remote(grads[w].at[:, rows_of(w, 3, side)], diag[w].at[side], ps.at[w, side], pr.at[w, side], place.plane(1 + side))

    def plane_copy(w, i, side):
        src = grads[w].at[:, rows_of(w, 1 + i, side)] if side == i else diag[w].at[side]
        n = 2 + 2 * i + side
        return remote(src, plane_in[w].at[i, side], ps.at[w, n], pr.at[w, n], place.plane(1 + i))

    def begin(w):
        diag_copy(w, 0).start()
        diag_copy(w, 1).start()
        plane_copy(w, 0, 0).start()
        plane_copy(w, 1, 1).start()

    def add_diag(w):
        for side in (0, 1):
            diag_copy(w, side).wait()
            rows = rows_of(w, 2 - side, side)
            for p in range(2):
                diag[w][side, p] = (grads[w][p, rows, :].astype(F32) + diag[w][side, p].astype(F32)).astype(BF16)
            plane_copy(w, 1 - side, side).start()

    def outer_copy(w):
        return remote(diag[w], col_in[w], cs.at[w, 0], cr.at[w, 0], place.column(c, z - 1 + 2 * c))

    def inner_copy(w, p):
        return remote(diag[w].at[:, p], col_in[w].at[:, 1], cs.at[w, p], cr.at[w, 1], place.column(c, 2 * c + p))

    def near_copy(w):
        to = place.column(c, 2 * place.half + 1 - par)
        return remote(diag[w].at[:, 1 - par], col_in[w].at[:, 0], cs.at[w, 0], cr.at[w, 0], to)

    def staged(w, n):
        e = grads[w].shape[1] // 8
        return stage.at[pl.ds(0, n), :, :, pl.ds(0, e), pl.ds(0, grads[w].shape[2])]

    def add_plane(w):
        for i in range(2):
            for side in range(2):
                plane_copy(w, i, side).wait()
        cp = pltpu.make_async_copy(plane_in[w], staged(w, 2), st_sem.at[0])
        cp.start()
        cp.wait()
        e, n = grads[w].shape[1] // 8, grads[w].shape[2]
        for side in range(2):
            rows = rows_of(w, 0, side)
            for p in range(2):
                total = (
                    grads[w][p, rows, :].astype(F32)
                    + stage[0, side, p, :e, :n].astype(F32)
                    + stage[1, side, p, :e, :n].astype(F32)
                )
                diag[w][side, p] = total.astype(BF16)
        pl.when(outer)(lambda: outer_copy(w).start())
        pl.when(near)(lambda: near_copy(w).start())

    def load_column(w):
        cp = pltpu.make_async_copy(col_in[w], staged(w, 1).at[0], st_sem.at[1])
        cp.start()
        cp.wait()

    def add_outer(w):
        @pl.when(inner)
        def _():
            outer_copy(w).wait_recv()
            load_column(w)
            e, n = grads[w].shape[1] // 8, grads[w].shape[2]
            for p in range(2):
                for side in range(2):
                    diag[w][side, p] = (diag[w][side, p].astype(F32) + stage[0, side, p, :e, :n].astype(F32)).astype(BF16)
                inner_copy(w, p).start()

    def last_view(w, k):
        return last.at[w % 2, k, pl.ds(0, grads[w].shape[1] // 8), pl.ds(0, grads[w].shape[2])]

    def last_remote(w):
        return remote(last_view(w, 1), sums[w], ls.at[w], lr.at[w], mate)

    def last_local(w):
        return pltpu.make_async_copy(last_view(w, 0), sums[w], ll.at[w])

    def release_last(w):
        @pl.when(near)
        def _():
            last_remote(w).wait_send()
            last_local(w).wait()

    def add_column(w):
        if w >= 2:
            release_last(w - 2)

        @pl.when(near)
        def _():
            e, n = grads[w].shape[1] // 8, grads[w].shape[2]
            near_copy(w).wait_recv()
            inner_copy(w, 0).wait_recv()
            load_column(w)
            for hc in range(2):
                total = (
                    diag[w][hc, par].astype(F32) + stage[0, hc, 0, :e, :n].astype(F32) + stage[0, hc, 1, :e, :n].astype(F32)
                )

                @pl.when(c == hc)
                def _():
                    last[w % 2, 0, :e, :n] = total

                @pl.when(c != hc)
                def _():
                    last[w % 2, 1, :e, :n] = total

            last_remote(w).start()
            last_local(w).start()

    def finish(w):
        pl.when(near)(lambda: near_copy(w).wait_send())
        pl.when(jnp.logical_not(near))(lambda: last_remote(w).wait_recv())
        pl.when(outer)(lambda: outer_copy(w).wait_send())

        @pl.when(inner)
        def _():
            inner_copy(w, 0).wait_send()
            inner_copy(w, 1).wait_send()

    def trade(n):
        return remote(give.at[n % 2], take.at[n], ms.at[n], mr.at[n], mate)

    def load(n, src, dst):
        return pltpu.make_async_copy(src, dst, ld.at[n])

    def ffn(n2, din, n2t, wg, wu, wd, acc_o, acc_n, act, gr, ur):
        loads = [load(0, n2_ref, n2), load(1, din_ref, din)]
        for cp in loads:
            cp.start()

        def tile_loads(i, go):
            t, p = i // 2, i % 2
            b = i % 2
            cols = pl.ds(t * TILE, TILE)
            mine = near & (par == p)

            def run(g, u, d):
                for k, (src, dst) in enumerate(((g.at[:, cols], wg.at[b]), (u.at[:, cols], wu.at[b]), (d.at[cols], wd.at[b]))):
                    cp = pltpu.make_async_copy(src, dst, wl.at[b, k])
                    cp.start() if go else cp.wait()

            if go:
                pl.when(mine)(lambda: run(wg_ref, wu_ref, wd_ref))
                pl.when(jnp.logical_not(mine))(lambda: run(gg.at[p], gu.at[p], gd.at[p]))
            else:
                run(gg.at[p], gu.at[p], gd.at[p])

        tile_loads(0, True)
        for cp in loads:
            cp.wait()

        @pl.loop(0, seq // BLK)
        def _(r):
            cols = pl.ds(pl.multiple_of(r * BLK, BLK), BLK)
            n2t[:, cols] = n2[cols, :].T

        for i in range(2 * PIECES):
            t, p = i // 2, i % 2
            b = i % 2
            if i + 1 < 2 * PIECES:
                tile_loads(i + 1, True)
            tile_loads(i, False)

            @pl.loop(0, seq // BLK)
            def _(r):
                rows = rows_at(r * BLK, BLK)
                a = n2[rows, :]
                g = mm(a, wg[b])
                u = mm(a, wu[b])
                ag = mm_nt(din[rows, :], wd[b])
                sig = jax.nn.sigmoid(g)
                gs_ = g * sig
                av = (gs_ * u).astype(BF16)
                act[p, rows, t * TILE : (t + 1) * TILE] = av
                gv = (ag * u * sig * (1.0 + g * (1.0 - sig))).astype(BF16)
                uv = (ag * gs_).astype(BF16)
                gr[rows, :] = gv
                ur[rows, :] = uv
                dn = mm_nt(gv, wg[b]) + mm_nt(uv, wu[b])
                do = mm(av, wd[b])
                if i == 0:
                    acc_n[rows, :] = dn
                    acc_o[rows, :] = do
                else:
                    acc_n[rows, :] += dn
                    acc_o[rows, :] += do

            @pl.loop(0, width // BLK)
            def _(r):
                rows = rows_at(r * BLK, BLK)
                grads[t][p, rows, :TILE] = mm(n2t[rows, :], gr[...]).astype(BF16)
                grads[t][p, rows, TILE:] = mm(n2t[rows, :], ur[...]).astype(BF16)

            if p == 1:
                begin(t)
                if t == 1:
                    add_diag(0)
                    add_plane(0)

        @pl.loop(0, half // BLK)
        def _(r):
            rows = rows_at(r * BLK, BLK)
            give[0, rows, :] = acc_n[rows_at(other_at + r * BLK, BLK), :].astype(BF16)
            give[1, rows, :] = acc_o[rows_at(other_at + r * BLK, BLK), :].astype(BF16)

        trade(0).start()
        trade(1).start()
        hid_load = load(2, hidden_ref, hgrad)
        hid_load.start()
        for p in range(2):
            @pl.loop(0, width // BLK)
            def _(r):
                cols = pl.ds(pl.multiple_of(r * BLK, BLK), BLK)
                for k in range(PIECES):
                    rows = pl.ds(k * TILE, TILE)
                    grads[D_][p, rows, cols] = mm_tn(act[p, :, rows], din[:, cols]).astype(BF16)

        begin(D_)
        hid_load.wait()
        trade(0).wait_recv()
        trade(1).wait_recv()
        gain_out[8:16, :] = jnp.zeros((8, 128), F32)

        @pl.loop(0, half // step)
        def _(r):
            rows = rows_at(r * step, step)
            own = rows_at(own_at + r * step, step)
            h = hgrad[rows, :]
            obuf[rows, :] = (h + acc_o[own, :] + take[1, rows, :].astype(F32)).astype(BF16)
            ng = acc_n[own, :] + take[0, rows, :].astype(F32)
            sc = lax.rsqrt(jnp.mean(h * h, axis=-1, keepdims=True) + EPS)
            unit = h * sc
            acc_gain(8, ng * unit)
            e = ng * gain2_ref[...]
            hg = din[own, :].astype(F32) + sc * (e - unit * jnp.mean(e * unit, axis=-1, keepdims=True))
            hgrad[rows, :] = hg
            attn_in[own, :] = hg.astype(BF16)

        token_copies(0, obuf, oo, True)

    def acc_gain(at, v):
        s = jnp.sum(v, axis=0, keepdims=True)
        for k in range(width // 128):
            gain_out[at + k : at + k + 1, :] += s[:, k * 128 : (k + 1) * 128]

    gain_out[...] = jnp.zeros(gain_out.shape, F32)
    pl.run_scoped(
        ffn,
        pltpu.VMEM((seq, width), BF16), pltpu.VMEM((seq, width), BF16), pltpu.VMEM((width, seq), BF16),
        pltpu.VMEM((2, width, TILE), BF16), pltpu.VMEM((2, width, TILE), BF16), pltpu.VMEM((2, TILE, width), BF16),
        pltpu.VMEM((seq, width), F32), pltpu.VMEM((seq, width), F32), pltpu.VMEM((2, seq, PIECES * TILE), BF16),
        pltpu.VMEM((seq, TILE), BF16), pltpu.VMEM((seq, TILE), BF16),
    )

    def attn_swap():
        own = rows_at(own_at, half)
        return remote(attn_in.at[own], attn_in.at[own], ms.at[3], mr.at[3], mate)

    attn_swap().start()

    def attention(dos, dq, dk, dv, drow):
        def front(wo, att, linv):
            loads = [load(3, wo_ref, wo), load(4, att_ref, att), load(5, linv_ref, linv)]
            for cp in loads:
                cp.start()
            add_diag(1)
            for cp in loads:
                cp.wait()
            other = rows_at(other_at, half)
            remote(attn_in.at[other], attn_in.at[other], ms.at[3], mr.at[3], mate).wait_recv()

            @pl.loop(0, seq // BLK)
            def _(r):
                rows = rows_at(r * BLK, BLK)
                left = lax.broadcasted_iota(jnp.int32, (BLK, 128), 1) < 64
                for p in range(2):
                    ag = mm_nt(attn_in[rows, :], wo[p]).astype(BF16).astype(F32)
                    for s in range(2):
                        g = 2 * p + s
                        cols = slice(g * 128, (g + 1) * 128)
                        d = ag[:, s * 128 : (s + 1) * 128] * linv[rows, cols]
                        d0, d1 = jnp.where(left, d, 0.0).astype(BF16), jnp.where(left, 0.0, d).astype(BF16)
                        dos[g, 0, rows, :] = d0
                        dos[g, 1, rows, :] = d1
                        o = att[rows, cols].astype(F32)
                        one = jnp.ones((8, 128), BF16)
                        for k, dd in enumerate((d0, d1)):
                            prod = dd.astype(F32) * o
                            high = prod.astype(BF16)
                            low = (prod - high.astype(F32)).astype(BF16)
                            drow[g, k, :, rows] = mm_nt(one, high) + mm_nt(one, low)

            @pl.loop(0, width // BLK)
            def _(r):
                cols = pl.ds(pl.multiple_of(r * BLK, BLK), BLK)
                for p in range(2):
                    grads[O_][p, :, cols] = mm_tn(att[:, p * 256 : (p + 1) * 256], attn_in[:, cols]).astype(BF16)

            begin(O_)

        pl.run_scoped(
            front, pltpu.VMEM(wo_ref.shape, BF16), pltpu.VMEM(att_ref.shape, BF16), pltpu.VMEM(linv_ref.shape, F32),
        )
        add_plane(1)
        add_diag(2)

        def rest(q, k, v, mt, qk, rows_, wqkv, normed, x):
            loads = [load(6, q_ref, q), load(7, k_ref, k), load(8, v_ref, v)]
            later = [load(9, qk_ref, qk), load(10, wqkv_ref, wqkv), load(11, normed_ref, normed), load(12, x_ref, x)]
            for cp in loads + later:
                cp.start()
            for cp in loads:
                cp.wait()
            dq[...] = jnp.zeros(dq.shape, F32)
            todo = {
                0: [lambda: add_outer(0), lambda: add_plane(2)],
                1: [lambda: add_diag(D_), lambda: add_column(0), lambda: add_outer(1)],
                2: [lambda: add_plane(D_), lambda: add_diag(O_), lambda: add_column(1), lambda: add_outer(2)],
                3: [lambda: add_plane(O_), lambda: add_column(2), lambda: add_outer(D_)],
            }
            for jb in range(seq // BLK):
                at = jb * BLK
                ni = seq - at
                keys = pl.ds(at, BLK)
                cols = pl.ds(at, ni)
                ki = lax.broadcasted_iota(jnp.int32, (BLK, ni), 0)
                qi = lax.broadcasted_iota(jnp.int32, (BLK, ni), 1)
                same = jnp.logical_and(ki < qi, kcol_ref[keys, :] == qrow_ref[:, cols])
                mt[:, :ni] = jnp.where(jnp.logical_or(ki == qi, same), 1.0, 0.0).astype(F32)

                @pl.loop(0, 4)
                def _(g):
                    kb = k[g, keys, :]
                    qb = q[g, :, cols, :].reshape(2 * ni, 128)
                    db = dos[g, :, cols, :].reshape(2 * ni, 128)
                    m = mt[:, :ni]
                    e = jnp.exp(mm_nt(kb, qb)) * jnp.concatenate([m, m], axis=1)
                    dv[g, keys, :] = mm(e.astype(BF16), db)
                    dp = mm_nt(v[g, keys, :], db)
                    dr = jnp.concatenate([drow[g, 0, :1, cols], drow[g, 1, :1, cols]], axis=1)
                    ds = (e * (dp - dr)).astype(BF16)
                    dk[g, keys, :] = mm(ds, qb)
                    dqs = mm_tn(ds, kb)
                    left = lax.broadcasted_iota(jnp.int32, (ni, 128), 1) < 64
                    lanes = pl.ds(pl.multiple_of(g * 128, 128), 128)
                    dq[cols, lanes] += jnp.where(left, dqs[:ni], dqs[ni:])

                for f in todo[jb]:
                    f()
            for cp in later:
                cp.wait()

            @pl.loop(0, seq // BLK)
            def _(r):
                rows = rows_at(r * BLK, BLK)
                cos, sin = cos_ref[rows, :], sin_ref[rows, :]
                left = lax.broadcasted_iota(jnp.int32, (BLK, 128), 1) < 64

                def fold(ref, p):
                    a, b = ref[2 * p, rows, :], ref[2 * p + 1, rows, :]
                    return jnp.where(left, a + pltpu.roll(a, 64, 1), b + pltpu.roll(b, 64, 1))

                for p in range(2):
                    raw = qk[p, rows, :]
                    sc = lax.rsqrt(head_mean(raw * raw, ones_ref, 384) + EPS)
                    unit = raw * sc
                    parts = []
                    for s in range(3):
                        if s < 2:
                            v_ = dq[rows, (2 * p + s) * 128 : (2 * p + s + 1) * 128] * 0.125
                        else:
                            v_ = fold(dk, p)
                        v_ = v_.astype(BF16).astype(F32)
                        parts.append(v_ * cos - lane_swap(v_) * sin)
                    ng = jnp.concatenate(parts, axis=1)
                    gsum = jnp.sum(ng * unit, axis=0, keepdims=True)
                    qsum = gsum[:, :128] + gsum[:, 128:256]
                    ksum = gsum[:, 256:]
                    gain_out[16:17, :] += qsum
                    gain_out[17:18, :] += ksum
                    e = ng * gainqk_ref[...]
                    back = sc * (e - unit * head_mean(e * unit, ones_ref, 384))
                    rows_[p, rows, :384] = back.astype(BF16)
                    rows_[p, rows, 384:] = fold(dv, p).astype(BF16)

            def back_rows(start):
                at = rows_at(start, BLK)
                return mm_nt(rows_[0, at, :], wqkv[0]) + mm_nt(rows_[1, at, :], wqkv[1])

            trade(0).wait_send()

            @pl.loop(0, half // BLK)
            def _(r):
                give[0, rows_at(r * BLK, BLK), :] = back_rows(other_at + r * BLK).astype(BF16)

            trade(2).start()
            for p in range(2):
                @pl.loop(0, width // BLK)
                def _(r):
                    cols = pl.ds(pl.multiple_of(r * BLK, BLK), BLK)
                    grads[QKV_][p, cols, :] = mm_tn(normed[:, cols], rows_[p]).astype(BF16)

            begin(QKV_)
            add_column(D_)
            add_outer(O_)
            trade(2).wait_recv()
            token_copies(0, obuf, oo, False)

            @pl.loop(0, half // BLK)
            def _(r):
                rows = rows_at(r * BLK, BLK)
                ng = back_rows(own_at + r * BLK) + take[2, rows, :].astype(F32)
                xs = x[rows, :].astype(F32)
                sc = lax.rsqrt(jnp.mean(xs * xs, axis=-1, keepdims=True) + EPS)
                unit = xs * sc
                acc_gain(0, ng * unit)
                e = ng * gain1_ref[...]
                ig = hgrad[rows, :] + sc * (e - unit * jnp.mean(e * unit, axis=-1, keepdims=True))
                obuf[rows, :] = ig.astype(BF16)

        V = pltpu.VMEM
        pl.run_scoped(
            rest, V(q_ref.shape, BF16), V(k_ref.shape, BF16), V(v_ref.shape, BF16), V((BLK, seq), F32), V(qk_ref.shape, F32),
            V((2, seq, 512), BF16), V(wqkv_ref.shape, BF16), V(normed_ref.shape, BF16), V(x_ref.shape, BF16),
        )

    pl.run_scoped(
        attention, pltpu.VMEM(q_ref.shape, BF16), pltpu.VMEM((seq, 512), F32), pltpu.VMEM((4, seq, 128), F32),
        pltpu.VMEM((4, seq, 128), F32), pltpu.VMEM((4, 2, 8, seq), F32),
    )
    token_copies(1, obuf, io, True)

    def gain_copy(i):
        to = (mate, place.plane(1), place.plane(2), place.column(c, 2 * place.half + 1 - par),
              place.column(c, 2 - 2 * place.half + par))[i]
        return remote(gain_out, gain_in.at[i], gs.at[i], gr.at[i], to)

    for i in range(5):
        gain_copy(i).start()
        if i == 0:
            add_diag(QKV_)
        if i == 1:
            add_column(O_)
        if i == 2:
            add_plane(QKV_)
        if i == 3:
            add_outer(QKV_)
        gain_copy(i).wait()
        gain_out[...] += gain_in[i]
    add_column(QKV_)
    release_last(nw - 2)
    release_last(nw - 1)
    for w in range(nw):
        finish(w)
    trade(1).wait_send()
    trade(2).wait_send()
    attn_swap().wait_send()
    token_copies(1, obuf, io, False)
    token_arrivals(0, obuf, oo)
    token_arrivals(1, obuf, io)


def second_part(gathered, shards, kept, qrow, kcol, gain1, gain2, gainqk, cos, sin, ones):
    anywhere = pl.BlockSpec(memory_space=pl.ANY)
    vmem = pl.BlockSpec(memory_space=pltpu.VMEM)
    dma = pltpu.SemaphoreType.DMA
    half, width = kept["x"].shape
    SDS = jax.ShapeDtypeStruct
    wg, wu, wd = shards
    r_d = wd.shape[0]
    sizes = [(width, 2 * TILE)] * 3 + [(r_d, width), (kept["wo"].shape[1], width), (width, kept["wqkv"].shape[2])]
    held = [sizes[0], sizes[1]] + sizes[3:]
    nw = 6
    order = ("wqkv", "wo", "x", "din", "normed", "n2", "hidden", "qk", "q", "k", "v", "att", "linv")
    gains = (24, 128)
    out_shape = (
        [SDS((2, half // 2, width), BF16)] * 2
        + [SDS(gains, F32)]
        + [SDS((r // 8, n), F32) for r, n in sizes]
        + [SDS((2, 2, 2, r // 8, n), BF16) for r, n in sizes]
        + [SDS((2, 2, r // 8, n), BF16) for r, n in sizes]
    )
    V = pltpu.VMEM
    e_max, n_max = max(r // 8 for r, _ in sizes), max(n for _, n in sizes)
    out = pl.pallas_call(
        second_kernel,
        out_shape=out_shape,
        in_specs=[anywhere] * (6 + len(order)) + [vmem] * 8,
        out_specs=[anywhere] * 2 + [vmem] + [anywhere] * 18,
        scratch_shapes=[V((2, r, n), BF16) for r, n in held]
        + [V((2, 2, r // 8, n), BF16) for r, n in sizes]
        + [
            V((2, 2, 2, e_max, n_max), BF16), V((2, 2, e_max, n_max), F32), V((2, half, width), BF16), V((3, half, width), BF16),
            V((half, width), BF16), V((half, width), F32), V((5,) + gains, F32), V((2 * half, width), BF16),
        ]
        + [
            dma((2, 2)), dma((2, 2)), dma((2,)), dma((nw, 6)), dma((nw, 6)), dma((nw, 2)), dma((nw, 2)), dma((nw,)), dma((nw,)),
            dma((nw,)), dma((5,)), dma((5,)), dma((4,)), dma((4,)), dma((13,)), dma((2, 3)), dma((2,)),
        ],
        compiler_params=pltpu.CompilerParams(collective_id=1, has_side_effects=True, vmem_limit_bytes=60 * 1024 * 1024),
        name="backward_scatter",
    )(*gathered, *shards, *[kept[k] for k in order], qrow, kcol, gain1, gain2, gainqk, cos, sin, ones)
    return out[0], out[1], out[2], out[3:9]


def rope_tables(length, width):
    k = np.arange(width // 2)
    angles = np.arange(length)[:, None] * (THETA ** (-2.0 * k / width))[None]
    cos, sin = np.cos(angles), np.sin(angles)
    return (
        jnp.asarray(np.concatenate([cos] * 4, axis=1), F32),
        jnp.asarray(np.concatenate([-sin, sin] * 2, axis=1), F32),
    )


def per_device(n_dp, inputs, query_weight, key_weight, value_weight, out_weight, gate_weight, up_weight, down_weight,
               attn_gain, ffn_gain, query_gain, key_gain, cotangent, segment_ids, padding, row_count):
    slots, _, width = inputs.shape
    seq_len = segment_ids.shape[1]
    head_dim = query_gain.shape[0]
    nq, nk = query_weight.shape[1], key_weight.shape[1]
    z = lax.axis_index("tensor")
    c = lax.axis_index("dp") % 2
    groups = n_dp // 8
    half = seq_len // 2

    alive_all = padding * (jnp.arange(slots)[:, None] < row_count[0]).astype(jnp.int32)
    code = (segment_ids + ALIVE * alive_all)[z % 2]
    code = jnp.where(c == z // 2, code, lax.ppermute(code, "dp", [(i, i ^ 1) for i in range(n_dp)]))
    segment, alive_row = code % ALIVE, code // ALIVE
    key_code = jnp.where(alive_row > 0, segment, -1)
    alive_own = lax.dynamic_slice_in_dim(alive_row, c * half, half).astype(F32)

    qkv_shard = jnp.concatenate([query_weight, key_weight, value_weight], axis=1)
    cos, sin = rope_tables(seq_len, head_dim)
    gain_qk = jnp.concatenate([query_gain] * (nq // head_dim) + [key_gain] * (nk // head_dim))[None]
    lanes = np.arange(nq + nk) // head_dim
    ones = jnp.asarray(np.where(lanes[:, None] == lanes[None], 1.0 / head_dim, 0.0), BF16)
    gain1, gain2 = attn_gain[None], ffn_gain[None]
    ffn_shards = (gate_weight, up_weight, down_weight)
    gathered, kept = first_part(
        inputs, cotangent, (qkv_shard, out_weight) + ffn_shards, segment[:, None], key_code[None], alive_own[:, None],
        gain1, gain2, gain_qk, cos, sin, ones,
    )
    outs, in_grad, gains, sums = second_part(
        gathered, ffn_shards, kept, segment[None], key_code[:, None], gain1, gain2, gain_qk, cos, sin, ones
    )
    if groups > 1:
        same = [[g * 8 + k for g in range(groups)] for k in range(8)]
        sums = [lax.psum_scatter(s, "dp", scatter_dimension=0, axis_index_groups=same, tiled=True) for s in sums]
        gains = lax.psum(gains, "dp", axis_index_groups=same)
    down_sum, out_sum, qkv_sum = sums[3:]
    pair = gains[16:18, :head_dim] + gains[16:18, head_dim:]
    return (
        outs,
        in_grad.astype(F32),
        qkv_sum[:, :nq],
        qkv_sum[:, nq : nq + nk],
        qkv_sum[:, nq + nk :],
        out_sum,
        jnp.concatenate([s[:, :TILE] for s in sums[:3]], axis=1),
        jnp.concatenate([s[:, TILE:] for s in sums[:3]], axis=1),
        down_sum,
        gains[:8].reshape(-1),
        gains[8:16].reshape(-1),
        pair[0],
        pair[1],
    )


def solution(mesh):
    return jax.shard_map(
        functools.partial(per_device, mesh.shape["dp"]),
        mesh=mesh,
        in_specs=(
            P("dp", "tensor", None),
            P(None, "tensor"),
            P(None, "tensor"),
            P(None, "tensor"),
            P("tensor", None),
            P(None, "tensor"),
            P(None, "tensor"),
            P("tensor", None),
            P(),
            P(),
            P(),
            P(),
            P("dp", "tensor", None),
            P("dp", None),
            P("dp", None),
            P("dp"),
        ),
        out_specs=(
            P("dp", "tensor", None),
            P("dp", "tensor", None),
            P("dp", "tensor"),
            P("dp", "tensor"),
            P("dp", "tensor"),
            P(("tensor", "dp"), None),
            P("dp", "tensor"),
            P("dp", "tensor"),
            P(("tensor", "dp"), None),
            P(),
            P(),
            P(),
            P(),
        ),
        check_vma=False,
    )
```

time: 749 us -> 485 us (0.65)
  matrix products: 145 us -> 0 us
  starting transfers between devices: 124 us -> 0.74 us
  Pallas kernels: 384 us -> 453 us
  other arithmetic: 55.1 us -> 9.06 us
  local copies, waits for them, and re-layouts: 30.2 us -> 12.7 us
    dot_general x27 -> x0, matrix products: 145 us -> none  [the longest x25 136 us: dot(): return jnp.einsum(spec, a, b, preferred_element_type=F32)]
    ppermute x9 -> x1, starting transfers between devices: 124 us -> 0.74 us  [per_device(): lax.ppermute(code, 'dp', [(i, i ^ 1) for i in range(n_dp)])]
    pallas_call x2, Pallas kernels: 384 us -> 453 us  [the longest x1 280 us: second_part(): pl.pallas_call(second_kernel, out_shape=out_shape, in_specs=[anywhere] *...]
    convert_element_type x8 -> x0, other arithmetic: 20.7 us -> none  [the longest x2 10.8 us: per_device(): score_grad = (soft_rows * (prob_grad - row_inner)).astype(BF16)]
    reduce_sum x12 -> x0, other arithmetic: 19.3 us -> none  [the longest x2 9.2 us: per_device(): row_total = jnp.sum(exponent, axis=-1, keepdims=True)]
    unnamed x197 -> x21, local copies, waits for them, and re-layouts: 14 us -> 2.48 us
  transfers between devices with their start and end apart: 9 -> 1, of which waited for: 2 -> 0; matrix products, arithmetic and copies ran while one was open for 9% -> 1% of each run, Pallas kernels for 0% -> 0%
where the time goes in v2:
time: 485 us; the launch traced here: 477 us
  Pallas kernels  453 us (93%)
  local copies, waits for them, and re-layouts  12.7 us (3%)
  other arithmetic  9.06 us (2%)
    pallas_call x1, Pallas kernels, second_part(): pl.pallas_call(second_kernel, out_shape=out_shape, in_specs=[anywhere] *...  280 us
    pallas_call x1, Pallas kernels, first_part(): pl.pallas_call(first_kernel, out_shape=out_shape, in_specs=[anywhere] * 7...  173 us
  transfers between devices with their start and end apart: 1, of which 0 were waited for; matrix products, arithmetic and copies ran while one was open for 1% of the time, Pallas kernels for 0%

profile of v2, /device:TPU:9, one launch (start us, length us, event | category | flops | bytes accessed | tf_op | source)
XLA Modules:
  0.0 477.0 jit_solution(14909305046668696856)
XLA Ops:
  1.3 0.6 dynamic-slice
  1.9 1.4 dynamic-slice_add_fusion
  3.3 0.7 collective-permute-start
  4.1 2.3 pad_maximum_fusion.wqkv_ref
  6.3 0.1 concatenate.13
  6.4 0.6 broadcast_in_dim.32.gainqk_ref
  7.0 0.1 dynamic-slice_convert_fusion
  7.1 0.9 copy.33.alive_ref
  8.0 1.0 copy.32.qcode_ref
  9.0 1.0 copy.34.kcol_ref
  10.0 173.1 %gather_attention.1 = (bf16[2,1024,1152]{2,1,0:T(8,128)(2,1)}, bf16[2,1024,1152]{2,1,0:T(8,128)(2,1)}, bf16[2,1152,1024]{2,1,0:T(8,128)(2,1)}, bf16[2,1024,512]{...) custom-call(bf16[2,256,1024]{2,1,0:T(8,128)(2,1)} %x_ref.1, ...), custom_call_target="tpu_custom_call" | custom-call | tf_op jit(solution)/shard_map/gather_attention/pallas_call | solution.py:407
  183.1 279.8 %backward_scatter.1 = (bf16[2,256,1024]{2,1,0:T(8,128)(2,1)}, bf16[2,256,1024]{2,1,0:T(8,128)(2,1)}, f32[24,128]{1,0:T(8,128)}, f32[128,768]{1,0:T(8,128)}, f32[...) custom-call(bf16[2,1024,1152]{2,1,0:T(8,128)(2,1)} %get-tuple-elemen, ...), custom_call_target="tpu_custom_call" | custom-call | tf_op jit(solution)/shard_map/backward_scatter/pallas_call | solution.py:982
  462.9 0.8 slice_add_fusion
  463.7 1.3 slice_bitcast_fusion
  465.0 1.6 slice.45
  466.6 1.6 fusion.6
  468.2 0.5 slice_bitcast_fusion.2
  468.7 1.0 fusion.5
  469.7 2.8 convert_element_type.16
  472.6 0.9 pad_maximum_fusion.2
  473.5 0.9 pad_maximum_fusion.1
  474.3 1.0 copy.39
  475.3 0.7 copy.40
  476.0 0.8 copy.41
  (22 shorter events, 0.1 us)
Async XLA Ops:
  0.6 5.7 %copy-start.8 = (f32[64]{0:T(128)S(1)}, f32[64]{0:T(128)}, u32[]{:S(2)}) copy-start(f32[64]{0:T(128)} %param.30) | copy-start | bytes 772
  0.7 5.7 %copy-start.7 = (f32[64]{0:T(128)S(1)}, f32[64]{0:T(128)}, u32[]{:S(2)}) copy-start(f32[64]{0:T(128)} %param.29) | copy-start | bytes 772
  3.3 3.7 collective-permute-start
  7.0 3.0 copy-start.6
  7.0 176.1 %copy-start.5 = (s32[1024]{0:T(1024)}, s32[1024]{0:T(1024)S(1)}, u32[]{:S(2)}) copy-start(s32[1024]{0:T(1024)S(1)} %get-tuple-element.65) | copy-start | bytes 12292
  466.6 6.0 %copy-start.2 = (f32[128,768]{1,0:T(8,128)S(1)}, f32[128,768]{1,0:T(8,128)}, u32[]{:S(2)}) copy-start(f32[128,768]{1,0:T(8,128)} %get-tuple-element.58) | copy-start | bytes 1179652
  466.6 6.0 %copy-start.3 = (f32[128,768]{1,0:T(8,128)S(1)}, f32[128,768]{1,0:T(8,128)}, u32[]{:S(2)}) copy-start(f32[128,768]{1,0:T(8,128)} %get-tuple-element.59) | copy-start | bytes 1179652
  472.5 1.8 copy-start
  472.6 2.7 copy-start.4
  472.6 3.4 copy-start.1

commit v3 on v2

--- a/solution.py
+++ b/solution.py
@@ -154,66 +154,79 @@
             else:
                 wait()
 
-    def part(w, p, k, side=None):
+    pieces = []
+    for w in range(nw):
         q = shards[w].shape[0] // 4
-        start, size = pl.multiple_of(place.quarter(k) * q, q), q
+        if w < 2:
+            pieces.append((w, 0, q))
+        else:
+            cut = (q // 2 + 31) // 32 * 32
+            pieces += [(w, 0, cut), (w, cut, q - cut)]
+    QKV_, O_, G0, G1, U0, U1, D0, D1 = range(8)
+
+    def part(n, p, k, side=None):
+        w, at, size = pieces[n]
+        q = shards[w].shape[0] // 4
+        start = pl.multiple_of(place.quarter(k) * q + at, 16)
         if side is not None:
-            size = q // 2
-            start = pl.multiple_of(start + side * size, size)
+            size = size // 2
+            start = pl.multiple_of(start + side * size, 16)
         return full[w].at[p, pl.ds(start, size)]
 
-    def z_copies(w, go):
+    def z_copies(n, go):
+        w, at, size = pieces[n]
         q = shards[w].shape[0] // 4
 
         @pl.when(near)
         def _():
-            for i, to in enumerate((2 * place.half + 1 - par, 2 - c)):
-                cp = remote(shards[w].at[rows_at(j * q, q)], part(w, par, 0), zs.at[w, i], zr.at[w, par], place.column(c, to))
+            rows = pl.ds(pl.multiple_of(j * q + at, 16), size)
+            for i, to in enumerate((2 - c, 2 * place.half + 1 - par)):
+                cp = remote(shards[w].at[rows], part(n, par, 0), zs.at[n, i], zr.at[n, par], place.column(c, to))
                 cp.start() if go else cp.wait_send()
 
-    def z_onward(w, p):
-        return remote(part(w, p, 0), part(w, p, 0), zs.at[w, p], zr.at[w, p], place.column(c, 3 - 3 * c))
+    def z_onward(n, p):
+        return remote(part(n, p, 0), part(n, p, 0), zs.at[n, p], zr.at[n, p], place.column(c, 3 - 3 * c))
 
     def missing(p, body):
         pl.when(jnp.logical_or(jnp.logical_not(near), par != p))(body)
 
-    def step_copy(w, p, i):
+    def step_copy(n, p, i):
         k, side, to = ((0, None, 1), (0, None, 2), (1, 0, 2), (2, 1, 1))[i]
-        return remote(part(w, p, k, side), part(w, p, k, side), fs.at[w, p, i], fr.at[w, p, i], place.plane(to))
-
-    def first(w):
+        return remote(part(n, p, k, side), part(n, p, k, side), fs.at[n, p, i], fr.at[n, p, i], place.plane(to))
+
+    def first(n):
         for p in range(2):
             @functools.partial(missing, p)
             def _():
-                z_onward(w, p).wait_recv()
-                pl.when(inner)(lambda: z_onward(w, p).start())
-                step_copy(w, p, 0).start()
-                step_copy(w, p, 1).start()
-
-    def second(w):
+                z_onward(n, p).wait_recv()
+                pl.when(inner)(lambda: z_onward(n, p).start())
+                step_copy(n, p, 0).start()
+                step_copy(n, p, 1).start()
+
+    def second(n):
         for p in range(2):
             @functools.partial(missing, p)
             def _():
-                step_copy(w, p, 0).wait_recv()
-                step_copy(w, p, 2).start()
-                step_copy(w, p, 1).wait_recv()
-                step_copy(w, p, 3).start()
-
-    def third(w):
+                step_copy(n, p, 0).wait_recv()
+                step_copy(n, p, 2).start()
+                step_copy(n, p, 1).wait_recv()
+                step_copy(n, p, 3).start()
+
+    def third(n):
         for p in range(2):
             @functools.partial(missing, p)
             def _():
-                step_copy(w, p, 2).wait_recv()
-                step_copy(w, p, 3).wait_recv()
-
-    def sent(w):
-        z_copies(w, False)
+                step_copy(n, p, 2).wait_recv()
+                step_copy(n, p, 3).wait_recv()
+
+    def sent(n):
+        z_copies(n, False)
         for p in range(2):
             @functools.partial(missing, p)
             def _():
-                pl.when(inner)(lambda: z_onward(w, p).wait_send())
+                pl.when(inner)(lambda: z_onward(n, p).wait_send())
                 for i in range(4):
-                    step_copy(w, p, i).wait_send()
+                    step_copy(n, p, i).wait_send()
 
     def own_load(w):
         return pltpu.make_async_copy(shards[w], full[w].at[par], own_l.at[w])
@@ -225,11 +238,12 @@
 
     saves = []
 
-    token_copies(0, x_ref, xbuf, True)
-    for w in range(nw):
-        z_copies(w, True)
-        if w < 2:
-            pl.when(near)(lambda: own_load(w).start())
+    for n in range(len(pieces)):
+        z_copies(n, True)
+        if n < 2:
+            pl.when(near)(lambda: own_load(n).start())
+        if n == U0:
+            token_copies(0, x_ref, xbuf, True)
     token_copies(1, ct_ref, cbuf, True)
 
     for i in range(seq // BLK):
@@ -242,6 +256,16 @@
             mask[i * BLK : (i + 1) * BLK, jb * BLK : (jb + 1) * BLK] = jnp.where(same, 1.0, 0.0).astype(F32)
     v2[:, :, 128:] = jnp.ones((v2.shape[0], v2.shape[1], 128), BF16)
 
+    first(QKV_)
+    first(O_)
+    second(QKV_)
+    first(G0)
+    second(O_)
+    first(G1)
+    second(G0)
+    first(U0)
+    second(G1)
+
     token_arrivals(0, x_ref, xbuf)
     step = 128
 
@@ -259,15 +283,13 @@
         remote(buf.at[rows_at((1 - c) * half, half)], buf.at[rows_at((1 - c) * half, half)], ms.at[n], mr.at[n], mate).wait_recv()
 
     swap_rows(normed, 0).start()
-    first(0)
-    first(1)
-    second(0)
-    second(1)
+    second(U0)
+    first(U1)
     save(0, xbuf, o_x)
     swap_wait(normed, 0)
     save(1, normed, o_normed)
     pl.when(near)(lambda: own_load(0).wait())
-    third(0)
+    third(QKV_)
 
     @pl.loop(0, seq // BLK)
     def _(r):
@@ -302,7 +324,8 @@
     save(4, qs, o_q)
     save(5, k2, o_k)
     save(6, v2.at[:, :, pl.ds(0, 128)], o_v)
-    first(2)
+    first(D0)
+    second(U1)
     for i in range(seq // BLK):
         n = (i + 1) * BLK
         rows = pl.ds(i * BLK, BLK)
@@ -320,13 +343,12 @@
             linv[rows, cols] = jnp.where(left, inv[:BLK], inv[BLK:])
 
         if i == 1:
-            second(2)
-            first(3)
+            first(D1)
+            second(D0)
     save(7, att, o_att)
     save(8, linv, o_linv)
-    second(3)
     pl.when(near)(lambda: own_load(1).wait())
-    third(1)
+    third(O_)
     save(9, wo, o_wo)
 
     def out_rows(start):
@@ -343,7 +365,7 @@
     def _(r):
         hidden[rows_at(r * BLK, BLK), :] = out_rows(c * half + r * BLK) + xbuf[rows_at(r * BLK, BLK), :].astype(F32)
 
-    first(4)
+    second(D1)
     swap_give.wait_recv()
 
     @pl.loop(0, half // step)
@@ -355,7 +377,6 @@
 
     swap_rows(n2, 2).start()
     save(10, hidden, o_hidden)
-    second(4)
     token_arrivals(1, ct_ref, cbuf)
 
     @pl.loop(0, half // step)
@@ -368,10 +389,10 @@
     save(11, n2, o_n2)
     swap_wait(din, 3)
     save(12, din, o_din)
-    for w in range(2, nw):
-        third(w)
-    for w in range(nw):
-        sent(w)
+    for n in range(2, len(pieces)):
+        third(n)
+    for n in range(len(pieces)):
+        sent(n)
     token_sent(0, x_ref, xbuf)
     token_sent(1, ct_ref, cbuf)
     swap_rows(normed, 0).wait_send()
@@ -413,7 +434,7 @@
             vm("wqkv"), vm("wo"), vm("x"), pltpu.VMEM((half, width), BF16), vm("normed"), vm("n2"), vm("din"), vm("hidden"), vm("qk"),
             vm("q"), vm("k"), pltpu.VMEM((groups, seq, 256), BF16), pltpu.VMEM((seq, seq), F32), vm("att"), vm("linv"), pltpu.VMEM((half, width), BF16),
             pltpu.VMEM((half, width), BF16),
-            dma((2, 2)), dma((2, 2)), dma((2,)), dma((nw,)), dma((nw, 2)), dma((nw, 2)), dma((nw, 2, 4)), dma((nw, 2, 4)),
+            dma((2, 2)), dma((2, 2)), dma((2,)), dma((2,)), dma((8, 2)), dma((8, 2)), dma((8, 2, 4)), dma((8, 2, 4)),
             dma((4,)), dma((4,)), dma((13,)),
         ],
         compiler_params=pltpu.CompilerParams(collective_id=0, has_side_effects=True, vmem_limit_bytes=60 * 1024 * 1024),
@@ -432,10 +453,10 @@
                   ones_ref,
                   oo, io, gain_out, s_gu0, s_gu1, s_gu2, s_d, s_o, s_qkv,
                   p_gu0, p_gu1, p_gu2, p_d, p_o, p_qkv, c_gu0, c_gu1, c_gu2, c_d, c_o, c_qkv,
-                  g_a, g_b, g_d, g_o, g_qkv, d_gu0, d_gu1, d_gu2, d_d, d_o, d_qkv, stage, last, give, take, obuf, hgrad,
+                  g_a, g_b, g_c, g_d, g_o, g_qkv, d_gu0, d_gu1, d_gu2, d_d, d_o, d_qkv, stage, last, give, take, obuf, hgrad,
                   gain_in, attn_in,
                   tok_s, tok_r, tok_l, ps, pr, cs, cr, ls, lr, ll, gs, gr, ms, mr, ld, wl, st_sem):
-    grads = (g_a, g_b, g_a, g_d, g_o, g_qkv)
+    grads = (g_a, g_b, g_c, g_d, g_o, g_qkv)
     diag = (d_gu0, d_gu1, d_gu2, d_d, d_o, d_qkv)
     plane_in = (p_gu0, p_gu1, p_gu2, p_d, p_o, p_qkv)
     col_in = (c_gu0, c_gu1, c_gu2, c_d, c_o, c_qkv)
@@ -523,32 +544,32 @@
         to = place.column(c, 2 * place.half + 1 - par)
         return remote(diag[w].at[:, 1 - par], col_in[w].at[:, 0], cs.at[w, 0], cr.at[w, 0], to)
 
-    def staged(w, n):
+    def staged(w):
         e = grads[w].shape[1] // 8
-        return stage.at[pl.ds(0, n), :, :, pl.ds(0, e), pl.ds(0, grads[w].shape[2])]
+        return stage.at[:, :, pl.ds(0, e), pl.ds(0, grads[w].shape[2])]
 
     def add_plane(w):
         for i in range(2):
             for side in range(2):
                 plane_copy(w, i, side).wait()
-        cp = pltpu.make_async_copy(plane_in[w], staged(w, 2), st_sem.at[0])
-        cp.start()
-        cp.wait()
         e, n = grads[w].shape[1] // 8, grads[w].shape[2]
+        cps = [pltpu.make_async_copy(plane_in[w].at[:, side], staged(w), st_sem.at[side]) for side in range(2)]
         for side in range(2):
+            cps[side].start()
+            cps[side].wait()
             rows = rows_of(w, 0, side)
             for p in range(2):
                 total = (
                     grads[w][p, rows, :].astype(F32)
-                    + stage[0, side, p, :e, :n].astype(F32)
-                    + stage[1, side, p, :e, :n].astype(F32)
+                    + stage[0, p, :e, :n].astype(F32)
+                    + stage[1, p, :e, :n].astype(F32)
                 )
                 diag[w][side, p] = total.astype(BF16)
         pl.when(outer)(lambda: outer_copy(w).start())
         pl.when(near)(lambda: near_copy(w).start())
 
     def load_column(w):
-        cp = pltpu.make_async_copy(col_in[w], staged(w, 1).at[0], st_sem.at[1])
+        cp = pltpu.make_async_copy(col_in[w], staged(w), st_sem.at[0])
         cp.start()
         cp.wait()
 
@@ -560,11 +581,11 @@
             e, n = grads[w].shape[1] // 8, grads[w].shape[2]
             for p in range(2):
                 for side in range(2):
-                    diag[w][side, p] = (diag[w][side, p].astype(F32) + stage[0, side, p, :e, :n].astype(F32)).astype(BF16)
+                    diag[w][side, p] = (diag[w][side, p].astype(F32) + stage[side, p, :e, :n].astype(F32)).astype(BF16)
                 inner_copy(w, p).start()
 
     def last_view(w, k):
-        return last.at[w % 2, k, pl.ds(0, grads[w].shape[1] // 8), pl.ds(0, grads[w].shape[2])]
+        return last.at[k, pl.ds(0, grads[w].shape[1] // 8), pl.ds(0, grads[w].shape[2])]
 
     def last_remote(w):
         return remote(last_view(w, 1), sums[w], ls.at[w], lr.at[w], mate)
@@ -579,8 +600,8 @@
             last_local(w).wait()
 
     def add_column(w):
-        if w >= 2:
-            release_last(w - 2)
+        if w >= 1:
+            release_last(w - 1)
 
         @pl.when(near)
         def _():
@@ -590,16 +611,16 @@
             load_column(w)
             for hc in range(2):
                 total = (
-                    diag[w][hc, par].astype(F32) + stage[0, hc, 0, :e, :n].astype(F32) + stage[0, hc, 1, :e, :n].astype(F32)
+                    diag[w][hc, par].astype(F32) + stage[hc, 0, :e, :n].astype(F32) + stage[hc, 1, :e, :n].astype(F32)
                 )
 
                 @pl.when(c == hc)
                 def _():
-                    last[w % 2, 0, :e, :n] = total
+                    last[0, :e, :n] = total
 
                 @pl.when(c != hc)
                 def _():
-                    last[w % 2, 1, :e, :n] = total
+                    last[1, :e, :n] = total
 
             last_remote(w).start()
             last_local(w).start()
@@ -615,84 +636,78 @@
             inner_copy(w, 1).wait_send()
 
     def trade(n):
-        return remote(give.at[n % 2], take.at[n], ms.at[n], mr.at[n], mate)
+        return remote(give.at[n % 2], take.at[n % 2], ms.at[n], mr.at[n], mate)
 
     def load(n, src, dst):
         return pltpu.make_async_copy(src, dst, ld.at[n])
 
-    def ffn(n2, din, n2t, wg, wu, wd, acc_o, acc_n, act, gr, ur):
+    n2 = attn_in
+
+    def ffn(din, wg, wu, wd, acc_o, acc_n, act, gu_rows):
         loads = [load(0, n2_ref, n2), load(1, din_ref, din)]
         for cp in loads:
             cp.start()
 
-        def tile_loads(i, go):
-            t, p = i // 2, i % 2
-            b = i % 2
+        def tile_loads(t, go):
             cols = pl.ds(t * TILE, TILE)
-            mine = near & (par == p)
-
-            def run(g, u, d):
-                for k, (src, dst) in enumerate(((g.at[:, cols], wg.at[b]), (u.at[:, cols], wu.at[b]), (d.at[cols], wd.at[b]))):
-                    cp = pltpu.make_async_copy(src, dst, wl.at[b, k])
-                    cp.start() if go else cp.wait()
-
-            if go:
-                pl.when(mine)(lambda: run(wg_ref, wu_ref, wd_ref))
-                pl.when(jnp.logical_not(mine))(lambda: run(gg.at[p], gu.at[p], gd.at[p]))
-            else:
-                run(gg.at[p], gu.at[p], gd.at[p])
+            for p in range(2):
+                here = pl.ds(p * TILE, TILE)
+
+                def run(g, u, d):
+                    pairs = ((g.at[:, cols], wg.at[:, here]), (u.at[:, cols], wu.at[:, here]), (d.at[cols], wd.at[here]))
+                    for k, (src, dst) in enumerate(pairs):
+                        cp = pltpu.make_async_copy(src, dst, wl.at[p, k])
+                        cp.start() if go else cp.wait()
+
+                if go:
+                    mine = near & (par == p)
+                    pl.when(mine)(lambda: run(wg_ref, wu_ref, wd_ref))
+                    pl.when(jnp.logical_not(mine))(lambda: run(gg.at[p], gu.at[p], gd.at[p]))
+                else:
+                    run(gg.at[p], gu.at[p], gd.at[p])
 
         tile_loads(0, True)
         for cp in loads:
             cp.wait()
-
-        @pl.loop(0, seq // BLK)
-        def _(r):
-            cols = pl.ds(pl.multiple_of(r * BLK, BLK), BLK)
-            n2t[:, cols] = n2[cols, :].T
-
-        for i in range(2 * PIECES):
-            t, p = i // 2, i % 2
-            b = i % 2
-            if i + 1 < 2 * PIECES:
-                tile_loads(i + 1, True)
-            tile_loads(i, False)
+        for t in range(PIECES):
+            tile_loads(t, False)
 
             @pl.loop(0, seq // BLK)
             def _(r):
                 rows = rows_at(r * BLK, BLK)
                 a = n2[rows, :]
-                g = mm(a, wg[b])
-                u = mm(a, wu[b])
-                ag = mm_nt(din[rows, :], wd[b])
+                g = mm(a, wg[...])
+                u = mm(a, wu[...])
+                ag = mm_nt(din[rows, :], wd[...])
                 sig = jax.nn.sigmoid(g)
                 gs_ = g * sig
                 av = (gs_ * u).astype(BF16)
-                act[p, rows, t * TILE : (t + 1) * TILE] = av
-                gv = (ag * u * sig * (1.0 + g * (1.0 - sig))).astype(BF16)
+                act[t, rows, :] = av
+                gv = (ag * u * (sig + gs_ * (1.0 - sig))).astype(BF16)
                 uv = (ag * gs_).astype(BF16)
-                gr[rows, :] = gv
-                ur[rows, :] = uv
-                dn = mm_nt(gv, wg[b]) + mm_nt(uv, wu[b])
-                do = mm(av, wd[b])
-                if i == 0:
+                for p in range(2):
+                    gu_rows[rows, 2 * p * TILE : (2 * p + 1) * TILE] = gv[:, p * TILE : (p + 1) * TILE]
+                    gu_rows[rows, (2 * p + 1) * TILE : (2 * p + 2) * TILE] = uv[:, p * TILE : (p + 1) * TILE]
+                dn = mm_nt(gv, wg[...]) + mm_nt(uv, wu[...])
+                do = mm(av, wd[...])
+                if t == 0:
                     acc_n[rows, :] = dn
                     acc_o[rows, :] = do
                 else:
                     acc_n[rows, :] += dn
                     acc_o[rows, :] += do
 
+            if t + 1 < PIECES:
+                tile_loads(t + 1, True)
+
             @pl.loop(0, width // BLK)
             def _(r):
-                rows = rows_at(r * BLK, BLK)
-                grads[t][p, rows, :TILE] = mm(n2t[rows, :], gr[...]).astype(BF16)
-                grads[t][p, rows, TILE:] = mm(n2t[rows, :], ur[...]).astype(BF16)
-
-            if p == 1:
-                begin(t)
-                if t == 1:
-                    add_diag(0)
-                    add_plane(0)
+                cols = pl.ds(pl.multiple_of(r * BLK, BLK), BLK)
+                o = mm_tn(n2[:, cols], gu_rows[...]).astype(BF16)
+                for p in range(2):
+                    grads[t][p, cols, :] = o[:, 2 * p * TILE : 2 * (p + 1) * TILE]
+
+            begin(t)
 
         @pl.loop(0, half // BLK)
         def _(r):
@@ -704,13 +719,14 @@
         trade(1).start()
         hid_load = load(2, hidden_ref, hgrad)
         hid_load.start()
+        add_diag(0)
         for p in range(2):
             @pl.loop(0, width // BLK)
             def _(r):
                 cols = pl.ds(pl.multiple_of(r * BLK, BLK), BLK)
                 for k in range(PIECES):
                     rows = pl.ds(k * TILE, TILE)
-                    grads[D_][p, rows, cols] = mm_tn(act[p, :, rows], din[:, cols]).astype(BF16)
+                    grads[D_][p, rows, cols] = mm_tn(act[k, :, p * TILE : (p + 1) * TILE], din[:, cols]).astype(BF16)
 
         begin(D_)
         hid_load.wait()
@@ -743,10 +759,10 @@
     gain_out[...] = jnp.zeros(gain_out.shape, F32)
     pl.run_scoped(
         ffn,
-        pltpu.VMEM((seq, width), BF16), pltpu.VMEM((seq, width), BF16), pltpu.VMEM((width, seq), BF16),
-        pltpu.VMEM((2, width, TILE), BF16), pltpu.VMEM((2, width, TILE), BF16), pltpu.VMEM((2, TILE, width), BF16),
-        pltpu.VMEM((seq, width), F32), pltpu.VMEM((seq, width), F32), pltpu.VMEM((2, seq, PIECES * TILE), BF16),
-        pltpu.VMEM((seq, TILE), BF16), pltpu.VMEM((seq, TILE), BF16),
+        pltpu.VMEM((seq, width), BF16),
+        pltpu.VMEM((width, 2 * TILE), BF16), pltpu.VMEM((width, 2 * TILE), BF16), pltpu.VMEM((2 * TILE, width), BF16),
+        pltpu.VMEM((seq, width), F32), pltpu.VMEM((seq, width), F32), pltpu.VMEM((PIECES, seq, 2 * TILE), BF16),
+        pltpu.VMEM((seq, 4 * TILE), BF16),
     )
 
     def attn_swap():
@@ -794,14 +810,15 @@
                     grads[O_][p, :, cols] = mm_tn(att[:, p * 256 : (p + 1) * 256], attn_in[:, cols]).astype(BF16)
 
             begin(O_)
+            add_plane(0)
+            add_diag(2)
 
         pl.run_scoped(
             front, pltpu.VMEM(wo_ref.shape, BF16), pltpu.VMEM(att_ref.shape, BF16), pltpu.VMEM(linv_ref.shape, F32),
         )
-        add_plane(1)
-        add_diag(2)
-
-        def rest(q, k, v, mt, qk, rows_, wqkv, normed, x):
+        def rest(q, k, v, mt, qk, rows_, wqkv, normed):
+            trade(1).wait_send()
+            x = give.at[1]
             loads = [load(6, q_ref, q), load(7, k_ref, k), load(8, v_ref, v)]
             later = [load(9, qk_ref, qk), load(10, wqkv_ref, wqkv), load(11, normed_ref, normed), load(12, x_ref, x)]
             for cp in loads + later:
@@ -809,12 +826,7 @@
             for cp in loads:
                 cp.wait()
             dq[...] = jnp.zeros(dq.shape, F32)
-            todo = {
-                0: [lambda: add_outer(0), lambda: add_plane(2)],
-                1: [lambda: add_diag(D_), lambda: add_column(0), lambda: add_outer(1)],
-                2: [lambda: add_plane(D_), lambda: add_diag(O_), lambda: add_column(1), lambda: add_outer(2)],
-                3: [lambda: add_plane(O_), lambda: add_column(2), lambda: add_outer(D_)],
-            }
+            todo = {0: [], 1: [], 2: [lambda: add_diag(O_)], 3: [lambda: add_outer(0), lambda: add_plane(1), lambda: add_diag(D_)]}
             for jb in range(seq // BLK):
                 at = jb * BLK
                 ni = seq - at
@@ -898,15 +910,13 @@
                     grads[QKV_][p, cols, :] = mm_tn(normed[:, cols], rows_[p]).astype(BF16)
 
             begin(QKV_)
-            add_column(D_)
-            add_outer(O_)
             trade(2).wait_recv()
             token_copies(0, obuf, oo, False)
 
             @pl.loop(0, half // BLK)
             def _(r):
                 rows = rows_at(r * BLK, BLK)
-                ng = back_rows(own_at + r * BLK) + take[2, rows, :].astype(F32)
+                ng = back_rows(own_at + r * BLK) + take[0, rows, :].astype(F32)
                 xs = x[rows, :].astype(F32)
                 sc = lax.rsqrt(jnp.mean(xs * xs, axis=-1, keepdims=True) + EPS)
                 unit = xs * sc
@@ -918,38 +928,50 @@
         V = pltpu.VMEM
         pl.run_scoped(
             rest, V(q_ref.shape, BF16), V(k_ref.shape, BF16), V(v_ref.shape, BF16), V((BLK, seq), F32), V(qk_ref.shape, F32),
-            V((2, seq, 512), BF16), V(wqkv_ref.shape, BF16), V(normed_ref.shape, BF16), V(x_ref.shape, BF16),
+            V((2, seq, 512), BF16), V(wqkv_ref.shape, BF16), V(normed_ref.shape, BF16),
         )
 
     pl.run_scoped(
         attention, pltpu.VMEM(q_ref.shape, BF16), pltpu.VMEM((seq, 512), F32), pltpu.VMEM((4, seq, 128), F32),
         pltpu.VMEM((4, seq, 128), F32), pltpu.VMEM((4, 2, 8, seq), F32),
     )
-    token_copies(1, obuf, io, True)
-
     def gain_copy(i):
-        to = (mate, place.plane(1), place.plane(2), place.column(c, 2 * place.half + 1 - par),
-              place.column(c, 2 - 2 * place.half + par))[i]
+        to = (place.column(c, 2 * place.half + 1 - par), place.column(c, 2 - 2 * place.half + par), place.plane(1), place.plane(2),
+              mate)[i]
         return remote(gain_out, gain_in.at[i], gs.at[i], gr.at[i], to)
 
-    for i in range(5):
-        gain_copy(i).start()
-        if i == 0:
-            add_diag(QKV_)
-        if i == 1:
-            add_column(O_)
-        if i == 2:
-            add_plane(QKV_)
-        if i == 3:
-            add_outer(QKV_)
+    def gain_step(i):
         gain_copy(i).wait()
         gain_out[...] += gain_in[i]
+        if i < 4:
+            gain_copy(i + 1).start()
+
+    gain_copy(0).start()
+    token_copies(1, obuf, io, True)
+    add_plane(2)
+    add_column(0)
+    gain_step(0)
+    add_outer(1)
+    gain_step(1)
+    add_column(1)
+    add_plane(D_)
+    gain_step(2)
+    add_outer(2)
+    add_diag(QKV_)
+    gain_step(3)
+    add_column(2)
+    add_plane(O_)
+    gain_step(4)
+    add_outer(D_)
+    add_outer(O_)
+    add_plane(QKV_)
+    add_column(D_)
+    add_column(O_)
+    add_outer(QKV_)
     add_column(QKV_)
-    release_last(nw - 2)
     release_last(nw - 1)
     for w in range(nw):
         finish(w)
-    trade(1).wait_send()
     trade(2).wait_send()
     attn_swap().wait_send()
     token_copies(1, obuf, io, False)
@@ -966,7 +988,7 @@
     wg, wu, wd = shards
     r_d = wd.shape[0]
     sizes = [(width, 2 * TILE)] * 3 + [(r_d, width), (kept["wo"].shape[1], width), (width, kept["wqkv"].shape[2])]
-    held = [sizes[0], sizes[1]] + sizes[3:]
+    held = sizes
     nw = 6
     order = ("wqkv", "wo", "x", "din", "normed", "n2", "hidden", "qk", "q", "k", "v", "att", "linv")
     gains = (24, 128)
@@ -987,7 +1009,7 @@
         scratch_shapes=[V((2, r, n), BF16) for r, n in held]
         + [V((2, 2, r // 8, n), BF16) for r, n in sizes]
         + [
-            V((2, 2, 2, e_max, n_max), BF16), V((2, 2, e_max, n_max), F32), V((2, half, width), BF16), V((3, half, width), BF16),
+            V((2, 2, e_max, n_max), BF16), V((2, e_max, n_max), F32), V((2, half, width), BF16), V((2, half, width), BF16),
             V((half, width), BF16), V((half, width), F32), V((5,) + gains, F32), V((2 * half, width), BF16),
         ]
         + [

time: 485 us -> 399 us (0.82); the launches traced: 477 us -> 398 us
  Pallas kernels: 453 us -> 374 us
    pallas_call x1, Pallas kernels: 280 us -> 235 us  [second_part(): pl.pallas_call(second_kernel, out_shape=out_shape, in_specs=[anywhere] *...]
    pallas_call x1, Pallas kernels: 173 us -> 139 us  [first_part(): pl.pallas_call(first_kernel, out_shape=out_shape, in_specs=[anywhere] * 7...]
where the time goes in v3:
time: 399 us; the launch traced here: 398 us
  Pallas kernels  374 us (94%)
  local copies, waits for them, and re-layouts  12.7 us (3%)
  other arithmetic  9.06 us (2%)
    pallas_call x1, Pallas kernels, second_part(): pl.pallas_call(second_kernel, out_shape=out_shape, in_specs=[anywhere] *...  235 us
    pallas_call x1, Pallas kernels, first_part(): pl.pallas_call(first_kernel, out_shape=out_shape, in_specs=[anywhere] * 7...  139 us
  transfers between devices with their start and end apart: 1, of which 0 were waited for; matrix products, arithmetic and copies ran while one was open for 1% of the time, Pallas kernels for 0%

profile of v3, /device:TPU:9, one launch (start us, length us, event | category | flops | bytes accessed | tf_op | source)
XLA Modules:
  0.0 398.0 jit_solution(15458698190647972791)
XLA Ops:
  1.3 0.6 dynamic-slice
  1.9 1.4 dynamic-slice_add_fusion
  3.3 0.7 collective-permute-start
  4.1 2.3 pad_maximum_fusion.wqkv_ref
  6.3 0.1 concatenate.13
  6.4 0.6 broadcast_in_dim.32.gainqk_ref
  7.0 0.1 dynamic-slice_convert_fusion
  7.1 0.9 copy.33.alive_ref
  8.0 1.0 copy.32.qcode_ref
  9.0 1.0 copy.34.kcol_ref
  10.0 139.4 %gather_attention.1 = (bf16[2,1024,1152]{2,1,0:T(8,128)(2,1)}, bf16[2,1024,1152]{2,1,0:T(8,128)(2,1)}, bf16[2,1152,1024]{2,1,0:T(8,128)(2,1)}, bf16[2,1024,512]{...) custom-call(bf16[2,256,1024]{2,1,0:T(8,128)(2,1)} %x_ref.1, ...), custom_call_target="tpu_custom_call" | custom-call | tf_op jit(solution)/shard_map/gather_attention/pallas_call | solution.py:428
  149.5 234.7 %backward_scatter.1 = (bf16[2,256,1024]{2,1,0:T(8,128)(2,1)}, bf16[2,256,1024]{2,1,0:T(8,128)(2,1)}, f32[24,128]{1,0:T(8,128)}, f32[128,768]{1,0:T(8,128)}, f32[...) custom-call(bf16[2,1024,1152]{2,1,0:T(8,128)(2,1)} %get-tuple-elemen, ...), custom_call_target="tpu_custom_call" | custom-call | tf_op jit(solution)/shard_map/backward_scatter/pallas_call | solution.py:1004
  384.1 0.8 slice_add_fusion
  384.9 1.3 slice_bitcast_fusion
  386.2 1.6 slice.45
  387.8 1.6 fusion.6
  389.4 0.5 slice_bitcast_fusion.2
  389.9 1.0 fusion.5
  391.0 2.8 convert_element_type.16
  393.8 0.9 pad_maximum_fusion.2
  394.7 0.9 pad_maximum_fusion.1
  395.6 1.0 copy.39
  396.5 0.7 copy.40
  397.2 0.8 copy.41
  (22 shorter events, 0.1 us)
Async XLA Ops:
  0.6 5.7 %copy-start.8 = (f32[64]{0:T(128)S(1)}, f32[64]{0:T(128)}, u32[]{:S(2)}) copy-start(f32[64]{0:T(128)} %param.30) | copy-start | bytes 772
  0.7 5.7 %copy-start.7 = (f32[64]{0:T(128)S(1)}, f32[64]{0:T(128)}, u32[]{:S(2)}) copy-start(f32[64]{0:T(128)} %param.29) | copy-start | bytes 772
  3.3 3.7 collective-permute-start
  7.0 3.0 copy-start.6
  7.0 142.4 %copy-start.5 = (s32[1024]{0:T(1024)}, s32[1024]{0:T(1024)S(1)}, u32[]{:S(2)}) copy-start(s32[1024]{0:T(1024)S(1)} %get-tuple-element.65) | copy-start | bytes 12292
  387.8 6.0 %copy-start.2 = (f32[128,768]{1,0:T(8,128)S(1)}, f32[128,768]{1,0:T(8,128)}, u32[]{:S(2)}) copy-start(f32[128,768]{1,0:T(8,128)} %get-tuple-element.58) | copy-start | bytes 1179652
  387.8 6.0 %copy-start.3 = (f32[128,768]{1,0:T(8,128)S(1)}, f32[128,768]{1,0:T(8,128)}, u32[]{:S(2)}) copy-start(f32[128,768]{1,0:T(8,128)} %get-tuple-element.59) | copy-start | bytes 1179652
  393.8 1.8 copy-start
  393.8 2.7 copy-start.4
  393.8 3.4 copy-start.1

commit v4 on v3

v4 whole, which is shorter than its diff:
```python
import functools

import jax
import jax.numpy as jnp
import numpy as np
from jax import lax
from jax.experimental import pallas as pl
from jax.experimental.pallas import tpu as pltpu
from jax.sharding import PartitionSpec as P

EPS = 1e-05
THETA = 1000000.0
ALIVE = 4096
MESH = pl.DeviceIdType.MESH
BF16 = jnp.bfloat16
F32 = jnp.float32


class Place:
    def __init__(self):
        self.dp = lax.axis_index("dp")
        self.z = lax.axis_index("tensor")
        self.c = lax.rem(self.dp, 2)
        self.j = lax.rem(self.dp // 2, 4)
        self.half = self.z // 2
        self.par = lax.rem(self.z, 2)
        self.near = self.half == self.c

    def plane(self, k):
        j = self.j
        bit = lax.rem(j // k, 2)
        return (self.dp + (1 - 2 * bit) * 2 * k, self.z)

    def column(self, c, z):
        return (self.dp - self.c + c, z)

    def quarter(self, k):
        j = self.j
        low, high = lax.rem(j, 2), j // 2
        if k & 1:
            low = 1 - low
        if k & 2:
            high = 1 - high
        return 2 * high + low


def greet(place):
    barrier = pltpu.get_barrier_semaphore()
    for k in (1, 2):
        pl.semaphore_signal(barrier, inc=1, device_id=place.plane(k), device_id_type=MESH)
    for dc in range(2):
        for dz in range(4):
            if dc or dz:
                c = lax.rem(place.c + dc, 2)
                z = lax.rem(place.z + dz, 4)
                pl.semaphore_signal(barrier, inc=1, device_id=place.column(c, z), device_id_type=MESH)
    pl.semaphore_wait(barrier, 9)


def remote(src, dst, send, recv, device):
    return pltpu.make_async_remote_copy(
        src_ref=src, dst_ref=dst, send_sem=send, recv_sem=recv, device_id=device, device_id_type=MESH
    )


def lane_swap(v):
    lane = lax.broadcasted_iota(jnp.int32, v.shape, 1)
    return jnp.where(lane % 64 < 32, pltpu.roll(v, 96, 1), pltpu.roll(v, 32, 1))


def head_mean(v, ones_ref, n):
    high = v.astype(BF16)
    low = (v - high.astype(F32)).astype(BF16)
    ones = ones_ref[:n, :n]
    return jnp.dot(high, ones, preferred_element_type=F32) + jnp.dot(low, ones, preferred_element_type=F32)


def mm(a, b):
    return jnp.dot(a, b, preferred_element_type=F32)


def mm_nt(a, b):
    return lax.dot_general(a, b, (((1,), (1,)), ((), ())), preferred_element_type=F32)


def mm_tn(a, b):
    return lax.dot_general(a, b, (((0,), (0,)), ((), ())), preferred_element_type=F32)


BLK = 256


def rows_at(start, size):
    return pl.ds(pl.multiple_of(start, size), size)


TILE = 384
PIECES = 3


def layer_kernel(x_ref, ct_ref, wqkv_ref, wo_ref, wg_ref, wu_ref, wd_ref, cols_ref, rows_ref,
                 gain1_ref, gain2_ref, gainqk_ref, cos_ref, sin_ref, ones_ref,
                 oo, io, gain_out, s_q, s_k, s_v, s_o, s_gate, s_up, s_down,
                 gqkv, go, gg, gu, gd, hx, hc, h_normed, h_qk, h_q, h_k, h_v, h_att, h_linv,
                 p_gu0, p_gu1, p_gu2, p_d0, p_d1, p_o, p_qkv, c_gu0, c_gu1, c_gu2, c_d0, c_d1, c_o, c_qkv,
                 g_a, g_b, g_c, g_d0, g_d1, g_o, g_qkv, d_gu0, d_gu1, d_gu2, d_d0, d_d1, d_o, d_qkv, last, give, take, obuf, hgrad,
                 gain_in, attn_in, din,
                 in_s, in_r, tok_s, tok_r, tok_l, zs, zr, fs, fr, ps, pr, cs, cr, ls, lr, ll, gs, gr, ms, mr, ld, wl, pls, cls,
                 outs):
    shards = (wqkv_ref, wo_ref, wg_ref, wu_ref, wd_ref)
    full = (gqkv, go, gg, gu, gd)
    grads = (g_a, g_b, g_c, g_d0, g_d1, g_o, g_qkv)
    diag = (d_gu0, d_gu1, d_gu2, d_d0, d_d1, d_o, d_qkv)
    plane_in = (p_gu0, p_gu1, p_gu2, p_d0, p_d1, p_o, p_qkv)
    col_in = (c_gu0, c_gu1, c_gu2, c_d0, c_d1, c_o, c_qkv)
    nw = 7
    DA_, DB_, O_, QKV_ = 3, 4, 5, 6
    turn = (0, 1, 2, 3, 4, 5, 6)
    place = Place()
    z, c, par, near, j = place.z, place.c, place.par, place.near, place.j
    inner = jnp.where(c == 0, z == 2, z == 1)
    outer = jnp.where(c == 0, z == 3, z == 0)
    half = obuf.shape[0]
    seq = 2 * half
    seg = half // 2
    width = obuf.shape[1]
    mate = place.column(1 - c, z)
    own_at = c * half
    other_at = (1 - c) * half
    step = 128
    n2 = attn_in
    normed_buf = din
    greet(place)

    def fetch_copies(a, src, dst, go):
        for b in range(2):
            slot = par if b == 0 else 1 - par
            target = place.column(place.half, 2 * c + slot)

            def far_copy():
                cp = remote(src.at[slot], dst.at[rows_at(par * seg, seg)], in_s.at[a, b], in_r.at[a, par], target)
                cp.start() if go else cp.wait_send()

            if b == 0:
                pl.when(jnp.logical_not(near))(far_copy)
            else:
                far_copy()

    def fetch_arrivals(a, src, dst):
        for h in range(2):
            @pl.when(jnp.logical_not(near & (par == h)))
            def _():
                remote(src.at[0], dst.at[pl.ds(h * seg, seg)], in_s.at[a, 0], in_r.at[a, h], place.plane(1)).wait_recv()

    def fetch_load(a, src, landed, dst, go):
        for h in range(2):
            here = dst.at[pl.ds(h * seg, seg)]
            came = pltpu.make_async_copy(landed.at[pl.ds(h * seg, seg)], here, tok_l.at[a, h])
            if go:
                mine = near & (par == h)
                pl.when(mine)(lambda: pltpu.make_async_copy(src.at[h], here, tok_l.at[a, h]).start())
                pl.when(jnp.logical_not(mine))(came.start)
            else:
                came.wait()

    pieces = [(0, 256, 0, None), (1, 64, 0, None)]
    for t in range(PIECES):
        pieces += [(2, 256, 0, t), (3, 256, 0, t), (4, TILE // 4, t * TILE, None)]
    WQKV, WO = 0, 1

    def tile_pieces(t):
        return (2 + 3 * t, 3 + 3 * t, 4 + 3 * t)

    def piece_at(ref, n, k, side=None, p=None):
        w, q, at, t = pieces[n]
        start, size = pl.multiple_of(at + place.quarter(k) * q, 16), q
        if side is not None:
            size = q // 2
            start = pl.multiple_of(start + side * size, 16)
        index = (pl.ds(start, size),) + (() if t is None else (pl.ds(t * TILE, TILE),))
        return ref.at[index if p is None else (p,) + index]

    def part(n, p, k, side=None):
        return piece_at(full[pieces[n][0]], n, k, side, p)

    def z_copies(n, go):
        @pl.when(near)
        def _():
            for i, to in enumerate((2 - c, 2 * place.half + 1 - par)):
                cp = remote(piece_at(shards[pieces[n][0]], n, 0), part(n, par, 0), zs.at[n, i], zr.at[n, par], place.column(c, to))
                cp.start() if go else cp.wait_send()

    def z_onward(n, p):
        return remote(part(n, p, 0), part(n, p, 0), zs.at[n, p], zr.at[n, p], place.column(c, 3 - 3 * c))

    def missing(p, body):
        pl.when(jnp.logical_or(jnp.logical_not(near), par != p))(body)

    def step_copy(n, p, i):
        k, side, to = ((0, None, 1), (0, None, 2), (1, 0, 2), (2, 1, 1))[i]
        return remote(part(n, p, k, side), part(n, p, k, side), fs.at[n, p, i], fr.at[n, p, i], place.plane(to))

    def first(n):
        for p in range(2):
            @functools.partial(missing, p)
            def _():
                z_onward(n, p).wait_recv()
                pl.when(inner)(lambda: z_onward(n, p).start())
                step_copy(n, p, 0).start()
                step_copy(n, p, 1).start()

    def second(n):
        for p in range(2):
            @functools.partial(missing, p)
            def _():
                step_copy(n, p, 0).wait_recv()
                step_copy(n, p, 2).start()
                step_copy(n, p, 1).wait_recv()
                step_copy(n, p, 3).start()

    def third(n):
        for p in range(2):
            @functools.partial(missing, p)
            def _():
                step_copy(n, p, 2).wait_recv()
                step_copy(n, p, 3).wait_recv()

    def sent(n):
        z_copies(n, False)
        for p in range(2):
            @functools.partial(missing, p)
            def _():
                pl.when(inner)(lambda: z_onward(n, p).wait_send())
                for i in range(4):
                    step_copy(n, p, i).wait_send()

    def weight_load(w, dst, go):
        for p in range(2):
            came = pltpu.make_async_copy(full[w].at[p], dst.at[p], wl.at[w, p])
            if go:
                mine = near & (par == p)
                pl.when(mine)(lambda: pltpu.make_async_copy(shards[w], dst.at[p], wl.at[w, p]).start())
                pl.when(jnp.logical_not(mine))(came.start)
            else:
                came.wait()

    def token_copies(a, src, dst, go):
        for b in range(2):
            h = par if b == 0 else 1 - par
            piece = src.at[rows_at(h * seg, seg)]
            target = place.column(place.half, 2 * c + h)
            there = dst.at[par]

            def far_copy():
                cp = remote(piece, there, tok_s.at[a, b], tok_r.at[a, par], target)
                cp.start() if go else cp.wait_send()

            if b == 0:
                @pl.when(near)
                def _():
                    cp = pltpu.make_async_copy(piece, there, tok_l.at[a, 0])
                    cp.start() if go else cp.wait()

                pl.when(jnp.logical_not(near))(far_copy)
            else:
                far_copy()

    def token_arrivals(a, src, dst):
        for s in range(2):
            @pl.when(jnp.logical_not(near & (par == s)))
            def _():
                remote(src.at[pl.ds(0, seg)], dst.at[s], tok_s.at[a, 0], tok_r.at[a, s], place.plane(1)).wait_recv()

    def rows_of(w, k, side=None):
        q = grads[w].shape[1] // 4
        start, size = pl.multiple_of(place.quarter(k) * q, q), q
        if side is not None:
            size = q // 2
            start = pl.multiple_of(start + side * size, size)
        return pl.ds(start, size)

    def diag_copy(w, side):
        return remote(grads[w].at[:, rows_of(w, 3, side)], diag[w].at[side], ps.at[w, side], pr.at[w, side], place.plane(1 + side))

    def plane_copy(w, i, side):
        src = grads[w].at[:, rows_of(w, 1 + i, side)] if side == i else diag[w].at[side]
        n = 2 + 2 * i + side
        return remote(src, plane_in[w].at[i, side], ps.at[w, n], pr.at[w, n], place.plane(1 + i))

    def begin(w):
        diag_copy(w, 0).start()
        diag_copy(w, 1).start()
        plane_copy(w, 0, 0).start()
        plane_copy(w, 1, 1).start()

    def add_diag(w):
        for side in (0, 1):
            diag_copy(w, side).wait()
            rows = rows_of(w, 2 - side, side)
            for p in range(2):
                diag[w][side, p] = (grads[w][p, rows, :].astype(F32) + diag[w][side, p].astype(F32)).astype(BF16)
            plane_copy(w, 1 - side, side).start()

    def outer_copy(w):
        return remote(diag[w], col_in[w], cs.at[w, 0], cr.at[w, 0], place.column(c, z - 1 + 2 * c))

    def inner_copy(w, p):
        return remote(diag[w].at[:, p], col_in[w].at[:, 1], cs.at[w, p], cr.at[w, 1], place.column(c, 2 * c + p))

    def near_copy(w):
        to = place.column(c, 2 * place.half + 1 - par)
        return remote(diag[w].at[:, 1 - par], col_in[w].at[:, 0], cs.at[w, 0], cr.at[w, 0], to)

    def plane_local(w, i, side):
        return pltpu.make_async_copy(plane_in[w].at[i, side], grads[w].at[:, rows_of(w, 1 + i, side)], pls.at[w, i, side])

    def col_local(w, side):
        return pltpu.make_async_copy(col_in[w].at[side], grads[w].at[:, rows_of(w, 3, side)], cls.at[w, side])

    def load_plane(w):
        for i in range(2):
            for side in range(2):
                plane_copy(w, i, side).wait()
        for i in range(2):
            for side in range(2):
                plane_local(w, i, side).start()

    def add_plane(w):
        for side in range(2):
            for i in range(2):
                plane_local(w, i, side).wait()
            mine, one, two = rows_of(w, 0, side), rows_of(w, 1, side), rows_of(w, 2, side)
            for p in range(2):
                total = grads[w][p, mine, :].astype(F32) + grads[w][p, one, :].astype(F32) + grads[w][p, two, :].astype(F32)
                diag[w][side, p] = total.astype(BF16)
        pl.when(outer)(lambda: outer_copy(w).start())
        pl.when(near)(lambda: near_copy(w).start())

    def load_outer(w):
        @pl.when(inner)
        def _():
            outer_copy(w).wait_recv()
            for side in range(2):
                col_local(w, side).start()

    def add_outer(w):
        @pl.when(inner)
        def _():
            for side in range(2):
                col_local(w, side).wait()
            for p in range(2):
                for side in range(2):
                    came = grads[w][p, rows_of(w, 3, side), :].astype(F32)
                    diag[w][side, p] = (diag[w][side, p].astype(F32) + came).astype(BF16)
                inner_copy(w, p).start()

    def last_copies(w, k):
        e = grads[w].shape[1] // 8
        if w < PIECES:
            cut = ((0, TILE, s_gate, w * TILE), (TILE, TILE, s_up, w * TILE))
        elif w == QKV_:
            cut = ((0, 256, s_q, 0), (256, 128, s_k, 0), (384, 128, s_v, 0))
        else:
            n = grads[w].shape[2]
            cut = ((0, n, s_o, 0),) if w == O_ else ((0, n, s_down, (w - DA_) * n),)
        return [(last.at[turn[w] % 2, k, pl.ds(0, e), pl.ds(at, n)], ref.at[:, pl.ds(to, n)]) for at, n, ref, to in cut]

    def last_remote(w):
        return [remote(src, dst, ls.at[w, i], lr.at[w, i], mate) for i, (src, dst) in enumerate(last_copies(w, 1))]

    def last_local(w):
        return [pltpu.make_async_copy(src, dst, ll.at[w, i]) for i, (src, dst) in enumerate(last_copies(w, 0))]

    def release_last(w):
        @pl.when(near)
        def _():
            for cp in last_remote(w):
                cp.wait_send()
            for cp in last_local(w):
                cp.wait()

    def load_column(w):
        @pl.when(near)
        def _():
            near_copy(w).wait_recv()
            inner_copy(w, 0).wait_recv()
            for side in range(2):
                col_local(w, side).start()

    def add_column(w):
        if turn[w] >= 2:
            release_last(turn.index(turn[w] - 2))

        @pl.when(near)
        def _():
            e, n = grads[w].shape[1] // 8, grads[w].shape[2]
            for hc in range(2):
                col_local(w, hc).wait()
                came = rows_of(w, 3, hc)
                total = diag[w][hc, par].astype(F32) + grads[w][0, came, :].astype(F32) + grads[w][1, came, :].astype(F32)

                @pl.when(c == hc)
                def _():
                    last[turn[w] % 2, 0, :e, :n] = total

                @pl.when(c != hc)
                def _():
                    last[turn[w] % 2, 1, :e, :n] = total

            for cp in last_remote(w) + last_local(w):
                cp.start()

    def finish(w):
        pl.when(near)(lambda: near_copy(w).wait_send())

        @pl.when(jnp.logical_not(near))
        def _():
            for cp in last_remote(w):
                cp.wait_recv()

        pl.when(outer)(lambda: outer_copy(w).wait_send())

        @pl.when(inner)
        def _():
            inner_copy(w, 0).wait_send()
            inner_copy(w, 1).wait_send()

    def trade(n):
        return remote(give.at[n % 2], take.at[n % 2], ms.at[n], mr.at[n], mate)

    def load(n, src, dst):
        return pltpu.make_async_copy(src, dst, ld.at[n])

    for n in range(len(pieces)):
        z_copies(n, True)
        if n == 4:
            fetch_copies(0, x_ref, hx, True)
        if n == 7:
            fetch_copies(1, ct_ref, hc, True)

    def swap_rows(buf, n):
        own = rows_at(own_at, half)
        return remote(buf.at[own], buf.at[own], ms.at[n], mr.at[n], mate)

    def swap_wait(buf, n):
        other = rows_at(other_at, half)
        remote(buf.at[other], buf.at[other], ms.at[n], mr.at[n], mate).wait_recv()

    def phase_one(wqkv, wo, xbuf, cbuf, qk, qs, k2, v2, mask, att, linv):
        saves = []

        def save(n, src, dst):
            cp = pltpu.make_async_copy(src, dst, outs.at[n])
            saves.append(cp)
            cp.start()

        for i in range(seq // BLK):
            for jb in range(i + 1):
                same = cols_ref[i * BLK : (i + 1) * BLK, :1] == rows_ref[1:, jb * BLK : (jb + 1) * BLK]
                if i == jb:
                    ri = lax.broadcasted_iota(jnp.int32, (BLK, BLK), 0)
                    ci = lax.broadcasted_iota(jnp.int32, (BLK, BLK), 1)
                    same = jnp.logical_or(ri == ci, jnp.logical_and(ci < ri, same))
                mask[i * BLK : (i + 1) * BLK, jb * BLK : (jb + 1) * BLK] = jnp.where(same, 1.0, 0.0).astype(F32)
        v2[:, :, 128:] = jnp.ones((v2.shape[0], v2.shape[1], 128), BF16)
        first(WQKV)
        first(WO)
        second(WQKV)
        second(WO)
        for n in tile_pieces(0):
            first(n)
        third(WQKV)
        weight_load(0, wqkv, True)
        for n in tile_pieces(0):
            second(n)
        third(WO)
        weight_load(1, wo, True)

        fetch_arrivals(0, x_ref, hx)
        fetch_load(0, x_ref, hx, xbuf, True)
        fetch_load(0, x_ref, hx, xbuf, False)

        @pl.loop(0, half // step)
        def _(r):
            xs = xbuf[rows_at(r * step, step), :].astype(F32)
            sc = lax.rsqrt(jnp.mean(xs * xs, axis=-1, keepdims=True) + EPS)
            normed_buf[rows_at(own_at + r * step, step), :] = (xs * sc * gain1_ref[...]).astype(BF16)

        swap_rows(normed_buf, 4).start()
        first(tile_pieces(1)[0])
        weight_load(0, wqkv, False)
        swap_wait(normed_buf, 4)
        normed = normed_buf
        save(1, normed, h_normed)

        @pl.loop(0, seq // BLK)
        def _(r):
            rows = rows_at(r * BLK, BLK)
            cos, sin = cos_ref[rows, :], sin_ref[rows, :]
            lane = lax.broadcasted_iota(jnp.int32, (BLK, 128), 1)
            left = lane < 64
            for p in range(2):
                proj = mm(normed[rows, :], wqkv[p])
                pq = proj[:, :384]
                qk[p, rows, :] = pq
                sc = lax.rsqrt(head_mean(pq * pq, ones_ref, 384) + EPS)
                n = pq * sc * gainqk_ref[...]
                for s in range(3):
                    v = n[:, s * 128 : (s + 1) * 128]
                    rot = v * cos + lane_swap(v) * sin
                    if s < 2:
                        qr = rot.astype(BF16).astype(F32) * 0.125
                        qs[2 * p + s, 0, rows, :] = jnp.where(left, qr, 0.0).astype(BF16)
                        qs[2 * p + s, 1, rows, :] = jnp.where(left, 0.0, qr).astype(BF16)
                    else:
                        kr = pltpu.roll(rot, 64, 1)
                        k2[2 * p, rows, :] = jnp.where(left, rot, kr).astype(BF16)
                        k2[2 * p + 1, rows, :] = jnp.where(left, kr, rot).astype(BF16)
                v = proj[:, 384:]
                vr = pltpu.roll(v, 64, 1)
                v2[2 * p, rows, :128] = jnp.where(left, v, vr).astype(BF16)
                v2[2 * p + 1, rows, :128] = jnp.where(left, vr, v).astype(BF16)

        save(3, qk, h_qk)
        save(4, qs, h_q)
        save(5, k2, h_k)
        save(6, v2.at[:, :, pl.ds(0, 128)], h_v)
        first(tile_pieces(1)[1])
        first(tile_pieces(1)[2])
        second(tile_pieces(1)[0])
        for i in range(seq // BLK):
            n = (i + 1) * BLK
            rows = pl.ds(i * BLK, BLK)

            @pl.loop(0, k2.shape[0])
            def _(g):
                s = mm_nt(qs[g, :, rows, :].reshape(2 * BLK, 128), k2[g, :n, :])
                e = jnp.exp(s).reshape(2, BLK, n) * mask[rows, :n][None]
                acc = mm(e.astype(BF16).reshape(2 * BLK, n), v2[g, :n, :])
                inv = 1.0 / acc[:, 128:]
                o = acc[:, :128] * inv
                left = lax.broadcasted_iota(jnp.int32, (BLK, 128), 1) < 64
                cols = pl.ds(pl.multiple_of(g * 128, 128), 128)
                att[rows, cols] = jnp.where(left, o[:BLK], o[BLK:]).astype(BF16)
                linv[rows, cols] = jnp.where(left, inv[:BLK], inv[BLK:])

        save(7, att, h_att)
        save(8, linv, h_linv)
        second(tile_pieces(1)[1])
        second(tile_pieces(1)[2])
        weight_load(1, wo, False)

        def out_rows(start):
            return mm(att[rows_at(start, BLK), :], wo[...].reshape(2 * wo.shape[1], wo.shape[2]))

        @pl.loop(0, half // BLK)
        def _(r):
            give[0, rows_at(r * BLK, BLK), :] = out_rows(other_at + r * BLK).astype(BF16)

        saves[0].wait()
        swap_rows(normed_buf, 4).wait_send()
        swap_give = remote(give.at[0], take.at[0], ms.at[5], mr.at[5], mate)
        swap_give.start()

        @pl.loop(0, half // BLK)
        def _(r):
            hgrad[rows_at(r * BLK, BLK), :] = out_rows(own_at + r * BLK) + xbuf[rows_at(r * BLK, BLK), :].astype(F32)

        fetch_arrivals(1, ct_ref, hc)
        fetch_load(1, ct_ref, hc, cbuf, True)
        swap_give.wait_recv()

        @pl.loop(0, half // step)
        def _(r):
            h = hgrad[rows_at(r * step, step), :] + take[0, rows_at(r * step, step), :].astype(F32)
            hgrad[rows_at(r * step, step), :] = h
            sc = lax.rsqrt(jnp.mean(h * h, axis=-1, keepdims=True) + EPS)
            n2[rows_at(own_at + r * step, step), :] = (h * sc * gain2_ref[...]).astype(BF16)

        swap_rows(n2, 6).start()
        fetch_load(1, ct_ref, hc, cbuf, False)

        @pl.loop(0, half // step)
        def _(r):
            own = rows_at(own_at + r * step, step)
            v = cbuf[rows_at(r * step, step), :].astype(F32) * jnp.where(cols_ref[own, 1:] >= 0, 1.0, 0.0)
            din[own, :] = v.astype(BF16)

        swap_rows(din, 7).start()
        for n in tile_pieces(0):
            third(n)
        swap_wait(n2, 6)
        swap_wait(din, 7)
        swap_rows(n2, 6).wait_send()
        swap_rows(din, 7).wait_send()
        swap_give.wait_send()
        for cp in saves[1:]:
            cp.wait()

    V = pltpu.VMEM
    gain_out[...] = jnp.zeros(gain_out.shape, F32)
    pl.run_scoped(
        phase_one, V(gqkv.shape, BF16), V(go.shape, BF16), V((half, width), BF16), V((half, width), BF16), V(h_qk.shape, F32),
        V(h_q.shape, BF16), V(h_k.shape, BF16), V((4, seq, 256), BF16), V((seq, seq), F32), V(h_att.shape, BF16),
        V(h_linv.shape, F32),
    )

    def ffn(wg, wu, wd, acc_o, acc_n, act, gu_rows):
        def tile_loads(t, go):
            cols = pl.ds(t * TILE, TILE)
            for p in range(2):
                here = pl.ds(p * TILE, TILE)

                def run(g, u, d):
                    pairs = ((g.at[:, cols], wg.at[:, here]), (u.at[:, cols], wu.at[:, here]), (d.at[cols], wd.at[here]))
                    for k, (src, dst) in enumerate(pairs):
                        cp = pltpu.make_async_copy(src, dst, wl.at[2 + k, p])
                        cp.start() if go else cp.wait()

                if go:
                    mine = near & (par == p)
                    pl.when(mine)(lambda: run(wg_ref, wu_ref, wd_ref))
                    pl.when(jnp.logical_not(mine))(lambda: run(gg.at[p], gu.at[p], gd.at[p]))
                else:
                    run(gg.at[p], gu.at[p], gd.at[p])

        ones_, twos = tile_pieces(1), tile_pieces(2)
        tile_loads(0, True)
        for t in range(PIECES):
            tile_loads(t, False)

            @pl.loop(0, seq // BLK)
            def _(r):
                rows = rows_at(r * BLK, BLK)
                a = n2[rows, :]
                g = mm(a, wg[...])
                u = mm(a, wu[...])
                ag = mm_nt(din[rows, :], wd[...])
                sig = jax.nn.sigmoid(g)
                gs_ = g * sig
                av = (gs_ * u).astype(BF16)
                act[t, rows, :] = av
                gv = (ag * u * (sig + gs_ * (1.0 - sig))).astype(BF16)
                uv = (ag * gs_).astype(BF16)
                for p in range(2):
                    gu_rows[rows, 2 * p * TILE : (2 * p + 1) * TILE] = gv[:, p * TILE : (p + 1) * TILE]
                    gu_rows[rows, (2 * p + 1) * TILE : (2 * p + 2) * TILE] = uv[:, p * TILE : (p + 1) * TILE]
                dn = mm_nt(gv, wg[...]) + mm_nt(uv, wu[...])
                do = mm(av, wd[...])
                if t == 0:
                    acc_n[rows, :] = dn
                    acc_o[rows, :] = do
                else:
                    acc_n[rows, :] += dn
                    acc_o[rows, :] += do

            if t == 0:
                for n in twos:
                    first(n)
                second(twos[0])
            if t == 1:
                for n in twos:
                    third(n)
                tile_loads(2, True)

            @pl.loop(0, width // BLK)
            def _(r):
                cols = pl.ds(pl.multiple_of(r * BLK, BLK), BLK)
                o = mm_tn(n2[:, cols], gu_rows[...]).astype(BF16)
                for p in range(2):
                    grads[t][p, cols, :] = o[:, 2 * p * TILE : 2 * (p + 1) * TILE]

            if t == 1:
                add_diag(0)
            begin(t)
            if t == 0:
                second(twos[1])
                second(twos[2])
                for n in ones_:
                    third(n)
                tile_loads(1, True)

        @pl.loop(0, half // BLK)
        def _(r):
            rows = rows_at(r * BLK, BLK)
            give[0, rows, :] = acc_n[rows_at(other_at + r * BLK, BLK), :].astype(BF16)
            give[1, rows, :] = acc_o[rows_at(other_at + r * BLK, BLK), :].astype(BF16)

        trade(0).start()
        trade(1).start()
        load_plane(0)
        for w in (DA_, DB_):
            n = width // 2
            for p in range(2):
                @pl.loop(0, n // BLK)
                def _(r):
                    cols = pl.ds(pl.multiple_of(r * BLK, BLK), BLK)
                    come = pl.ds(pl.multiple_of((w - DA_) * n + r * BLK, BLK), BLK)
                    for k in range(PIECES):
                        rows = pl.ds(k * TILE, TILE)
                        grads[w][p, rows, cols] = mm_tn(act[k, :, p * TILE : (p + 1) * TILE], din[:, come]).astype(BF16)

            if w == DA_:
                add_diag(1)
            begin(w)
            if w == DA_:
                add_plane(0)

        trade(0).wait_recv()
        trade(1).wait_recv()

        @pl.loop(0, half // step)
        def _(r):
            rows = rows_at(r * step, step)
            own = rows_at(own_at + r * step, step)
            h = hgrad[rows, :]
            obuf[rows, :] = (h + acc_o[own, :] + take[1, rows, :].astype(F32)).astype(BF16)
            ng = acc_n[own, :] + take[0, rows, :].astype(F32)
            sc = lax.rsqrt(jnp.mean(h * h, axis=-1, keepdims=True) + EPS)
            unit = h * sc
            acc_gain(8, ng * unit)
            e = ng * gain2_ref[...]
            hg = din[own, :].astype(F32) + sc * (e - unit * jnp.mean(e * unit, axis=-1, keepdims=True))
            hgrad[rows, :] = hg
            attn_in[own, :] = hg.astype(BF16)

        token_copies(0, obuf, oo, True)

    def acc_gain(at, v):
        s = jnp.sum(v, axis=0, keepdims=True)
        for k in range(width // 128):
            gain_out[at + k : at + k + 1, :] += s[:, k * 128 : (k + 1) * 128]

    pl.run_scoped(
        ffn,
        pltpu.VMEM((width, 2 * TILE), BF16), pltpu.VMEM((width, 2 * TILE), BF16), pltpu.VMEM((2 * TILE, width), BF16),
        pltpu.VMEM((seq, width), F32), pltpu.VMEM((seq, width), F32), pltpu.VMEM((PIECES, seq, 2 * TILE), BF16),
        pltpu.VMEM((seq, 4 * TILE), BF16),
    )

    def attn_swap():
        own = rows_at(own_at, half)
        return remote(attn_in.at[own], attn_in.at[own], ms.at[3], mr.at[3], mate)

    attn_swap().start()

    def attention(dos, dq, dk, dv, drow):
        def front(wo, att, linv):
            loads = [load(4, h_att, att), load(5, h_linv, linv)]
            for cp in loads:
                cp.start()
            weight_load(1, wo, True)
            for cp in loads:
                cp.wait()
            weight_load(1, wo, False)
            other = rows_at(other_at, half)
            remote(attn_in.at[other], attn_in.at[other], ms.at[3], mr.at[3], mate).wait_recv()

            @pl.loop(0, seq // BLK)
            def _(r):
                rows = rows_at(r * BLK, BLK)
                left = lax.broadcasted_iota(jnp.int32, (BLK, 128), 1) < 64
                for p in range(2):
                    ag = mm_nt(attn_in[rows, :], wo[p]).astype(BF16).astype(F32)
                    for s in range(2):
                        g = 2 * p + s
                        cols = slice(g * 128, (g + 1) * 128)
                        d = ag[:, s * 128 : (s + 1) * 128] * linv[rows, cols]
                        d0, d1 = jnp.where(left, d, 0.0).astype(BF16), jnp.where(left, 0.0, d).astype(BF16)
                        dos[g, 0, rows, :] = d0
                        dos[g, 1, rows, :] = d1
                        o = att[rows, cols].astype(F32)
                        one = jnp.ones((8, 128), BF16)
                        for k, dd in enumerate((d0, d1)):
                            prod = dd.astype(F32) * o
                            high = prod.astype(BF16)
                            low = (prod - high.astype(F32)).astype(BF16)
                            drow[g, k, :, rows] = mm_nt(one, high) + mm_nt(one, low)

            @pl.loop(0, width // BLK)
            def _(r):
                cols = pl.ds(pl.multiple_of(r * BLK, BLK), BLK)
                for p in range(2):
                    grads[O_][p, :, cols] = mm_tn(att[:, p * 256 : (p + 1) * 256], attn_in[:, cols]).astype(BF16)

            add_diag(2)
            begin(O_)
            load_plane(1)
            load_outer(0)

        pl.run_scoped(
            front, pltpu.VMEM(go.shape, BF16), pltpu.VMEM(h_att.shape, BF16), pltpu.VMEM(h_linv.shape, F32),
        )
        def rest(q, k, v, mt, qk, rows_, wqkv):
            normed = din
            trade(1).wait_send()
            x = give.at[1]
            loads = [load(6, h_q, q), load(7, h_k, k), load(8, h_v, v)]
            later = [load(9, h_qk, qk), load(11, h_normed, normed)]
            for cp in loads + later:
                cp.start()
            weight_load(0, wqkv, True)
            fetch_load(0, x_ref, hx, x, True)
            for cp in loads:
                cp.wait()
            dq[...] = jnp.zeros(dq.shape, F32)
            todo = {
                0: [lambda: add_plane(1), lambda: add_outer(0)],
                1: [lambda: add_diag(DA_)],
                2: [lambda: load_plane(2), lambda: load_column(0), lambda: load_outer(1)],
                3: [lambda: add_plane(2), lambda: add_column(0), lambda: add_outer(1), lambda: add_diag(DB_)],
            }
            for jb in range(seq // BLK):
                at = jb * BLK
                ni = seq - at
                keys = pl.ds(at, BLK)
                cols = pl.ds(at, ni)
                ki = lax.broadcasted_iota(jnp.int32, (BLK, ni), 0)
                qi = lax.broadcasted_iota(jnp.int32, (BLK, ni), 1)
                same = jnp.logical_and(ki < qi, cols_ref[keys, 1:] == rows_ref[:1, cols])
                mt[:, :ni] = jnp.where(jnp.logical_or(ki == qi, same), 1.0, 0.0).astype(F32)

                @pl.loop(0, 4)
                def _(g):
                    kb = k[g, keys, :]
                    qb = q[g, :, cols, :].reshape(2 * ni, 128)
                    db = dos[g, :, cols, :].reshape(2 * ni, 128)
                    m = mt[:, :ni]
                    e = jnp.exp(mm_nt(kb, qb)) * jnp.concatenate([m, m], axis=1)
                    dv[g, keys, :] = mm(e.astype(BF16), db)
                    dp = mm_nt(v[g, keys, :], db)
                    dr = jnp.concatenate([drow[g, 0, :1, cols], drow[g, 1, :1, cols]], axis=1)
                    ds = (e * (dp - dr)).astype(BF16)
                    dk[g, keys, :] = mm(ds, qb)
                    dqs = mm_tn(ds, kb)
                    left = lax.broadcasted_iota(jnp.int32, (ni, 128), 1) < 64
                    lanes = pl.ds(pl.multiple_of(g * 128, 128), 128)
                    dq[cols, lanes] += jnp.where(left, dqs[:ni], dqs[ni:])

                for f in todo[jb]:
                    f()
            for cp in later:
                cp.wait()
            weight_load(0, wqkv, False)
            fetch_load(0, x_ref, hx, x, False)

            @pl.loop(0, seq // BLK)
            def _(r):
                rows = rows_at(r * BLK, BLK)
                cos, sin = cos_ref[rows, :], sin_ref[rows, :]
                left = lax.broadcasted_iota(jnp.int32, (BLK, 128), 1) < 64

                def fold(ref, p):
                    a, b = ref[2 * p, rows, :], ref[2 * p + 1, rows, :]
                    return jnp.where(left, a + pltpu.roll(a, 64, 1), b + pltpu.roll(b, 64, 1))

                for p in range(2):
                    raw = qk[p, rows, :]
                    sc = lax.rsqrt(head_mean(raw * raw, ones_ref, 384) + EPS)
                    unit = raw * sc
                    parts = []
                    for s in range(3):
                        if s < 2:
                            v_ = dq[rows, (2 * p + s) * 128 : (2 * p + s + 1) * 128] * 0.125
                        else:
                            v_ = fold(dk, p)
                        v_ = v_.astype(BF16).astype(F32)
                        parts.append(v_ * cos - lane_swap(v_) * sin)
                    ng = jnp.concatenate(parts, axis=1)
                    gsum = jnp.sum(ng * unit, axis=0, keepdims=True)
                    qsum = gsum[:, :128] + gsum[:, 128:256]
                    ksum = gsum[:, 256:]
                    gain_out[16:17, :] += qsum
                    gain_out[17:18, :] += ksum
                    e = ng * gainqk_ref[...]
                    back = sc * (e - unit * head_mean(e * unit, ones_ref, 384))
                    rows_[p, rows, :384] = back.astype(BF16)
                    rows_[p, rows, 384:] = fold(dv, p).astype(BF16)

            def back_rows(start):
                at = rows_at(start, BLK)
                return mm_nt(rows_[0, at, :], wqkv[0]) + mm_nt(rows_[1, at, :], wqkv[1])

            trade(0).wait_send()

            @pl.loop(0, half // BLK)
            def _(r):
                give[0, rows_at(r * BLK, BLK), :] = back_rows(other_at + r * BLK).astype(BF16)

            trade(2).start()
            load_plane(DA_)
            add_diag(O_)
            for p in range(2):
                @pl.loop(0, width // BLK)
                def _(r):
                    cols = pl.ds(pl.multiple_of(r * BLK, BLK), BLK)
                    grads[QKV_][p, cols, :] = mm_tn(normed[:, cols], rows_[p]).astype(BF16)

            begin(QKV_)
            add_plane(DA_)
            load_column(1)
            load_outer(2)
            trade(2).wait_recv()
            token_copies(0, obuf, oo, False)

            @pl.loop(0, half // BLK)
            def _(r):
                rows = rows_at(r * BLK, BLK)
                ng = back_rows(own_at + r * BLK) + take[0, rows, :].astype(F32)
                xs = x[rows, :].astype(F32)
                sc = lax.rsqrt(jnp.mean(xs * xs, axis=-1, keepdims=True) + EPS)
                unit = xs * sc
                acc_gain(0, ng * unit)
                e = ng * gain1_ref[...]
                ig = hgrad[rows, :] + sc * (e - unit * jnp.mean(e * unit, axis=-1, keepdims=True))
                obuf[rows, :] = ig.astype(BF16)

        pl.run_scoped(
            rest, V(h_q.shape, BF16), V(h_k.shape, BF16), V(h_v.shape, BF16), V((BLK, seq), F32), V(h_qk.shape, F32),
            V((2, seq, 512), BF16), V(gqkv.shape, BF16),
        )

    pl.run_scoped(
        attention, pltpu.VMEM(h_q.shape, BF16), pltpu.VMEM((seq, 512), F32), pltpu.VMEM((4, seq, 128), F32),
        pltpu.VMEM((4, seq, 128), F32), pltpu.VMEM((4, 2, 8, seq), F32),
    )
    def gain_copy(i):
        to = (place.column(c, 2 * place.half + 1 - par), place.column(c, 2 - 2 * place.half + par), place.plane(1), place.plane(2),
              mate)[i]
        return remote(gain_out, gain_in.at[i], gs.at[i], gr.at[i], to)

    def gain_step(i):
        gain_copy(i).wait()
        gain_out[...] += gain_in[i]
        if i < 4:
            gain_copy(i + 1).start()

    gain_copy(0).start()
    token_copies(1, obuf, io, True)
    add_column(1)
    add_outer(2)
    load_plane(DB_)
    gain_step(0)
    load_outer(DA_)
    load_column(2)
    add_plane(DB_)
    load_plane(O_)
    gain_step(1)
    add_outer(DA_)
    add_column(2)
    add_diag(QKV_)
    add_plane(O_)
    gain_step(2)
    load_outer(DB_)
    load_column(DA_)
    gain_step(3)
    add_outer(DB_)
    add_column(DA_)
    load_outer(O_)
    load_plane(QKV_)
    gain_step(4)
    add_plane(QKV_)
    add_outer(O_)
    load_column(DB_)
    load_outer(QKV_)
    add_column(DB_)
    load_column(O_)
    add_outer(QKV_)
    add_column(O_)
    load_column(QKV_)
    add_column(QKV_)
    release_last(O_)
    release_last(QKV_)
    for w in range(nw):
        finish(w)
    for n in range(len(pieces)):
        sent(n)
    fetch_copies(0, x_ref, hx, False)
    fetch_copies(1, ct_ref, hc, False)
    trade(2).wait_send()
    attn_swap().wait_send()
    token_copies(1, obuf, io, False)
    token_arrivals(0, obuf, oo)
    token_arrivals(1, obuf, io)


def layer(x, ct, shards, vectors):
    anywhere = pl.BlockSpec(memory_space=pl.ANY)
    vmem = pl.BlockSpec(memory_space=pltpu.VMEM)
    dma = pltpu.SemaphoreType.DMA
    SDS, V = jax.ShapeDtypeStruct, pltpu.VMEM
    seg, width = x.shape[1], x.shape[2]
    half, seq = 2 * seg, 4 * seg
    wqkv, wo, wg, wu, wd = shards
    sizes = [(width, 2 * TILE)] * 3 + [(wd.shape[0], width // 2)] * 2 + [(wo.shape[0], width), (width, wqkv.shape[1])]
    nw, pieces = 7, 2 + 3 * PIECES
    gains = (24, 128)
    results = [(width // 8, 256), (width // 8, 128), (width // 8, 128), (wo.shape[0] // 8, width)]
    results += [(width // 8, wg.shape[1])] * 2 + [(wd.shape[0] // 8, width)]
    held = [((half, width), BF16), ((half, width), BF16), ((seq, width), BF16), ((2, seq, 384), F32), ((4, 2, seq, 128), BF16),
            ((4, seq, 128), BF16), ((4, seq, 128), BF16), ((seq, 512), BF16), ((seq, 512), F32)]
    out_shape = (
        [SDS((2, seg, width), BF16)] * 2
        + [SDS(gains, F32)]
        + [SDS(r, F32) for r in results]
        + [SDS((2,) + s.shape, BF16) for s in shards]
        + [SDS(*h) for h in held]
        + [SDS((2, 2, 2, r // 8, n), BF16) for r, n in sizes]
        + [SDS((2, 2, r // 8, n), BF16) for r, n in sizes]
    )
    e_max, n_max = max(r // 8 for r, _ in sizes), max(n for _, n in sizes)
    out = pl.pallas_call(
        layer_kernel,
        out_shape=out_shape,
        in_specs=[anywhere] * 7 + [vmem] * len(vectors),
        out_specs=[anywhere] * 2 + [vmem] + [anywhere] * (len(out_shape) - 3),
        scratch_shapes=[V((2, r, n), BF16) for r, n in sizes]
        + [V((2, 2, r // 8, n), BF16) for r, n in sizes]
        + [
            V((2, 2, e_max, n_max), F32), V((2, half, width), BF16), V((2, half, width), BF16), V((half, width), BF16),
            V((half, width), F32), V((5,) + gains, F32), V((seq, width), BF16), V((seq, width), BF16),
        ]
        + [
            dma((2, 2)), dma((2, 2)), dma((2, 2)), dma((2, 2)), dma((2, 2)), dma((pieces, 2)), dma((pieces, 2)),
            dma((pieces, 2, 4)), dma((pieces, 2, 4)), dma((nw, 6)), dma((nw, 6)), dma((nw, 2)), dma((nw, 2)), dma((nw, 3)),
            dma((nw, 3)), dma((nw, 3)), dma((5,)), dma((5,)), dma((8,)), dma((8,)), dma((13,)), dma((5, 2)), dma((nw, 2, 2)),
            dma((nw, 2)), dma((9,)),
        ],
        compiler_params=pltpu.CompilerParams(collective_id=0, has_side_effects=True, vmem_limit_bytes=60 * 1024 * 1024),
        name="layer",
    )(x, ct, *shards, *vectors)
    return out[0], out[1], out[2], out[3:10]


def rope_tables(length, width):
    k = np.arange(width // 2)
    angles = np.arange(length)[:, None] * (THETA ** (-2.0 * k / width))[None]
    cos, sin = np.cos(angles), np.sin(angles)
    return (
        jnp.asarray(np.concatenate([cos] * 4, axis=1), F32),
        jnp.asarray(np.concatenate([-sin, sin] * 2, axis=1), F32),
    )


def per_device(n_dp, inputs, query_weight, key_weight, value_weight, out_weight, gate_weight, up_weight, down_weight,
               attn_gain, ffn_gain, query_gain, key_gain, cotangent, segment_ids, padding, row_count):
    slots, _, width = inputs.shape
    seq_len = segment_ids.shape[1]
    head_dim = query_gain.shape[0]
    nq, nk = query_weight.shape[1], key_weight.shape[1]
    z = lax.axis_index("tensor")
    c = lax.axis_index("dp") % 2
    groups = n_dp // 8

    alive_all = padding * (jnp.arange(slots)[:, None] < row_count[0]).astype(jnp.int32)
    code = (segment_ids + ALIVE * alive_all)[z % 2]
    code = jnp.where(c == z // 2, code, lax.ppermute(code, "dp", [(i, i ^ 1) for i in range(n_dp)]))
    segment, alive_row = code % ALIVE, code // ALIVE
    key_code = jnp.where(alive_row > 0, segment, -1)
    codes = jnp.stack([segment, key_code])

    qkv_shard = jnp.concatenate([query_weight, key_weight, value_weight], axis=1)
    cos, sin = rope_tables(seq_len, head_dim)
    gain_qk = jnp.concatenate([query_gain] * (nq // head_dim) + [key_gain] * (nk // head_dim))[None]
    lanes = np.arange(nq + nk) // head_dim
    ones = jnp.asarray(np.where(lanes[:, None] == lanes[None], 1.0 / head_dim, 0.0), BF16)
    gain1, gain2 = attn_gain[None], ffn_gain[None]
    outs, in_grad, gains, sums = layer(
        inputs, cotangent, (qkv_shard, out_weight, gate_weight, up_weight, down_weight),
        (codes.T, codes, gain1, gain2, gain_qk, cos, sin,
         ones),
    )
    if groups > 1:
        same = [[g * 8 + k for g in range(groups)] for k in range(8)]
        sums = [lax.psum_scatter(s, "dp", scatter_dimension=0, axis_index_groups=same, tiled=True) for s in sums]
        gains = lax.psum(gains, "dp", axis_index_groups=same)
    pair = gains[16:18, :head_dim] + gains[16:18, head_dim:]
    return (
        outs,
        in_grad.astype(F32),
        *sums,
        gains[:8].reshape(-1),
        gains[8:16].reshape(-1),
        pair[0],
        pair[1],
    )


def solution(mesh):
    return jax.shard_map(
        functools.partial(per_device, mesh.shape["dp"]),
        mesh=mesh,
        in_specs=(
            P("dp", "tensor", None),
            P(None, "tensor"),
            P(None, "tensor"),
            P(None, "tensor"),
            P("tensor", None),
            P(None, "tensor"),
            P(None, "tensor"),
            P("tensor", None),
            P(),
            P(),
            P(),
            P(),
            P("dp", "tensor", None),
            P("dp", None),
            P("dp", None),
            P("dp"),
        ),
        out_specs=(
            P("dp", "tensor", None),
            P("dp", "tensor", None),
            P("dp", "tensor"),
            P("dp", "tensor"),
            P("dp", "tensor"),
            P(("tensor", "dp"), None),
            P("dp", "tensor"),
            P("dp", "tensor"),
            P(("tensor", "dp"), None),
            P(),
            P(),
            P(),
            P(),
        ),
        check_vma=False,
    )
```

time: 399 us -> 392 us (0.982)
  the two profiles are of different devices: /device:TPU:9 before, /device:TPU:29 now
where the time goes in v4:
time: 392 us; the launch traced here: 385 us
  Pallas kernels  364 us (93%)
  local copies, waits for them, and re-layouts  10.1 us (3%)
  other arithmetic  7.94 us (2%)
    pallas_call x1, Pallas kernels, layer(): pl.pallas_call(layer_kernel, out_shape=out_shape, in_specs=[anywhere] * 7...  364 us
  transfers between devices with their start and end apart: 1, of which 0 were waited for; matrix products, arithmetic and copies ran while one was open for 1% of the time, Pallas kernels for 0%

profile of v4, /device:TPU:29, one launch (start us, length us, event | category | flops | bytes accessed | tf_op | source)
XLA Modules:
  0.0 385.0 jit_solution(3198587606235054525)
XLA Ops:
  1.3 0.6 dynamic-slice
  1.9 1.4 dynamic-slice_add_fusion
  3.3 0.7 collective-permute-start
  4.1 2.3 pad_maximum_fusion.wqkv_ref
  6.3 0.1 concatenate.7
  6.4 0.6 broadcast_in_dim.14.gainqk_ref
  7.0 0.0 collective-permute-done
  7.0 0.6 pad_add_fusion
  7.6 1.0 copy.32.cols_ref
  8.6 364.4 %layer.1 = (bf16[2,256,1024]{2,1,0:T(8,128)(2,1)}, bf16[2,256,1024]{2,1,0:T(8,128)(2,1)}, f32[24,128]{1,0:T(8,128)}, f32[128,256]{1,0:T(8,128)}, f32[128,128]{1,...) custom-call(bf16[2,256,1024]{2,1,0:T(8,128)(2,1)} %x_ref.1, ...), custom_call_target="tpu_custom_call" | custom-call | tf_op jit(solution)/shard_map/layer/pallas_call | solution.py:1012
  373.1 0.8 slice_add_fusion
  373.9 1.3 slice_bitcast_fusion
  375.2 0.5 slice_bitcast_fusion.2
  375.7 2.8 convert_element_type.12
  378.6 1.0 copy.42
  379.5 0.0 copy-done.5
  379.5 0.7 copy.43
  380.2 0.6 copy.44
  380.8 0.6 copy.45
  381.5 0.7 copy.46
  382.1 0.8 copy.47
  382.9 0.8 copy.48
  383.8 0.0 copy-done.1
  383.8 0.8 copy.49
  (20 shorter events, 0.1 us)
Async XLA Ops:
  0.6 5.7 %copy-start.9 = (f32[64]{0:T(128)S(1)}, f32[64]{0:T(128)}, u32[]{:S(2)}) copy-start(f32[64]{0:T(128)} %param.30) | copy-start | bytes 772
  0.7 5.7 %copy-start.8 = (f32[64]{0:T(128)S(1)}, f32[64]{0:T(128)}, u32[]{:S(2)}) copy-start(f32[64]{0:T(128)} %param.29) | copy-start | bytes 772
  3.3 3.7 collective-permute-start
  373.1 5.5 %copy-start = (bf16[2,256,1024]{2,1,0:T(8,128)(2,1)S(1)}, bf16[2,256,1024]{2,1,0:T(8,128)(2,1)}, u32[]{:S(2)}) copy-start(bf16[2,256,1024]{2,1,0:T(8,128)(2,1)} %get-tuple-element.54) | copy-start | bytes 3145732
  375.7 3.8 copy-start.5
  375.7 4.5 %copy-start.7 = (f32[128,128]{1,0:T(8,128)S(1)}, f32[128,128]{1,0:T(8,128)}, u32[]{:S(2)}) copy-start(f32[128,128]{1,0:T(8,128)} %get-tuple-element.57) | copy-start | bytes 196612
  375.7 5.1 %copy-start.6 = (f32[128,128]{1,0:T(8,128)S(1)}, f32[128,128]{1,0:T(8,128)}, u32[]{:S(2)}) copy-start(f32[128,128]{1,0:T(8,128)} %get-tuple-element.58) | copy-start | bytes 196612
  378.6 2.9 copy-start.4
  378.6 3.6 copy-start.3
  378.6 4.4 %copy-start.2 = (f32[128,1152]{1,0:T(8,128)S(1)}, f32[128,1152]{1,0:T(8,128)}, u32[]{:S(2)}) copy-start(f32[128,1152]{1,0:T(8,128)} %get-tuple-element.61) | copy-start | bytes 1769476
  379.5 4.2 %copy-start.1 = (f32[144,1024]{1,0:T(8,128)S(1)}, f32[144,1024]{1,0:T(8,128)}, u32[]{:S(2)}) copy-start(f32[144,1024]{1,0:T(8,128)} %get-tuple-element.62) | copy-start | bytes 1769476

commit v5 on v4

--- a/solution.py
+++ b/solution.py
@@ -433,7 +433,7 @@
 
     for n in range(len(pieces)):
         z_copies(n, True)
-        if n == 4:
+        if n == 3:
             fetch_copies(0, x_ref, hx, True)
         if n == 7:
             fetch_copies(1, ct_ref, hc, True)
@@ -658,6 +658,8 @@
                 for n in twos:
                     first(n)
                 second(twos[0])
+            if t == 2:
+                load_plane(0)
             if t == 1:
                 for n in twos:
                     third(n)
@@ -673,6 +675,8 @@
             if t == 1:
                 add_diag(0)
             begin(t)
+            if t == 2:
+                add_plane(0)
             if t == 0:
                 second(twos[1])
                 second(twos[2])
@@ -688,7 +692,6 @@
 
         trade(0).start()
         trade(1).start()
-        load_plane(0)
         for w in (DA_, DB_):
             n = width // 2
             for p in range(2):
@@ -703,8 +706,9 @@
             if w == DA_:
                 add_diag(1)
             begin(w)
-            if w == DA_:
-                add_plane(0)
+            if w == DB_:
+                load_plane(1)
+                load_outer(0)
 
         trade(0).wait_recv()
         trade(1).wait_recv()
@@ -724,6 +728,8 @@
             hgrad[rows, :] = hg
             attn_in[own, :] = hg.astype(BF16)
 
+        add_plane(1)
+        add_outer(0)
         token_copies(0, obuf, oo, True)
 
     def acc_gain(at, v):
@@ -737,6 +743,11 @@
         pltpu.VMEM((seq, width), F32), pltpu.VMEM((seq, width), F32), pltpu.VMEM((PIECES, seq, 2 * TILE), BF16),
         pltpu.VMEM((seq, 4 * TILE), BF16),
     )
+
+    def gain_copy(i):
+        to = (mate, place.column(c, 2 * place.half + 1 - par), place.column(c, 2 - 2 * place.half + par), place.plane(1),
+              place.plane(2))[i]
+        return remote(gain_out, gain_in.at[i], gs.at[i], gr.at[i], to)
 
     def attn_swap():
         own = rows_at(own_at, half)
@@ -785,8 +796,8 @@
 
             add_diag(2)
             begin(O_)
-            load_plane(1)
-            load_outer(0)
+            load_column(0)
+            load_outer(1)
 
         pl.run_scoped(
             front, pltpu.VMEM(go.shape, BF16), pltpu.VMEM(h_att.shape, BF16), pltpu.VMEM(h_linv.shape, F32),
@@ -805,10 +816,10 @@
                 cp.wait()
             dq[...] = jnp.zeros(dq.shape, F32)
             todo = {
-                0: [lambda: add_plane(1), lambda: add_outer(0)],
+                0: [lambda: add_column(0), lambda: add_outer(1)],
                 1: [lambda: add_diag(DA_)],
-                2: [lambda: load_plane(2), lambda: load_column(0), lambda: load_outer(1)],
-                3: [lambda: add_plane(2), lambda: add_column(0), lambda: add_outer(1), lambda: add_diag(DB_)],
+                2: [lambda: load_plane(2)],
+                3: [lambda: add_plane(2), lambda: add_diag(DB_)],
             }
             for jb in range(seq // BLK):
                 at = jb * BLK
@@ -890,16 +901,6 @@
             trade(2).start()
             load_plane(DA_)
             add_diag(O_)
-            for p in range(2):
-                @pl.loop(0, width // BLK)
-                def _(r):
-                    cols = pl.ds(pl.multiple_of(r * BLK, BLK), BLK)
-                    grads[QKV_][p, cols, :] = mm_tn(normed[:, cols], rows_[p]).astype(BF16)
-
-            begin(QKV_)
-            add_plane(DA_)
-            load_column(1)
-            load_outer(2)
             trade(2).wait_recv()
             token_copies(0, obuf, oo, False)
 
@@ -915,6 +916,19 @@
                 ig = hgrad[rows, :] + sc * (e - unit * jnp.mean(e * unit, axis=-1, keepdims=True))
                 obuf[rows, :] = ig.astype(BF16)
 
+            token_copies(1, obuf, io, True)
+            gain_copy(0).start()
+            for p in range(2):
+                @pl.loop(0, width // BLK)
+                def _(r):
+                    cols = pl.ds(pl.multiple_of(r * BLK, BLK), BLK)
+                    grads[QKV_][p, cols, :] = mm_tn(normed[:, cols], rows_[p]).astype(BF16)
+
+            begin(QKV_)
+            add_plane(DA_)
+            load_column(1)
+            load_outer(2)
+
         pl.run_scoped(
             rest, V(h_q.shape, BF16), V(h_k.shape, BF16), V(h_v.shape, BF16), V((BLK, seq), F32), V(h_qk.shape, F32),
             V((2, seq, 512), BF16), V(gqkv.shape, BF16),
@@ -924,48 +938,42 @@
         attention, pltpu.VMEM(h_q.shape, BF16), pltpu.VMEM((seq, 512), F32), pltpu.VMEM((4, seq, 128), F32),
         pltpu.VMEM((4, seq, 128), F32), pltpu.VMEM((4, 2, 8, seq), F32),
     )
-    def gain_copy(i):
-        to = (place.column(c, 2 * place.half + 1 - par), place.column(c, 2 - 2 * place.half + par), place.plane(1), place.plane(2),
-              mate)[i]
-        return remote(gain_out, gain_in.at[i], gs.at[i], gr.at[i], to)
-
-    def gain_step(i):
+    def gain_step(i, go=True):
         gain_copy(i).wait()
         gain_out[...] += gain_in[i]
-        if i < 4:
+        if go:
             gain_copy(i + 1).start()
 
-    gain_copy(0).start()
-    token_copies(1, obuf, io, True)
     add_column(1)
+    gain_step(0)
     add_outer(2)
     load_plane(DB_)
-    gain_step(0)
+    gain_step(1)
     load_outer(DA_)
     load_column(2)
+    gain_step(2, False)
     add_plane(DB_)
     load_plane(O_)
-    gain_step(1)
     add_outer(DA_)
     add_column(2)
     add_diag(QKV_)
+    gain_copy(3).start()
     add_plane(O_)
-    gain_step(2)
     load_outer(DB_)
     load_column(DA_)
-    gain_step(3)
     add_outer(DB_)
     add_column(DA_)
     load_outer(O_)
     load_plane(QKV_)
-    gain_step(4)
+    gain_step(3)
     add_plane(QKV_)
     add_outer(O_)
     load_column(DB_)
     load_outer(QKV_)
+    gain_step(4, False)
     add_column(DB_)
+    add_outer(QKV_)
     load_column(O_)
-    add_outer(QKV_)
     add_column(O_)
     load_column(QKV_)
     add_column(QKV_)

time: 392 us -> 391 us (level)
  the two profiles are of different devices: /device:TPU:29 before, /device:TPU:9 now
where the time goes in v5:
time: 391 us; the launch traced here: 383 us
  Pallas kernels  363 us (93%)
  local copies, waits for them, and re-layouts  10.1 us (3%)
  other arithmetic  7.94 us (2%)
    pallas_call x1, Pallas kernels, layer(): pl.pallas_call(layer_kernel, out_shape=out_shape, in_specs=[anywhere] * 7...  363 us
  transfers between devices with their start and end apart: 1, of which 0 were waited for; matrix products, arithmetic and copies ran while one was open for 1% of the time, Pallas kernels for 0%

profile of v5, /device:TPU:9, one launch (start us, length us, event | category | flops | bytes accessed | tf_op | source)
XLA Modules:
  0.0 383.4 jit_solution(4601006827108159621)
XLA Ops:
  1.3 0.6 dynamic-slice
  1.9 1.4 dynamic-slice_add_fusion
  3.3 0.7 collective-permute-start
  4.1 2.3 pad_maximum_fusion.wqkv_ref
  6.3 0.1 concatenate.7
  6.4 0.6 broadcast_in_dim.14.gainqk_ref
  7.0 0.0 collective-permute-done
  7.0 0.6 pad_add_fusion
  7.6 1.0 copy.32.cols_ref
  8.6 362.8 %layer.1 = (bf16[2,256,1024]{2,1,0:T(8,128)(2,1)}, bf16[2,256,1024]{2,1,0:T(8,128)(2,1)}, f32[24,128]{1,0:T(8,128)}, f32[128,256]{1,0:T(8,128)}, f32[128,128]{1,...) custom-call(bf16[2,256,1024]{2,1,0:T(8,128)(2,1)} %x_ref.1, ...), custom_call_target="tpu_custom_call" | custom-call | tf_op jit(solution)/shard_map/layer/pallas_call | solution.py:1020
  371.5 0.8 slice_add_fusion
  372.3 1.3 slice_bitcast_fusion
  373.6 0.5 slice_bitcast_fusion.2
  374.1 2.8 convert_element_type.12
  377.0 1.0 copy.42
  378.0 0.7 copy.43
  378.6 0.0 copy-done.7
  378.6 0.6 copy.44
  379.2 0.6 copy.45
  379.9 0.0 copy-done.4
  379.9 0.7 copy.46
  380.5 0.8 copy.47
  381.4 0.8 copy.48
  382.2 0.8 copy.49
  (20 shorter events, 0.1 us)
Async XLA Ops:
  0.6 5.7 %copy-start.9 = (f32[64]{0:T(128)S(1)}, f32[64]{0:T(128)}, u32[]{:S(2)}) copy-start(f32[64]{0:T(128)} %param.30) | copy-start | bytes 772
  0.7 5.7 %copy-start.8 = (f32[64]{0:T(128)S(1)}, f32[64]{0:T(128)}, u32[]{:S(2)}) copy-start(f32[64]{0:T(128)} %param.29) | copy-start | bytes 772
  3.3 3.7 collective-permute-start
  371.5 5.5 %copy-start = (bf16[2,256,1024]{2,1,0:T(8,128)(2,1)S(1)}, bf16[2,256,1024]{2,1,0:T(8,128)(2,1)}, u32[]{:S(2)}) copy-start(bf16[2,256,1024]{2,1,0:T(8,128)(2,1)} %get-tuple-element.54) | copy-start | bytes 3145732
  374.1 3.8 copy-start.5
  374.1 4.5 %copy-start.7 = (f32[128,128]{1,0:T(8,128)S(1)}, f32[128,128]{1,0:T(8,128)}, u32[]{:S(2)}) copy-start(f32[128,128]{1,0:T(8,128)} %get-tuple-element.57) | copy-start | bytes 196612
  374.1 5.1 %copy-start.6 = (f32[128,128]{1,0:T(8,128)S(1)}, f32[128,128]{1,0:T(8,128)}, u32[]{:S(2)}) copy-start(f32[128,128]{1,0:T(8,128)} %get-tuple-element.58) | copy-start | bytes 196612
  377.0 2.9 copy-start.4
  377.0 3.6 copy-start.3
  377.0 4.4 %copy-start.2 = (f32[128,1152]{1,0:T(8,128)S(1)}, f32[128,1152]{1,0:T(8,128)}, u32[]{:S(2)}) copy-start(f32[128,1152]{1,0:T(8,128)} %get-tuple-element.61) | copy-start | bytes 1769476
  378.0 4.2 %copy-start.1 = (f32[144,1024]{1,0:T(8,128)S(1)}, f32[144,1024]{1,0:T(8,128)}, u32[]{:S(2)}) copy-start(f32[144,1024]{1,0:T(8,128)} %get-tuple-element.62) | copy-start | bytes 1769476

commit v6 on v5

--- a/solution.py
+++ b/solution.py
@@ -435,7 +435,7 @@
         z_copies(n, True)
         if n == 3:
             fetch_copies(0, x_ref, hx, True)
-        if n == 7:
+        if n == 8:
             fetch_copies(1, ct_ref, hc, True)
 
     def swap_rows(buf, n):

time: 391 us -> 391 us (level)
  no operation moved by 1% of the time
where the time goes in v6:
time: 391 us; the launch traced here: 384 us
  Pallas kernels  363 us (93%)
  local copies, waits for them, and re-layouts  10.1 us (3%)
  other arithmetic  7.94 us (2%)
    pallas_call x1, Pallas kernels, layer(): pl.pallas_call(layer_kernel, out_shape=out_shape, in_specs=[anywhere] * 7...  363 us
  transfers between devices with their start and end apart: 1, of which 0 were waited for; matrix products, arithmetic and copies ran while one was open for 1% of the time, Pallas kernels for 0%

profile of v6, /device:TPU:9, one launch (start us, length us, event | category | flops | bytes accessed | tf_op | source)
XLA Modules:
  0.0 383.5 jit_solution(5051961685061891721)
XLA Ops:
  1.3 0.6 dynamic-slice
  1.9 1.4 dynamic-slice_add_fusion
  3.3 0.7 collective-permute-start
  4.1 2.3 pad_maximum_fusion.wqkv_ref
  6.3 0.1 concatenate.7
  6.4 0.6 broadcast_in_dim.14.gainqk_ref
  7.0 0.0 collective-permute-done
  7.0 0.6 pad_add_fusion
  7.6 1.0 copy.32.cols_ref
  8.6 362.9 %layer.1 = (bf16[2,256,1024]{2,1,0:T(8,128)(2,1)}, bf16[2,256,1024]{2,1,0:T(8,128)(2,1)}, f32[24,128]{1,0:T(8,128)}, f32[128,256]{1,0:T(8,128)}, f32[128,128]{1,...) custom-call(bf16[2,256,1024]{2,1,0:T(8,128)(2,1)} %x_ref.1, ...), custom_call_target="tpu_custom_call" | custom-call | tf_op jit(solution)/shard_map/layer/pallas_call | solution.py:1020
  371.6 0.8 slice_add_fusion
  372.4 1.3 slice_bitcast_fusion
  373.7 0.5 slice_bitcast_fusion.2
  374.2 2.8 convert_element_type.12
  377.0 0.0 copy-done
  377.1 1.0 copy.42
  378.0 0.0 copy-done.5
  378.0 0.7 copy.43
  378.7 0.6 copy.44
  379.3 0.6 copy.45
  380.0 0.7 copy.46
  380.6 0.8 copy.47
  381.4 0.8 copy.48
  382.2 0.8 copy.49
  (20 shorter events, 0.1 us)
Async XLA Ops:
  0.6 5.7 %copy-start.9 = (f32[64]{0:T(128)S(1)}, f32[64]{0:T(128)}, u32[]{:S(2)}) copy-start(f32[64]{0:T(128)} %param.30) | copy-start | bytes 772
  0.7 5.7 %copy-start.8 = (f32[64]{0:T(128)S(1)}, f32[64]{0:T(128)}, u32[]{:S(2)}) copy-start(f32[64]{0:T(128)} %param.29) | copy-start | bytes 772
  3.3 3.7 collective-permute-start
  371.5 5.5 %copy-start = (bf16[2,256,1024]{2,1,0:T(8,128)(2,1)S(1)}, bf16[2,256,1024]{2,1,0:T(8,128)(2,1)}, u32[]{:S(2)}) copy-start(bf16[2,256,1024]{2,1,0:T(8,128)(2,1)} %get-tuple-element.54) | copy-start | bytes 3145732
  374.2 3.8 copy-start.5
  374.2 4.5 %copy-start.7 = (f32[128,128]{1,0:T(8,128)S(1)}, f32[128,128]{1,0:T(8,128)}, u32[]{:S(2)}) copy-start(f32[128,128]{1,0:T(8,128)} %get-tuple-element.57) | copy-start | bytes 196612
  374.2 5.1 %copy-start.6 = (f32[128,128]{1,0:T(8,128)S(1)}, f32[128,128]{1,0:T(8,128)}, u32[]{:S(2)}) copy-start(f32[128,128]{1,0:T(8,128)} %get-tuple-element.58) | copy-start | bytes 196612
  377.0 2.9 copy-start.4
  377.0 3.6 copy-start.3
  377.0 4.4 %copy-start.2 = (f32[128,1152]{1,0:T(8,128)S(1)}, f32[128,1152]{1,0:T(8,128)}, u32[]{:S(2)}) copy-start(f32[128,1152]{1,0:T(8,128)} %get-tuple-element.61) | copy-start | bytes 1769476
  378.0 4.2 %copy-start.1 = (f32[144,1024]{1,0:T(8,128)S(1)}, f32[144,1024]{1,0:T(8,128)}, u32[]{:S(2)}) copy-start(f32[144,1024]{1,0:T(8,128)} %get-tuple-element.62) | copy-start | bytes 1769476
